TPU v7x, 32 devices: a whole 2x2x4 slice. The times are simulated.
32 devices in a mesh: groups: 2 (over y), qring: 4 (over x, core), kvring: 4 (over z), head: 1.
Axes of the slice: x: 2, y: 2, z: 4, core: 2. Of those that a mesh axis runs over, the one named last changes fastest.
Arguments:
- queries: bfloat16 [1536, 4096], P(('groups', 'qring', 'kvring'), 'head'), parts along dimension 0, may hold values from -6 to 6
- keys: bfloat16 [1536, 512], P(('groups', 'qring', 'kvring'), 'head'), parts along dimension 0, may hold values from -6 to 6
- values: bfloat16 [1536, 512], P(('groups', 'qring', 'kvring'), 'head'), parts along dimension 0, may hold values from -6 to 6
- doc_ids: int32 [1536], P('groups'), parts along dimension 0, may hold values from 0 to 15, never falling along the last dimension, each value on 1 to 480 neighbouring positions
- head_mask: int32 [32], P('head'), may hold values 0 or 1
- w_out: bfloat16 [4096, 8192], P('head', 'kvring'), may hold values from -0.5 to 0.5
Outputs:
- mixed: bfloat16 [1536, 8192], P(('groups', 'qring', 'head'), 'kvring'), parts along dimension 0
There are 2 independent parts, one for each index of `groups`. A program takes and returns all parts, laid end to end along the dimension named above; an argument that names none is the same for every part. Nothing has to cross between parts.
All inputs are finite; a program needn't handle non-finite values. No bound on the sum of `head_mask` on one device may be relied on, other than what follows from the above.
Results may differ from a plain program's by a relative error of at most 0.015.
Values may be sent and summed in bfloat16 or wider, within the bound.
No kernel may reach another device: no remote copies, remote signals or barrier semaphores. Data moves between devices by JAX's collectives and lax.ppermute only.
A program may use at most 64 MiB of HBM per device.

v0:
```python
import math

import jax
import jax.numpy as jnp
from jax import lax
from jax.sharding import PartitionSpec as P

HD = 128


NEG = -1e30


def block_rows(total_rows, shard_rows):
    best_size = shard_rows
    for multiple in range(1, total_rows // shard_rows + 1):
        if total_rows // shard_rows % multiple == 0 and multiple * shard_rows <= 256:
            best_size = multiple * shard_rows
    return best_size


def attend_keys(state, visible, queries4, key_rows, value_rows, scale_factor):
    run_max, run_sum, run_out = state
    mask4 = visible[:, None, None, :]
    scores = (
        jnp.einsum("rgec,kgc->rgek", queries4, key_rows, preferred_element_type=jnp.float32)
        * scale_factor
    )
    scores = jnp.where(mask4, scores, NEG)
    new_max = jnp.maximum(run_max, jnp.max(scores, axis=-1))
    weights = jnp.where(mask4, jnp.exp(scores - new_max[..., None]), 0.0)
    shrink = jnp.exp(run_max - new_max)
    run_sum = run_sum * shrink + jnp.sum(weights, axis=-1)
    update = jnp.einsum(
        "rgek,kgc->rgec",
        weights.astype(jnp.bfloat16),
        value_rows,
        preferred_element_type=jnp.float32,
    )
    run_out = run_out * shrink[..., None] + update
    return (new_max, run_sum, run_out)


def fold_piece(
    state, pieces, key_start, queries4, query_doc, query_pos, doc_ids, shard_rows, scale_factor
):
    key_all, value_all = pieces
    total_rows = key_all.shape[0]
    block_size = block_rows(total_rows, shard_rows)

    def one_block(index, carry):
        offset = index * block_size
        key_rows = lax.dynamic_slice_in_dim(key_all, offset, block_size, 0)
        value_rows = lax.dynamic_slice_in_dim(value_all, offset, block_size, 0)
        first = key_start + offset
        key_doc = lax.dynamic_slice_in_dim(doc_ids, first, block_size, 0)
        key_pos = first + jnp.arange(block_size, dtype=jnp.int32)
        visible = (query_doc[:, None] == key_doc[None, :]) & (
            key_pos[None, :] <= query_pos[:, None]
        )
        return attend_keys(carry, visible, queries4, key_rows, value_rows, scale_factor)

    return lax.fori_loop(0, total_rows // block_size, one_block, state)


def per_device(queries, keys, values, doc_ids, head_mask, w_out):
    shard_rows = queries.shape[0]
    kv_local = keys.shape[1] // HD
    q_local = queries.shape[1] // HD
    per_group = q_local // kv_local
    scale_factor = 1.0 / math.sqrt(HD)
    cycle_size = lax.axis_size("kvring")
    cycle_index = lax.axis_index("kvring")
    loop_index = lax.axis_index("qring")
    quarter = cycle_size * shard_rows
    key_rows = keys.reshape(shard_rows, kv_local, HD)
    value_rows = values.reshape(shard_rows, kv_local, HD)
    loop_size = lax.axis_size("qring")
    gathered = lax.all_gather(queries, "qring", axis=0, tiled=True)
    query_total = loop_size * shard_rows
    row_ids = jnp.arange(query_total, dtype=jnp.int32)
    query_pos = row_ids // shard_rows * quarter + cycle_index * shard_rows + row_ids % shard_rows
    queries4 = gathered.reshape(query_total, kv_local, per_group, HD)
    query_doc = jnp.take(doc_ids, query_pos)
    key_base = loop_index * quarter
    initial = (
        jnp.full((query_total, kv_local, per_group), NEG, jnp.float32),
        jnp.zeros((query_total, kv_local, per_group), jnp.float32),
        jnp.zeros((query_total, kv_local, per_group, HD), jnp.float32),
    )
    run_max, run_sum, run_out = fold_piece(
        initial,
        (
            lax.all_gather(key_rows, "kvring", axis=0, tiled=True),
            lax.all_gather(value_rows, "kvring", axis=0, tiled=True),
        ),
        key_base,
        queries4,
        query_doc,
        query_pos,
        doc_ids,
        shard_rows,
        scale_factor,
    )
    top = lax.pmax(run_max, "qring")
    factor = jnp.exp(run_max - top)
    numer, denom = (
        lax.psum_scatter(
            (run_out * factor[..., None]).astype(jnp.bfloat16),
            "qring",
            scatter_dimension=0,
            tiled=True,
        ).astype(jnp.float32),
        lax.psum_scatter(
            (run_sum * factor).astype(jnp.bfloat16), "qring", scatter_dimension=0, tiled=True
        ).astype(jnp.float32),
    )
    mask_f = head_mask.reshape(kv_local, per_group).astype(jnp.float32)
    attended = (
        (numer / denom[..., None] * mask_f[None, :, :, None])
        .astype(jnp.bfloat16)
        .reshape(shard_rows, q_local * HD)
    )
    partial_sum = jnp.dot(
        lax.all_gather(attended, "kvring", axis=0, tiled=True),
        w_out,
        preferred_element_type=jnp.float32,
    )
    return lax.psum_scatter(
        partial_sum.astype(jnp.bfloat16), "head", scatter_dimension=0, tiled=True
    )


def solution(mesh):
    placed = (
        P(("groups", "qring", "kvring"), "head"),
        P(("groups", "qring", "kvring"), "head"),
        P(("groups", "qring", "kvring"), "head"),
        P("groups"),
        P("head"),
        P("head", "kvring"),
    )
    return jax.shard_map(
        per_device,
        mesh=mesh,
        in_specs=placed,
        out_specs=P(("groups", "qring", "head"), "kvring"),
        check_vma=False,
    )
```

profile of v0, /device:TPU:0, one launch (start us, length us, event | category | flops | bytes accessed | tf_op | source)
XLA Modules:
  0.0 177.1 jit_solution(12851402233796282457)
XLA Ops:
  6.5 0.7 all-gather.3.cloned.1.call-update
  7.3 0.8 dynamic_slice.8
  8.1 1.9 %gather_fusion = s32[192]{0:T(256)S(1)} fusion(s32[768]{0:T(1024)} %param.9, s32[1024]{0:T(1024)S(1)} %pad_clamp_fusion), kind=kCustom, calls=%fused_computation | custom fusion | bytes 2304 | tf_op jit(solution)/shard_map/jit(_take)/gather | solution.py:84
  10.1 15.5 %all_gather.12 = bf16[192,4,128]{2,0,1:T(8,128)(2,1)S(1)} all-gather(bf16[48,4,128]{2,0,1:T(8,128)(2,1)S(1)} %copy_bitcast_fusion.3), channel_id=1, replica_groups=mesh['groups'=2,'qring'=4,'kvring'=4,'head'=1] {'kvring'}, dimensions={0}, use_global_device_ids=true | all-gather | bytes 245760 | tf_op jit(solution)/shard_map/all_gather | solution.py:94
  25.5 0.8 copy_bitcast_fusion.2
  26.3 14.7 %all_gather.14 = bf16[192,4,128]{2,0,1:T(8,128)(2,1)} all-gather(bf16[48,4,128]{2,0,1:T(8,128)(2,1)S(1)} %copy_bitcast_fusion.2), channel_id=1, replica_groups=mesh['groups'=2,'qring'=4,'kvring'=4,'head'=1] {'kvring'}, dimensions={0}, use_global_device_ids=true | all-gather | bytes 245760 | tf_op jit(solution)/shard_map/all_gather | solution.py:95
  41.2 1.7 copy.37
  42.9 4.5 %fusion = (f32[192,4,8]{0,2,1:T(8,128)S(1)}, f32[4,192,192,8]{2,1,3,0:T(8,128)}) fusion(pred[192,192]{0,1:T(8,128)(4,1)S(1)} %compare_and_fusion, bf16[192,4,8,128]{3,2,1,0:T(8,128)(2,1)S(1)} %bitcast.68, bf16[192,4,128]{2,0,1:T(8,128)(2,1)S(1)} %all_gather.12), kind=kOutput, calls=%fused_computation.3 | convolution fusion | flops 305522688 | bytes 6549504 | tf_op jit(solution)/shard_map/while/body/eval_jaxpr/rgec,kgc->rgek/dot_general | solution.py:26
  47.4 10.3 %pmax.7 = f32[192,4,8]{0,2,1:T(8,128)S(1)} all-reduce(f32[192,4,8]{0,2,1:T(8,128)S(1)} %broadcast_maximum_fusion), channel_id=1, replica_groups=mesh['groups'=2,'qring'=4,'kvring'=4,'head'=1] {'qring'}, use_global_device_ids=true, to_apply=%region_1.2 | all-reduce | flops 6144 | bytes 49152 | tf_op jit(solution)/shard_map/pmax | solution.py:105
  57.7 4.6 %fusion.1 = (f32[192,4,8]{0,2,1:T(8,128)S(1)}, bf16[192,4,8,192]{0,3,2,1:T(8,128)(2,1)S(1)}) fusion(f32[4,192,192,8]{2,1,3,0:T(8,128)} %get-tuple-element.33, f32[192,4,8]{0,2,1:T(8,128)S(1)} %broadcast_maximum_fusion, pred[192,192]{0,1:T(8,128)(4,1)S(1)} %compare_and_fusion), kind=kLoop, calls=%fused_computation.4 | loop fusion | flops 7071744 | bytes 7163904 | tf_op jit(solution)/shard_map/while/body/eval_jaxpr/reduce_sum | solution.py:33
  62.3 0.9 copy.21
  63.2 0.9 copy.24
  64.2 3.9 %copy.23 = bf16[192,4,8,192]{3,2,0,1:T(8,128)(2,1)} copy(bf16[192,4,8,192]{0,3,2,1:T(8,128)(2,1)S(1)} %get-tuple-element.30) | data formatting | bytes 4718592 | tf_op jit(solution)/shard_map/while/body/eval_jaxpr/convert_element_type | solution.py:36
  68.1 0.7 copy.33
  68.9 3.4 %fusion.4 = bf16[192,4,8,128]{3,2,0,1:T(8,128)(2,1)S(1)} fusion(bf16[192,4,8,192]{3,2,0,1:T(8,128)(2,1)} %copy.23, f32[192,4,8]{2,0,1:T(8,128)} %copy.24, f32[192,4,8]{2,0,1:T(8,128)} %copy.21, bf16[192,4,128]{2,0,1:T(8,128)(2,1)S(1)} %copy-done.1), kind=kOutput, calls=%fused_computation.8 | convolution fusion | flops 304349184 | bytes 4177920 | tf_op jit(solution)/shard_map/while/body/eval_jaxpr/rgek,kgc->rgec/dot_general | solution.py:34
  72.6 1.9 %copy.50 = bf16[24,8,32,128]{3,1,2,0:T(8,128)(2,1)} copy(bf16[24,8,32,128]{3,2,1,0:T(8,128)(2,1)S(1)} %bitcast.67) | data formatting | bytes 3145728
  74.8 14.7 %reduce-scatter.10.cloned.1.call-done = bf16[48,32]{1,0:T(8,128)(2,1)} async-done(((bf16[192,32]{1,0:T(8,128)(2,1)}), bf16[48,32]{1,0:T(8,128)(2,1)}) %reduce-scatter.10.cloned.1.call-update) | async-done | bytes 3088
  89.5 0.8 copy.34
  90.4 30.0 %reduce-scatter.8.cloned.1.call-done = bf16[48,4096]{1,0:T(8,128)(2,1)} async-done(((bf16[192,4096]{1,0:T(8,128)(2,1)}), bf16[48,4096]{1,0:T(8,128)(2,1)}) %reduce-scatter.8.cloned.1.call-update) | async-done | bytes 393232
  120.4 1.1 copy.39
  121.5 0.3 multiply_convert_fusion
  121.9 0.9 copy.51
  122.8 37.3 %all-gather.5.cloned.1.call-done = bf16[192,4096]{1,0:T(8,128)(2,1)} async-done(((bf16[48,4096]{1,0:T(8,128)(2,1)}), bf16[192,4096]{1,0:T(8,128)(2,1)}) %all-gather.5.cloned.1.call-update) | async-done | bytes 1572880 | tf_op jit(solution)/shard_map/all_gather | solution.py:125
  160.1 10.6 %convolution_convert_fusion = bf16[192,2048]{1,0:T(8,128)(2,1)} fusion(bf16[192,4096]{1,0:T(8,128)(2,1)} %all-gather.5.cloned.1.call-done, bf16[4096,2048]{1,0:T(8,128)(2,1)} %param.11), kind=kOutput, calls=%fused_computation.9 | convolution fusion | flops 3221618688 | bytes 19136512 | tf_op jit(solution)/shard_map/dot_general | solution.py:124
  (28 shorter events, 1.1 us)
Async XLA Ops:
  6.5 3.5 %copy-start = (bf16[48,512]{1,0:T(8,128)(2,1)S(1)}, bf16[48,512]{1,0:T(8,128)(2,1)}, u32[]{:S(2)}) copy-start(bf16[48,512]{1,0:T(8,128)(2,1)} %param.7) | copy-start | bytes 147460
  6.5 34.6 %all-gather.3.cloned.1.call-start = ((), (), s32[]{:S(2)}) async-start(), calls=%async_computation.2 | async-start | bytes 1966080 | tf_op jit(solution)/shard_map/all_gather | solution.py:79
  7.3 82.3 %reduce-scatter.10.cloned.1.call-start = ((), (), s32[]{:S(2)}) async-start(), calls=%async_computation.5 | async-start | bytes 61440
  64.2 4.7 %copy-start.1 = (bf16[192,4,128]{2,0,1:T(8,128)(2,1)S(1)}, bf16[192,4,128]{2,0,1:T(8,128)(2,1)}, u32[]{:S(2)}) copy-start(bf16[192,4,128]{2,0,1:T(8,128)(2,1)} %all_gather.14) | copy-start | bytes 589828
  68.8 51.6 %reduce-scatter.8.cloned.1.call-start = ((), (), s32[]{:S(2)}) async-start(), calls=%async_computation.4 | async-start | bytes 1966080
  72.6 2.1 %copy-start.2 = (s32[32]{0:T(128)S(1)}, s32[32]{0:T(128)}, u32[]{:S(2)}) copy-start(s32[32]{0:T(128)} %param.10) | copy-start | bytes 388
  74.5 85.6 %all-gather.5.cloned.1.call-start = ((), (), s32[]{:S(2)}) async-start(), calls=%async_computation.3 | async-start | bytes 1966080 | tf_op jit(solution)/shard_map/all_gather | solution.py:125
Sparse Core Ops, SparseCore 0:
  8.9 22.3 all-gather.2
  69.0 20.5 reduce-scatter.9
  92.2 28.1 reduce-scatter.7
  122.9 37.1 all-gather.4
where the time goes:
time: 178 us; the launch traced here: 177 us
  waiting for transfers between devices  82.8 us (47%)
  blocking collectives  40.4 us (23%)
  matrix products  18.4 us (10%)
  local copies, waits for them, and re-layouts  16.9 us (9%)
  between operations  13.3 us (7%)
  other arithmetic  5.11 us (3%)
    unnamed x6, waiting for transfers between devices  45.5 us
    all_gather x1, waiting for transfers between devices, per_device(): lax.all_gather(attended, 'kvring', axis=0, tiled=True)  37.3 us
    all_gather x1, blocking collectives, per_device(): lax.all_gather(key_rows, 'kvring', axis=0, tiled=True)  15.5 us
    all_gather x1, blocking collectives, per_device(): lax.all_gather(value_rows, 'kvring', axis=0, tiled=True)  14.7 us
    dot_general x1, matrix products, per_device(): jnp.dot(lax.all_gather(attended, 'kvring', axis=0, tiled=True), w_out, pr...  10.6 us
    pmax x1, blocking collectives, per_device(): top = lax.pmax(run_max, 'qring')  10.3 us
    unnamed x13, local copies, waits for them, and re-layouts  7.34 us
    reduce_sum x1, other arithmetic, attend_keys(): run_sum = run_sum * shrink + jnp.sum(weights, axis=-1)  4.63 us
  transfers between devices with their start and end apart: 4, of which 3 were waited for; matrix products, arithmetic and copies ran while one was open for 6% of the time, Pallas kernels for 0%

commit v1 on v0

--- a/solution.py
+++ b/solution.py
@@ -1,8 +1,11 @@
+import functools
 import math
 
 import jax
 import jax.numpy as jnp
 from jax import lax
+from jax.experimental import pallas as pl
+from jax.experimental.pallas import tpu as pltpu
 from jax.sharding import PartitionSpec as P
 
 HD = 128
@@ -63,7 +66,7 @@
     return lax.fori_loop(0, total_rows // block_size, one_block, state)
 
 
-def per_device(queries, keys, values, doc_ids, head_mask, w_out):
+def per_device_any_ring(queries, keys, values, doc_ids, head_mask, w_out):
     shard_rows = queries.shape[0]
     kv_local = keys.shape[1] // HD
     q_local = queries.shape[1] // HD
@@ -131,6 +134,200 @@
     )
 
 
+VMEM_LIMIT = 56 * 1024 * 1024
+LOG2E = math.log2(math.e)
+
+
+def small_ring(mesh):
+    return (mesh.shape["qring"], mesh.shape["kvring"], mesh.shape["head"]) == (4, 4, 1)
+
+
+def swap_along(array, axis_name, partner):
+    size = lax.axis_size(axis_name)
+    return lax.ppermute(array, axis_name, [(i, i ^ partner) for i in range(size)])
+
+
+def after(array, *others):
+    return lax.optimization_barrier((array, *others))[0]
+
+
+def slot_of(index, width, count):
+    slot = jnp.zeros_like(index)
+    for bound in range(1, count):
+        slot = slot + (index >= bound * width).astype(jnp.int32)
+    return slot
+
+
+def prep_kernel(rows, nq, nz, slots_a, slots_b, mask_ref, doc_ref, q_ref, qa_ref, qb_ref, bias_ref):
+    for slot in range(slots_a + slots_b):
+        block = q_ref[:, slot * HD : (slot + 1) * HD]
+        if slot < slots_a:
+            qa_ref[:, slot * HD : (slot + 1) * HD] = block
+        else:
+            qb_ref[:, (slot - slots_a) * HD : (slot - slots_a + 1) * HD] = block
+    quarter = rows * nz
+    total = quarter * nq
+    q_at = lax.axis_index("qring")
+    z_at = lax.axis_index("kvring")
+    doc = doc_ref[...]
+    row = lax.broadcasted_iota(jnp.int32, (quarter, 1), 0)
+    row_z = slot_of(row, rows, nz)
+    row_pos = q_at * quarter + (row_z ^ z_at) * rows + row - row_z * rows
+    col = lax.broadcasted_iota(jnp.int32, (1, total), 1)
+    col_q = slot_of(col, quarter, nq)
+    rest = col - col_q * quarter
+    col_z = slot_of(rest, rows, nz)
+    col_pos = (col_q ^ q_at) * quarter + (col_z ^ z_at) * rows + rest - col_z * rows
+    own_doc = jnp.sum(jnp.where(col == row_pos, doc, 0), axis=1, keepdims=True)
+    first = jnp.sum((doc < own_doc).astype(jnp.int32), axis=1, keepdims=True)
+    bias_ref[...] = jnp.where((col_pos >= first) & (col_pos <= row_pos), 0.0, NEG)
+
+
+def attend_slots(nz, slots, first_slot, kv_refs, q_refs, bias_ref, mask_ref, att_ref):
+    heads = mask_ref.shape[0]
+    kv_heads = kv_refs[0].shape[1] // (2 * HD)
+    scale = LOG2E / math.sqrt(HD)
+
+    def one_slot(slot):
+        head = first_slot + slot
+        at = pl.multiple_of(slot * HD, HD)
+        group = head // (heads // kv_heads)
+        k_at = pl.multiple_of(group * HD, HD)
+        v_at = pl.multiple_of((group + kv_heads) * HD, HD)
+        q = jnp.concatenate([ref[:, pl.ds(at, HD)] for ref in q_refs], axis=0)
+        k = jnp.concatenate([ref[:, pl.ds(k_at, HD)] for ref in kv_refs], axis=0)
+        v = jnp.concatenate([ref[:, pl.ds(v_at, HD)] for ref in kv_refs], axis=0)
+        scores = lax.dot_general(q, k, (((1,), (1,)), ((), ())), preferred_element_type=jnp.float32)
+        scores = scores * scale + bias_ref[...]
+        top = jnp.max(scores, axis=1, keepdims=True)
+        weights = jnp.exp2(scores - top)
+        total = jnp.sum(weights, axis=1, keepdims=True)
+        context = jnp.dot(weights.astype(jnp.bfloat16), v, preferred_element_type=jnp.float32)
+        keep = mask_ref[head].astype(jnp.float32)
+        att_ref[:, pl.ds(at, HD)] = (context * (keep / total)).astype(jnp.bfloat16)
+
+    pl.loop(0, slots, unroll=UNROLL)(one_slot)
+
+
+UNROLL = 2
+
+
+def w_copies(slots, first_slot, w_hbm, w_ref, sem):
+    return [
+        pltpu.make_async_copy(
+            w_hbm.at[pl.ds((first_slot + slot) * HD, HD)],
+            w_ref.at[pl.ds(slot * HD, HD)],
+            sem.at[slot],
+        )
+        for slot in range(slots)
+    ]
+
+
+def first_kernel(nq, nz, slots, mask_ref, *refs):
+    kv_refs, q_refs, (bias_ref, w_hbm, acc_ref, att_ref, w_ref, sem) = refs[:nq], refs[nq : nq + nz], refs[nq + nz :]
+    copies = w_copies(slots, 0, w_hbm, w_ref, sem)
+    for copy in copies:
+        copy.start()
+    attend_slots(nz, slots, 0, kv_refs, q_refs, bias_ref, mask_ref, att_ref)
+    for copy in copies:
+        copy.wait()
+    width = 512
+
+    def one_tile(tile):
+        at = pl.ds(pl.multiple_of(tile * width, width), width)
+        acc_ref[:, at] = jnp.dot(att_ref[...], w_ref[:, at], preferred_element_type=jnp.float32)
+
+    pl.loop(0, acc_ref.shape[1] // width)(one_tile)
+
+
+def last_kernel(nq, nz, first_slot, slots, mask_ref, *refs):
+    kv_refs, q_refs, (bias_ref, w_hbm, acc_ref, out_ref, att_ref, w_ref, sem) = refs[:nq], refs[nq : nq + nz], refs[nq + nz :]
+    copies = w_copies(slots, first_slot, w_hbm, w_ref, sem)
+    for copy in copies:
+        copy.start()
+    attend_slots(nz, slots, first_slot, kv_refs, q_refs, bias_ref, mask_ref, att_ref)
+    for copy in copies:
+        copy.wait()
+    width = 512
+    rows = q_refs[0].shape[0]
+    z_at = lax.axis_index("kvring")
+
+    def one_tile(tile):
+        at = pl.ds(pl.multiple_of(tile * width, width), width)
+        mixed = acc_ref[:, at] + jnp.dot(att_ref[...], w_ref[:, at], preferred_element_type=jnp.float32)
+        mixed = mixed.astype(jnp.bfloat16)
+        for slot in range(nz):
+            place = pl.multiple_of((z_at ^ slot) * rows, rows)
+            out_ref[pl.ds(place, rows), at] = mixed[slot * rows : (slot + 1) * rows]
+
+    pl.loop(0, acc_ref.shape[1] // width)(one_tile)
+
+
+def per_device_small_ring(queries, keys, values, doc_ids, head_mask, w_out):
+    rows = queries.shape[0]
+    nq = lax.axis_size("qring")
+    nz = lax.axis_size("kvring")
+    heads = head_mask.shape[0]
+    width = w_out.shape[1]
+    quarter = rows * nz
+    total = quarter * nq
+    slots_b = heads // 4
+    slots_a = heads - slots_b
+    smem = pl.BlockSpec(memory_space=pltpu.SMEM)
+    vmem = pl.BlockSpec(memory_space=pltpu.VMEM)
+    hbm = pl.BlockSpec(memory_space=pl.ANY)
+
+    kv_own = jnp.concatenate([keys, values], axis=1)
+    kv_parts = [kv_own] + [swap_along(kv_own, "kvring", m) for m in range(1, nz)]
+    qa, qb, bias = pl.pallas_call(
+        functools.partial(prep_kernel, rows, nq, nz, slots_a, slots_b),
+        out_shape=(
+            jax.ShapeDtypeStruct((rows, slots_a * HD), jnp.bfloat16),
+            jax.ShapeDtypeStruct((rows, slots_b * HD), jnp.bfloat16),
+            jax.ShapeDtypeStruct((quarter, total), jnp.float32),
+        ),
+        in_specs=[smem, vmem, vmem],
+        out_specs=(vmem, vmem, vmem),
+        name="prep",
+    )(head_mask, doc_ids.reshape(1, total), queries)
+    kv0 = jnp.concatenate(kv_parts, axis=0)
+    kv2 = swap_along(kv0, "qring", 2)
+    kv1 = swap_along(kv0, "qring", 1)
+    kv3 = swap_along(kv2, "qring", 1)
+    kv = (kv0, kv1, kv2, kv3)
+    qa = after(qa, kv_parts[1])
+    qa_parts = [qa] + [swap_along(qa, "kvring", m) for m in range(1, nz)]
+    qb_parts = [qb] + [swap_along(after(qb, qa_parts[m]), "kvring", m) for m in range(1, nz)]
+
+    params = pltpu.CompilerParams(vmem_limit_bytes=VMEM_LIMIT)
+    acc = pl.pallas_call(
+        functools.partial(first_kernel, nq, nz, slots_a),
+        out_shape=jax.ShapeDtypeStruct((quarter, width), jnp.float32),
+        in_specs=[smem] + [vmem] * (nq + nz + 1) + [hbm],
+        out_specs=vmem,
+        scratch_shapes=[
+            pltpu.VMEM((quarter, slots_a * HD), jnp.bfloat16),
+            pltpu.VMEM((slots_a * HD, width), jnp.bfloat16),
+            pltpu.SemaphoreType.DMA((slots_a,)),
+        ],
+        compiler_params=params,
+        name="first",
+    )(head_mask, *kv, *qa_parts, bias, w_out)
+    return pl.pallas_call(
+        functools.partial(last_kernel, nq, nz, slots_a, slots_b),
+        out_shape=jax.ShapeDtypeStruct((quarter, width), jnp.bfloat16),
+        in_specs=[smem] + [vmem] * (nq + nz + 1) + [hbm, vmem],
+        out_specs=vmem,
+        scratch_shapes=[
+            pltpu.VMEM((quarter, slots_b * HD), jnp.bfloat16),
+            pltpu.VMEM((slots_b * HD, width), jnp.bfloat16),
+            pltpu.SemaphoreType.DMA((slots_b,)),
+        ],
+        compiler_params=params,
+        name="last",
+    )(head_mask, *kv, *qb_parts, bias, w_out, acc)
+
+
 def solution(mesh):
     placed = (
         P(("groups", "qring", "kvring"), "head"),
@@ -140,6 +337,7 @@
         P("head"),
         P("head", "kvring"),
     )
+    per_device = per_device_small_ring if small_ring(mesh) else per_device_any_ring
     return jax.shard_map(
         per_device,
         mesh=mesh,

time: 178 us -> 78.9 us (0.44)
  waiting for transfers between devices: 82.8 us -> 20.6 us
  blocking collectives: 40.4 us -> 0 us
  Pallas kernels: 0 us -> 28.4 us
  starting transfers between devices: 0.31 us -> 24.3 us
  matrix products: 18.4 us -> 0 us
  between operations: 13.3 us -> 0.14 us
  local copies, waits for them, and re-layouts: 16.9 us -> 5.09 us
  other arithmetic: 5.11 us -> 0.03 us
    unnamed x6 -> x0, waiting for transfers between devices: 45.5 us -> none
    all_gather x2 -> x0, waiting for transfers between devices: 37.3 us -> none  [the longest x1 37.3 us: per_device(): lax.all_gather(attended, 'kvring', axis=0, tiled=True)]
    all_gather x2 -> x0, blocking collectives: 30.1 us -> none  [the longest x1 15.5 us: per_device(): lax.all_gather(key_rows, 'kvring', axis=0, tiled=True)]
    pallas_call x0 -> x3, Pallas kernels: none -> 28.4 us  [the longest x1 17.7 us: per_device_small_ring(): pl.pallas_call(functools.partial(first_kernel, nq, nz, slots_a), out_shap...]
    ppermute x0 -> x12, starting transfers between devices: none -> 24.3 us  [swap_along(): lax.ppermute(array, axis_name, [(i, i ^ partner) for i in range(size)])]
    ppermute x0 -> x12, waiting for transfers between devices: none -> 20.6 us  [swap_along(): lax.ppermute(array, axis_name, [(i, i ^ partner) for i in range(size)])]
    dot_general x3 -> x0, matrix products: 18.4 us -> none  [the longest x1 10.6 us: per_device(): jnp.dot(lax.all_gather(attended, 'kvring', axis=0, tiled=True), w_out, pr...]
    pmax x1 -> x0, blocking collectives: 10.3 us -> none  [per_device(): top = lax.pmax(run_max, 'qring')]
  transfers between devices with their start and end apart: 4 -> 12, of which waited for: 3 -> 6; matrix products, arithmetic and copies ran while one was open for 6% -> 2% of each run, Pallas kernels for 0% -> 25%
where the time goes in v1:
time: 78.9 us; the launch traced here: 78.6 us
  Pallas kernels  28.4 us (36%)
  starting transfers between devices  24.3 us (31%)
  waiting for transfers between devices  20.6 us (26%)
  local copies, waits for them, and re-layouts  5.09 us (6%)
    ppermute x12, starting transfers between devices, swap_along(): lax.ppermute(array, axis_name, [(i, i ^ partner) for i in range(size)])  24.3 us
    ppermute x12, waiting for transfers between devices, swap_along(): lax.ppermute(array, axis_name, [(i, i ^ partner) for i in range(size)])  20.6 us
    pallas_call x1, Pallas kernels, per_device_small_ring(): pl.pallas_call(functools.partial(first_kernel, nq, nz, slots_a), out_shap...  17.7 us
    pallas_call x1, Pallas kernels, per_device_small_ring(): pl.pallas_call(functools.partial(last_kernel, nq, nz, slots_a, slots_b),...  8.51 us
    unnamed x21, local copies, waits for them, and re-layouts  3 us
    pallas_call x1, Pallas kernels, per_device_small_ring(): pl.pallas_call(functools.partial(prep_kernel, rows, nq, nz, slots_a, slot...  2.2 us
  transfers between devices with their start and end apart: 12, of which 6 were waited for; matrix products, arithmetic and copies ran while one was open for 2% of the time, Pallas kernels for 25%

profile of v1, /device:TPU:0, one launch (start us, length us, event | category | flops | bytes accessed | tf_op | source)
XLA Modules:
  0.0 78.6 jit_solution(2370769990950888807)
XLA Ops:
  0.0 0.8 %constant_dynamic-update-slice_fusion.1 = bf16[48,1024]{1,0:T(8,128)(2,1)S(1)} fusion(bf16[48,512]{1,0:T(8,128)(2,1)} %param.7), kind=kLoop, calls=%fused_computation.2 | loop fusion | bytes 98304
  0.8 0.8 %constant_dynamic-update-slice_fusion = bf16[48,1024]{1,0:T(8,128)(2,1)S(1)} fusion(bf16[48,1024]{1,0:T(8,128)(2,1)S(1)} %constant_dynamic-update-slice_fusion.1, bf16[48,512]{1,0:T(8,128)(2,1)} %param.8), kind=kLoop, calls=%fused_computation.1 | loop fusion | bytes 98304 | tf_op jit(solution)/shard_map/concatenate | solution.py:280
  1.6 3.0 %collective-permute-start = (bf16[48,1024]{1,0:T(8,128)(2,1)S(1)}, bf16[48,1024]{1,0:T(8,128)(2,1)S(1)}, u32[]{:S(2)}, u32[]{:S(2)}) collective-permute-start(bf16[48,1024]{1,0:T(8,128)(2,1)S(1)} %constant_dynamic-update-slice_fusion), channel_id=1, source_target_pairs={{0,1},{1,0},{2,3},{3,2},{4,5},{5,4},{6,7},{7,6},{8,9},{9,8},{10,11... | collective-permute-start | bytes 294920 | tf_op jit(solution)/shard_map/ppermute | solution.py:147
  4.6 2.6 %collective-permute-start.1 = (bf16[48,1024]{1,0:T(8,128)(2,1)S(1)}, bf16[48,1024]{1,0:T(8,128)(2,1)S(1)}, u32[]{:S(2)}, u32[]{:S(2)}) collective-permute-start(bf16[48,1024]{1,0:T(8,128)(2,1)S(1)} %constant_dynamic-update-slice_fusion), channel_id=1, source_target_pairs={{0,2},{1,3},{2,0},{3,1},{4,6},{5,7},{6,4},{7,5},{8,10},{9,11},{10,... | collective-permute-start | bytes 294920 | tf_op jit(solution)/shard_map/ppermute | solution.py:147
  7.2 0.2 collective-permute-done
  7.4 7.6 %collective-permute-done.1 = bf16[48,1024]{1,0:T(8,128)(2,1)S(1)} collective-permute-done((bf16[48,1024]{1,0:T(8,128)(2,1)S(1)}, bf16[48,1024]{1,0:T(8,128)(2,1)S(1)}, u32[]{:S(2)}, u32[]{:S(2)}) %collective-permute-start.1) | collective-permute-done | bytes 98336 | tf_op jit(solution)/shard_map/ppermute | solution.py:147
  15.1 1.6 %collective-permute-start.4 = (bf16[192,1024]{1,0:T(8,128)(2,1)S(1)}, bf16[192,1024]{1,0:T(8,128)(2,1)S(1)}, u32[]{:S(2)}, u32[]{:S(2)}) collective-permute-start(bf16[192,1024]{1,0:T(8,128)(2,1)S(1)} %pad_maximum_fusion.refs_0_), channel_id=1, source_target_pairs={{0,8},{4,12},{8,0},{12,4},{1,9},{5,13},{9,1},{13,5},{2,10},{6,14},... | collective-permute-start | bytes 1179656 | tf_op jit(solution)/shard_map/ppermute | solution.py:147
  16.7 1.3 %reshape.3.doc_ref = s32[1,768]{1,0:T(1,128)} reshape(s32[768]{0:T(1024)} %param.9) | data formatting | bytes 6144 | tf_op jit(solution)/shard_map/reshape | solution.py:292
  17.9 2.2 %prep.1 = (bf16[48,3072]{1,0:T(8,128)(2,1)}, bf16[48,1024]{1,0:T(8,128)(2,1)}, f32[192,768]{1,0:T(8,128)}) custom-call(s32[32]{0:T(128)} %mask_ref.5, s32[1,768]{1,0:T(1,128)} %reshape.3.doc_ref, bf16[48,4096]{1,0:T(8,128)(2,1)} %q_ref.1), custom_call_target="tpu_custom_call" | custom-call | tf_op jit(solution)/shard_map/prep/pallas_call | solution.py:282
  20.1 2.5 %collective-permute-start.10 = (bf16[48,3072]{1,0:T(8,128)(2,1)}, bf16[48,3072]{1,0:T(8,128)(2,1)S(1)}, u32[]{:S(2)}, u32[]{:S(2)}) collective-permute-start(bf16[48,3072]{1,0:T(8,128)(2,1)} %get-tuple-element.14.refs_4_), channel_id=1, source_target_pairs={{0,3},{1,2},{2,1},{3,0},{4,7},{5,6},{6,5},{7,4},{8,11},{9,10},{10,... | collective-permute-start | bytes 884744 | tf_op jit(solution)/shard_map/ppermute | solution.py:147
  22.6 0.7 collective-permute-start.6
  23.3 0.8 %collective-permute-done.4.refs_2_ = bf16[192,1024]{1,0:T(8,128)(2,1)S(1)} collective-permute-done((bf16[192,1024]{1,0:T(8,128)(2,1)S(1)}, bf16[192,1024]{1,0:T(8,128)(2,1)S(1)}, u32[]{:S(2)}, u32[]{:S(2)}) %collective-permute-start.4) | collective-permute-done | bytes 393248 | tf_op jit(solution)/shard_map/ppermute | solution.py:147
  24.1 3.3 %collective-permute-start.8 = (bf16[48,3072]{1,0:T(8,128)(2,1)}, bf16[48,3072]{1,0:T(8,128)(2,1)S(1)}, u32[]{:S(2)}, u32[]{:S(2)}) collective-permute-start(bf16[48,3072]{1,0:T(8,128)(2,1)} %get-tuple-element.14.refs_4_), channel_id=1, source_target_pairs={{0,2},{1,3},{2,0},{3,1},{4,6},{5,7},{6,4},{7,5},{8,10},{9,11},{10,... | collective-permute-start | bytes 884744 | tf_op jit(solution)/shard_map/ppermute | solution.py:147
  27.5 4.7 %collective-permute-done.10.refs_7_ = bf16[48,3072]{1,0:T(8,128)(2,1)S(1)} collective-permute-done((bf16[48,3072]{1,0:T(8,128)(2,1)}, bf16[48,3072]{1,0:T(8,128)(2,1)S(1)}, u32[]{:S(2)}, u32[]{:S(2)}) %collective-permute-start.10) | collective-permute-done | bytes 294944 | tf_op jit(solution)/shard_map/ppermute | solution.py:147
  32.1 0.9 %collective-permute-start.11 = (bf16[48,1024]{1,0:T(8,128)(2,1)}, bf16[48,1024]{1,0:T(8,128)(2,1)S(1)}, u32[]{:S(2)}, u32[]{:S(2)}) collective-permute-start(bf16[48,1024]{1,0:T(8,128)(2,1)} %get-tuple-element.17.refs_4_), channel_id=1, source_target_pairs={{0,3},{1,2},{2,1},{3,0},{4,7},{5,6},{6,5},{7,4},{8,11},{9,10},{10,... | collective-permute-start | bytes 294920 | tf_op jit(solution)/shard_map/ppermute | solution.py:147
  33.0 2.1 %collective-permute-done.6.refs_5_ = bf16[48,3072]{1,0:T(8,128)(2,1)S(1)} collective-permute-done((bf16[48,3072]{1,0:T(8,128)(2,1)}, bf16[48,3072]{1,0:T(8,128)(2,1)S(1)}, u32[]{:S(2)}, u32[]{:S(2)}) %collective-permute-start.6) | collective-permute-done | bytes 294944 | tf_op jit(solution)/shard_map/ppermute | solution.py:147
  35.1 9.7 %collective-permute-start.7 = (bf16[48,1024]{1,0:T(8,128)(2,1)}, bf16[48,1024]{1,0:T(8,128)(2,1)S(1)}, u32[]{:S(2)}, u32[]{:S(2)}) collective-permute-start(bf16[48,1024]{1,0:T(8,128)(2,1)} %get-tuple-element.17.refs_4_), channel_id=1, source_target_pairs={{0,1},{1,0},{2,3},{3,2},{4,5},{5,4},{6,7},{7,6},{8,9},{9,8},{10,11... | collective-permute-start | bytes 294920 | tf_op jit(solution)/shard_map/ppermute | solution.py:147
  44.8 5.1 %collective-permute-done.8.refs_6_ = bf16[48,3072]{1,0:T(8,128)(2,1)S(1)} collective-permute-done((bf16[48,3072]{1,0:T(8,128)(2,1)}, bf16[48,3072]{1,0:T(8,128)(2,1)S(1)}, u32[]{:S(2)}, u32[]{:S(2)}) %collective-permute-start.8) | collective-permute-done | bytes 294944 | tf_op jit(solution)/shard_map/ppermute | solution.py:147
  50.1 0.6 copy-done.6
  50.8 0.1 copy-done.3
  51.0 17.7 %first.1.refs_10_ = f32[192,2048]{1,0:T(8,128)} custom-call(s32[32]{0:T(128)} %mask_ref.5, bf16[192,1024]{1,0:T(8,128)(2,1)} %copy-done, bf16[192,1024]{1,0:T(8,128)(2,1)} %copy-done.2, bf16[192,1024]{1,0:T(8,128)(2,1)} %copy-done.1, bf16[192,1024]{1,0:T(8,128)(2,1)} %copy-done.3, bf16[48,3072]{1,0:T(8,128)(2,1)} %get-tuple-element.14.refs_4_, ...), custom_call_target="tpu_custom_call" | custom-call | tf_op jit(solution)/shard_map/first/pallas_call | solution.py:303
  68.8 0.6 copy-done.7
  69.4 0.6 copy-done.9
  70.1 8.5 %last.1 = bf16[192,2048]{1,0:T(8,128)(2,1)} custom-call(s32[32]{0:T(128)} %mask_ref.5, bf16[192,1024]{1,0:T(8,128)(2,1)} %copy-done, bf16[192,1024]{1,0:T(8,128)(2,1)} %copy-done.2, bf16[192,1024]{1,0:T(8,128)(2,1)} %copy-done.1, bf16[192,1024]{1,0:T(8,128)(2,1)} %copy-done.3, bf16[48,1024]{1,0:T(8,128)(2,1)} %get-tuple-element.17.refs_4_, ...), custom_call_target="tpu_custom_call" | custom-call | tf_op jit(solution)/shard_map/last/pallas_call | solution.py:316
  (27 shorter events, 0.3 us)
Async XLA Ops:
  1.6 5.8 %collective-permute-start = (bf16[48,1024]{1,0:T(8,128)(2,1)S(1)}, bf16[48,1024]{1,0:T(8,128)(2,1)S(1)}, u32[]{:S(2)}, u32[]{:S(2)}) collective-permute-start(bf16[48,1024]{1,0:T(8,128)(2,1)S(1)} %constant_dynamic-update-slice_fusion), channel_id=1, source_target_pairs={{0,1},{1,0},{2,3},{3,2},{4,5},{5,4},{6,7},{7,6},{8,9},{9,8},{10,11... | collective-permute-start | bytes 294920 | tf_op jit(solution)/shard_map/ppermute | solution.py:147
  4.6 10.4 %collective-permute-start.1 = (bf16[48,1024]{1,0:T(8,128)(2,1)S(1)}, bf16[48,1024]{1,0:T(8,128)(2,1)S(1)}, u32[]{:S(2)}, u32[]{:S(2)}) collective-permute-start(bf16[48,1024]{1,0:T(8,128)(2,1)S(1)} %constant_dynamic-update-slice_fusion), channel_id=1, source_target_pairs={{0,2},{1,3},{2,0},{3,1},{4,6},{5,7},{6,4},{7,5},{8,10},{9,11},{10,... | collective-permute-start | bytes 294920 | tf_op jit(solution)/shard_map/ppermute | solution.py:147
  7.2 7.8 %collective-permute-start.2 = (bf16[48,1024]{1,0:T(8,128)(2,1)S(1)}, bf16[48,1024]{1,0:T(8,128)(2,1)S(1)}, u32[]{:S(2)}, u32[]{:S(2)}) collective-permute-start(bf16[48,1024]{1,0:T(8,128)(2,1)S(1)} %constant_dynamic-update-slice_fusion), channel_id=1, source_target_pairs={{0,3},{1,2},{2,1},{3,0},{4,7},{5,6},{6,5},{7,4},{8,11},{9,10},{10,... | collective-permute-start | bytes 294920 | tf_op jit(solution)/shard_map/ppermute | solution.py:147
  15.1 35.0 %copy-start = (bf16[192,1024]{1,0:T(8,128)(2,1)}, bf16[192,1024]{1,0:T(8,128)(2,1)S(1)}, u32[]{:S(2)}) copy-start(bf16[192,1024]{1,0:T(8,128)(2,1)S(1)} %pad_maximum_fusion.refs_0_) | copy-start | bytes 1179652
  15.1 9.0 %collective-permute-start.4 = (bf16[192,1024]{1,0:T(8,128)(2,1)S(1)}, bf16[192,1024]{1,0:T(8,128)(2,1)S(1)}, u32[]{:S(2)}, u32[]{:S(2)}) collective-permute-start(bf16[192,1024]{1,0:T(8,128)(2,1)S(1)} %pad_maximum_fusion.refs_0_), channel_id=1, source_target_pairs={{0,8},{4,12},{8,0},{12,4},{1,9},{5,13},{9,1},{13,5},{2,10},{6,14},... | collective-permute-start | bytes 1179656 | tf_op jit(solution)/shard_map/ppermute | solution.py:147
  20.1 12.0 %collective-permute-start.10 = (bf16[48,3072]{1,0:T(8,128)(2,1)}, bf16[48,3072]{1,0:T(8,128)(2,1)S(1)}, u32[]{:S(2)}, u32[]{:S(2)}) collective-permute-start(bf16[48,3072]{1,0:T(8,128)(2,1)} %get-tuple-element.14.refs_4_), channel_id=1, source_target_pairs={{0,3},{1,2},{2,1},{3,0},{4,7},{5,6},{6,5},{7,4},{8,11},{9,10},{10,... | collective-permute-start | bytes 884744 | tf_op jit(solution)/shard_map/ppermute | solution.py:147
  22.6 12.5 %collective-permute-start.6 = (bf16[48,3072]{1,0:T(8,128)(2,1)}, bf16[48,3072]{1,0:T(8,128)(2,1)S(1)}, u32[]{:S(2)}, u32[]{:S(2)}) collective-permute-start(bf16[48,3072]{1,0:T(8,128)(2,1)} %get-tuple-element.14.refs_4_), channel_id=1, source_target_pairs={{0,1},{1,0},{2,3},{3,2},{4,5},{5,4},{6,7},{7,6},{8,9},{9,8},{10,11... | collective-permute-start | bytes 884744 | tf_op jit(solution)/shard_map/ppermute | solution.py:147
  23.3 26.7 %collective-permute-start.3 = (bf16[192,1024]{1,0:T(8,128)(2,1)S(1)}, bf16[192,1024]{1,0:T(8,128)(2,1)S(1)}, u32[]{:S(2)}, u32[]{:S(2)}) collective-permute-start(bf16[192,1024]{1,0:T(8,128)(2,1)S(1)} %pad_maximum_fusion.refs_0_), channel_id=1, source_target_pairs={{0,4},{4,0},{8,12},{12,8},{1,5},{5,1},{9,13},{13,9},{2,6},{6,2},{1... | collective-permute-start | bytes 1179656 | tf_op jit(solution)/shard_map/ppermute | solution.py:147
  24.1 25.9 %copy-start.1 = (bf16[192,1024]{1,0:T(8,128)(2,1)}, bf16[192,1024]{1,0:T(8,128)(2,1)S(1)}, u32[]{:S(2)}) copy-start(bf16[192,1024]{1,0:T(8,128)(2,1)S(1)} %collective-permute-done.4.refs_2_) | copy-start | bytes 1179652
  24.1 25.9 %collective-permute-start.5 = (bf16[192,1024]{1,0:T(8,128)(2,1)S(1)}, bf16[192,1024]{1,0:T(8,128)(2,1)S(1)}, u32[]{:S(2)}, u32[]{:S(2)}) collective-permute-start(bf16[192,1024]{1,0:T(8,128)(2,1)S(1)} %collective-permute-done.4.refs_2_), channel_id=1, source_target_pairs={{0,4},{4,0},{8,12},{12,8},{1,5},{5,1},{9,13},{13,9},{2,6},{6,2},{1... | collective-permute-start | bytes 1179656 | tf_op jit(solution)/shard_map/ppermute | solution.py:147
  24.1 25.8 %collective-permute-start.8 = (bf16[48,3072]{1,0:T(8,128)(2,1)}, bf16[48,3072]{1,0:T(8,128)(2,1)S(1)}, u32[]{:S(2)}, u32[]{:S(2)}) collective-permute-start(bf16[48,3072]{1,0:T(8,128)(2,1)} %get-tuple-element.14.refs_4_), channel_id=1, source_target_pairs={{0,2},{1,3},{2,0},{3,1},{4,6},{5,7},{6,4},{7,5},{8,10},{9,11},{10,... | collective-permute-start | bytes 884744 | tf_op jit(solution)/shard_map/ppermute | solution.py:147
  32.1 17.9 %copy-start.4 = (bf16[48,3072]{1,0:T(8,128)(2,1)}, bf16[48,3072]{1,0:T(8,128)(2,1)S(1)}, u32[]{:S(2)}) copy-start(bf16[48,3072]{1,0:T(8,128)(2,1)S(1)} %collective-permute-done.10.refs_7_) | copy-start | bytes 884740
  32.1 36.6 %collective-permute-start.11 = (bf16[48,1024]{1,0:T(8,128)(2,1)}, bf16[48,1024]{1,0:T(8,128)(2,1)S(1)}, u32[]{:S(2)}, u32[]{:S(2)}) collective-permute-start(bf16[48,1024]{1,0:T(8,128)(2,1)} %get-tuple-element.17.refs_4_), channel_id=1, source_target_pairs={{0,3},{1,2},{2,1},{3,0},{4,7},{5,6},{6,5},{7,4},{8,11},{9,10},{10,... | collective-permute-start | bytes 294920 | tf_op jit(solution)/shard_map/ppermute | solution.py:147
  35.1 14.9 %copy-start.5 = (bf16[48,3072]{1,0:T(8,128)(2,1)}, bf16[48,3072]{1,0:T(8,128)(2,1)S(1)}, u32[]{:S(2)}) copy-start(bf16[48,3072]{1,0:T(8,128)(2,1)S(1)} %collective-permute-done.6.refs_5_) | copy-start | bytes 884740
  35.1 33.6 %collective-permute-start.7 = (bf16[48,1024]{1,0:T(8,128)(2,1)}, bf16[48,1024]{1,0:T(8,128)(2,1)S(1)}, u32[]{:S(2)}, u32[]{:S(2)}) collective-permute-start(bf16[48,1024]{1,0:T(8,128)(2,1)} %get-tuple-element.17.refs_4_), channel_id=1, source_target_pairs={{0,1},{1,0},{2,3},{3,2},{4,5},{5,4},{6,7},{7,6},{8,9},{9,8},{10,11... | collective-permute-start | bytes 294920 | tf_op jit(solution)/shard_map/ppermute | solution.py:147
  50.0 0.7 copy-start.6
  50.0 18.8 %collective-permute-start.9 = (bf16[48,1024]{1,0:T(8,128)(2,1)}, bf16[48,1024]{1,0:T(8,128)(2,1)S(1)}, u32[]{:S(2)}, u32[]{:S(2)}) collective-permute-start(bf16[48,1024]{1,0:T(8,128)(2,1)} %get-tuple-element.17.refs_4_), channel_id=1, source_target_pairs={{0,2},{1,3},{2,0},{3,1},{4,6},{5,7},{6,4},{7,5},{8,10},{9,11},{10,... | collective-permute-start | bytes 294920 | tf_op jit(solution)/shard_map/ppermute | solution.py:147
  50.0 0.8 %copy-start.2 = (bf16[192,1024]{1,0:T(8,128)(2,1)}, bf16[192,1024]{1,0:T(8,128)(2,1)S(1)}, u32[]{:S(2)}) copy-start(bf16[192,1024]{1,0:T(8,128)(2,1)S(1)} %collective-permute-done.3.refs_1_) | copy-start | bytes 1179652
  50.0 1.0 %copy-start.3 = (bf16[192,1024]{1,0:T(8,128)(2,1)}, bf16[192,1024]{1,0:T(8,128)(2,1)S(1)}, u32[]{:S(2)}) copy-start(bf16[192,1024]{1,0:T(8,128)(2,1)S(1)} %collective-permute-done.5.refs_3_) | copy-start | bytes 1179652
  68.7 0.6 copy-start.7
  68.8 0.7 copy-start.8
  69.4 0.6 copy-start.9

commit v2 on v0

--- a/solution.py
+++ b/solution.py
@@ -1,8 +1,11 @@
+import functools
 import math
 
 import jax
 import jax.numpy as jnp
 from jax import lax
+from jax.experimental import pallas as pl
+from jax.experimental.pallas import tpu as pltpu
 from jax.sharding import PartitionSpec as P
 
 HD = 128
@@ -63,7 +66,7 @@
     return lax.fori_loop(0, total_rows // block_size, one_block, state)
 
 
-def per_device(queries, keys, values, doc_ids, head_mask, w_out):
+def per_device_any_ring(queries, keys, values, doc_ids, head_mask, w_out):
     shard_rows = queries.shape[0]
     kv_local = keys.shape[1] // HD
     q_local = queries.shape[1] // HD
@@ -131,6 +134,296 @@
     )
 
 
+VMEM_LIMIT = 32 * 1024 * 1024
+LOG2E = math.log2(math.e)
+PAIR = 2
+NEAR_SPLIT = (8, 6)
+NEAR_SLOTS = sum(NEAR_SPLIT)
+FAR_SLOTS = 12
+TILE = 1024
+
+
+def small_ring(mesh):
+    return (mesh.shape["qring"], mesh.shape["kvring"], mesh.shape["head"]) == (4, 4, 1)
+
+
+def swap_along(array, axis_name, partner):
+    size = lax.axis_size(axis_name)
+    return lax.ppermute(array, axis_name, [(i, i ^ partner) for i in range(size)])
+
+
+def swaps_along(array, axis_name):
+    return [swap_along(array, axis_name, partner) for partner in range(1, lax.axis_size(axis_name))]
+
+
+def in_vmem(*arrays):
+    return [pltpu.with_memory_space_constraint(array, pltpu.VMEM) for array in arrays]
+
+
+def slot_of(index, width, count):
+    slot = jnp.zeros_like(index)
+    for bound in range(1, count):
+        slot = slot + (index >= bound * width).astype(jnp.int32)
+    return slot
+
+
+def rows_of(slot):
+    return pl.ds(pl.multiple_of(slot * HD, HD), HD)
+
+
+def join_kernel(k_ref, v_ref, out_ref):
+    width = k_ref.shape[1]
+    out_ref[:, :width] = k_ref[...]
+    out_ref[:, width:] = v_ref[...]
+
+
+def prep_kernel(rows, nq, nz, mask_ref, doc_ref, q_ref, order_ref, *refs):
+    *slot_refs, bias_ref = refs
+    heads = mask_ref.shape[0]
+    for slot in range(heads):
+        order_ref[slot] = 0
+    kept = jnp.int32(0)
+    for head in range(heads):
+        order_ref[kept] = head
+        kept = kept + mask_ref[head]
+    order_ref[heads] = kept
+    slot = 0
+    for ref in slot_refs:
+        for place in range(ref.shape[0]):
+            ref[place] = q_ref[:, rows_of(order_ref[slot])]
+            slot += 1
+    quarter = rows * nz
+    total = quarter * nq
+    q_at = lax.axis_index("qring")
+    z_at = lax.axis_index("kvring")
+    doc = doc_ref[...].reshape(1, total)
+    row = lax.broadcasted_iota(jnp.int32, (quarter, 1), 0)
+    row_z = slot_of(row, rows, nz)
+    row_pos = q_at * quarter + (row_z ^ z_at) * rows + row - row_z * rows
+    col = lax.broadcasted_iota(jnp.int32, (1, total), 1)
+    col_q = slot_of(col, quarter, nq)
+    rest = col - col_q * quarter
+    col_z = slot_of(rest, rows, nz)
+    col_pos = (col_q ^ q_at) * quarter + (col_z ^ z_at) * rows + rest - col_z * rows
+    own_doc = jnp.sum(jnp.where(col == row_pos, doc, 0), axis=1, keepdims=True)
+    first = jnp.sum((doc < own_doc).astype(jnp.int32), axis=1, keepdims=True)
+    bias_ref[...] = jnp.where((col_pos >= first) & (col_pos <= row_pos), 0.0, NEG)
+
+
+def kv_at(slot, kv_refs, order_ref, is_value):
+    heads = order_ref.shape[0] - 1
+    kv_heads = kv_refs[0].shape[1] // (2 * HD)
+    group = order_ref[slot] // (heads // kv_heads) + is_value * kv_heads
+    return jnp.concatenate([ref[:, rows_of(group)] for ref in kv_refs], axis=0)
+
+
+def scores_of(q, slot, kv_refs, order_ref):
+    k = kv_at(slot, kv_refs, order_ref, 0)
+    return lax.dot_general(q, k, (((1,), (1,)), ((), ())), preferred_element_type=jnp.float32)
+
+
+def attended(scores, bias, slot, kv_refs, order_ref):
+    scores = scores * (LOG2E / math.sqrt(HD)) + bias
+    weights = jnp.exp2(scores - jnp.max(scores, axis=1, keepdims=True))
+    v = kv_at(slot, kv_refs, order_ref, 1)
+    v_and_ones = jnp.concatenate([v, jnp.ones_like(v)], axis=1)
+    sums = jnp.dot(weights.astype(jnp.bfloat16), v_and_ones, preferred_element_type=jnp.float32)
+    keep = (slot < order_ref[order_ref.shape[0] - 1]).astype(jnp.float32)
+    return (sums[:, :HD] * (keep / sums[:, HD:])).astype(jnp.bfloat16)
+
+
+def own_kernel(nq, order_ref, *refs):
+    kv_refs, (q_ref, bias_ref, att_ref) = refs[:nq], refs[nq:]
+    rows = q_ref.shape[1]
+
+    def one_slot(slot):
+        scores = scores_of(q_ref[slot], slot, kv_refs, order_ref)
+        att_ref[slot] = attended(scores, bias_ref[:rows], slot, kv_refs, order_ref)
+
+    pl.loop(0, FAR_SLOTS, unroll=FAR_SLOTS // 2)(one_slot)
+
+
+def first_kernel(nq, nz, order_ref, *refs):
+    queries = nz * len(NEAR_SPLIT) + 1
+    kv_refs, query_refs = refs[:nq], refs[nq : nq + queries]
+    bias_ref, w_hbm, acc_ref, w_far_ref, w_ref, q_ref, att_ref, score_ref, sem = refs[nq + queries :]
+    heads = order_ref.shape[0] - 1
+    rest_slots = heads - FAR_SLOTS - NEAR_SLOTS
+    kept = order_ref[heads]
+    extra = jnp.clip((kept - FAR_SLOTS - NEAR_SLOTS + PAIR - 1) // PAIR, 0, rest_slots // PAIR)
+    pairs = NEAR_SLOTS // PAIR + extra
+
+    def near_copy(slot):
+        return pltpu.make_async_copy(
+            w_hbm.at[rows_of(order_ref[FAR_SLOTS + slot])], w_ref.at[rows_of(slot)], sem.at[slot]
+        )
+
+    def far_copy(slot):
+        return pltpu.make_async_copy(
+            w_hbm.at[rows_of(order_ref[slot])], w_far_ref.at[rows_of(slot)], sem.at[heads - FAR_SLOTS + slot]
+        )
+
+    pl.loop(0, pairs * PAIR)(lambda slot: near_copy(slot).start())
+    pl.loop(0, FAR_SLOTS)(lambda slot: far_copy(slot).start())
+    def place_rows(start, part_refs):
+        for slot in range(part_refs[0].shape[0]):
+            q_ref[start + slot] = jnp.concatenate([ref[slot] for ref in part_refs], axis=0)
+
+    start = 0
+    for index, slots in enumerate(NEAR_SPLIT):
+        place_rows(start, query_refs[index * nz : (index + 1) * nz])
+        start += slots
+    rest_refs = [query_refs[-1].at[part * rest_slots : (part + 1) * rest_slots] for part in range(nz)]
+    pl.when(extra > 0)(lambda: place_rows(start, rest_refs))
+
+    def score(pair, place):
+        slot = pair * PAIR + place
+        score_ref[place] = scores_of(q_ref[slot], FAR_SLOTS + slot, kv_refs, order_ref)
+
+    def project(pair):
+        rows = pl.ds(pl.multiple_of(pair * PAIR * HD, HD), PAIR * HD)
+        for at in range(0, acc_ref.shape[1], TILE):
+            acc_ref[:, at : at + TILE] += jnp.dot(
+                att_ref[...], w_ref[rows, at : at + TILE], preferred_element_type=jnp.float32
+            )
+
+    acc_ref[...] = jnp.zeros_like(acc_ref)
+    att_ref[...] = jnp.zeros_like(att_ref)
+    for place in range(PAIR):
+        score(0, place)
+        near_copy(place).wait()
+
+    def one_pair(pair):
+        later = jnp.minimum(pair + 1, pairs - 1)
+        project(jnp.maximum(pair - 1, 0))
+        for place in range(PAIR):
+            slot = pair * PAIR + place
+            att_ref[:, place * HD : (place + 1) * HD] = attended(
+                score_ref[place], bias_ref[...], FAR_SLOTS + slot, kv_refs, order_ref
+            )
+            score(later, place)
+
+        @pl.when(pair + 1 < pairs)
+        def _():
+            for place in range(PAIR):
+                near_copy((pair + 1) * PAIR + place).wait()
+
+    pl.loop(0, pairs)(one_pair)
+    project(pairs - 1)
+    pl.loop(0, FAR_SLOTS)(lambda slot: far_copy(slot).wait())
+
+
+def last_kernel(nz, *refs):
+    att_refs, (w_ref, acc_ref, out_ref, att_ref) = refs[:nz], refs[nz:]
+    for slot in range(FAR_SLOTS):
+        att_ref[:, slot * HD : (slot + 1) * HD] = jnp.concatenate([ref[slot] for ref in att_refs], axis=0)
+    rows = att_refs[0].shape[1]
+    z_at = lax.axis_index("kvring")
+    for at in range(0, acc_ref.shape[1], TILE):
+        mixed = acc_ref[:, at : at + TILE] + jnp.dot(
+            att_ref[...], w_ref[:, at : at + TILE], preferred_element_type=jnp.float32
+        )
+        mixed = mixed.astype(jnp.bfloat16)
+        for slot in range(nz):
+            place = pl.multiple_of((z_at ^ slot) * rows, rows)
+            out_ref[pl.ds(place, rows), at : at + TILE] = mixed[slot * rows : (slot + 1) * rows]
+
+
+def per_device_small_ring(queries, keys, values, doc_ids, head_mask, w_out):
+    rows = queries.shape[0]
+    nq = lax.axis_size("qring")
+    nz = lax.axis_size("kvring")
+    heads = head_mask.shape[0]
+    width = w_out.shape[1]
+    quarter = rows * nz
+    total = quarter * nq
+    rest_slots = heads - FAR_SLOTS - NEAR_SLOTS
+    smem = pl.BlockSpec(memory_space=pltpu.SMEM)
+    vmem = pl.BlockSpec(memory_space=pltpu.VMEM)
+    hbm = pl.BlockSpec(memory_space=pl.ANY)
+    params = pltpu.CompilerParams(vmem_limit_bytes=VMEM_LIMIT)
+
+    def cost(micros):
+        return pl.CostEstimate(flops=int(micros * 1e9), bytes_accessed=0, transcendentals=0)
+
+    def slots_in_vmem(slots):
+        return pltpu.VMEM((slots, rows, HD), jnp.bfloat16)
+
+    kv_own = pl.pallas_call(
+        join_kernel,
+        out_shape=pltpu.VMEM((rows, 2 * keys.shape[1]), jnp.bfloat16),
+        in_specs=[vmem, vmem],
+        out_specs=vmem,
+        name="join",
+    )(keys, values)
+    kv_parts = [kv_own, *swaps_along(kv_own, "kvring")]
+    order, far, *near, rest, bias = pl.pallas_call(
+        functools.partial(prep_kernel, rows, nq, nz),
+        out_shape=(
+            jax.ShapeDtypeStruct((heads + 1,), jnp.int32),
+            *(slots_in_vmem(slots) for slots in (FAR_SLOTS, *NEAR_SPLIT, rest_slots)),
+            pltpu.VMEM((quarter, total), jnp.float32),
+        ),
+        in_specs=[smem, vmem, vmem],
+        out_specs=[smem] + [vmem] * (len(NEAR_SPLIT) + 3),
+        cost_estimate=cost(4),
+        name="prep",
+    )(head_mask, doc_ids, queries)
+    many = jnp.sum(head_mask) > NEAR_SLOTS + FAR_SLOTS
+    *kv_parts, near[0], near[1], order, many = lax.optimization_barrier((*kv_parts, *near, order, many))
+    kv0 = jnp.concatenate(kv_parts, axis=0)
+    kv2 = swap_along(kv0, "qring", 2)
+    near_parts = [[array, *swaps_along(array, "kvring")] for array in near]
+    rest_all = lax.cond(
+        many,
+        lambda array: jnp.concatenate([array, *swaps_along(array, "kvring")]),
+        lambda array: jnp.zeros((nz * rest_slots, rows, HD), array.dtype),
+        lax.optimization_barrier((rest, kv0))[0],
+    )
+    kv0, rest_all, *near_parts[0] = lax.optimization_barrier((kv0, rest_all, *near_parts[0]))
+    kv1 = swap_along(kv0, "qring", 1)
+    kv3 = swap_along(kv2, "qring", 1)
+    kv = (kv0, kv1, kv2, kv3)
+    far_own = pl.pallas_call(
+        functools.partial(own_kernel, nq),
+        out_shape=slots_in_vmem(FAR_SLOTS),
+        in_specs=[smem] + [vmem] * (nq + 2),
+        out_specs=vmem,
+        compiler_params=params,
+        cost_estimate=cost(2),
+        name="own",
+    )(order, *in_vmem(*kv, far, bias))
+    far_parts = [far_own, *swaps_along(far_own, "kvring")]
+    acc, w_far = pl.pallas_call(
+        functools.partial(first_kernel, nq, nz),
+        out_shape=(
+            pltpu.VMEM((quarter, width), jnp.float32),
+            pltpu.VMEM((FAR_SLOTS * HD, width), jnp.bfloat16),
+        ),
+        in_specs=[smem] + [vmem] * (nq + nz * len(near) + 2) + [hbm],
+        out_specs=(vmem, vmem),
+        scratch_shapes=[
+            pltpu.VMEM(((heads - FAR_SLOTS) * HD, width), jnp.bfloat16),
+            pltpu.VMEM((heads - FAR_SLOTS, quarter, HD), jnp.bfloat16),
+            pltpu.VMEM((quarter, PAIR * HD), jnp.bfloat16),
+            pltpu.VMEM((PAIR, quarter, total), jnp.float32),
+            pltpu.SemaphoreType.DMA((heads,)),
+        ],
+        compiler_params=params,
+        cost_estimate=cost(6),
+        name="first",
+    )(order, *in_vmem(*kv, *sum(near_parts, []), rest_all, bias), w_out)
+    return pl.pallas_call(
+        functools.partial(last_kernel, nz),
+        out_shape=jax.ShapeDtypeStruct((quarter, width), jnp.bfloat16),
+        in_specs=[vmem] * (nz + 2),
+        out_specs=vmem,
+        scratch_shapes=[pltpu.VMEM((quarter, FAR_SLOTS * HD), jnp.bfloat16)],
+        compiler_params=params,
+        name="last",
+    )(*in_vmem(*far_parts, w_far, acc))
+
+
 def solution(mesh):
     placed = (
         P(("groups", "qring", "kvring"), "head"),
@@ -140,6 +433,7 @@
         P("head"),
         P("head", "kvring"),
     )
+    per_device = per_device_small_ring if small_ring(mesh) else per_device_any_ring
     return jax.shard_map(
         per_device,
         mesh=mesh,

time: 178 us -> 51.7 us (0.29)
  waiting for transfers between devices: 82.8 us -> 11.4 us
  blocking collectives: 40.4 us -> 0 us
  starting transfers between devices: 0.31 us -> 21 us
  matrix products: 18.4 us -> 0 us
  Pallas kernels: 0 us -> 17.1 us
  local copies, waits for them, and re-layouts: 16.9 us -> 0.73 us
  between operations: 13.3 us -> 0.68 us
  other arithmetic: 5.11 us -> 0.63 us
    unnamed x6 -> x0, waiting for transfers between devices: 45.5 us -> none
    all_gather x2 -> x0, waiting for transfers between devices: 37.3 us -> none  [the longest x1 37.3 us: per_device(): lax.all_gather(attended, 'kvring', axis=0, tiled=True)]
    all_gather x2 -> x0, blocking collectives: 30.1 us -> none  [the longest x1 15.5 us: per_device(): lax.all_gather(key_rows, 'kvring', axis=0, tiled=True)]
    ppermute x0 -> x15, starting transfers between devices: none -> 21 us  [swap_along(): lax.ppermute(array, axis_name, [(i, i ^ partner) for i in range(size)])]
    dot_general x3 -> x0, matrix products: 18.4 us -> none  [the longest x1 10.6 us: per_device(): jnp.dot(lax.all_gather(attended, 'kvring', axis=0, tiled=True), w_out, pr...]
    pallas_call x0 -> x5, Pallas kernels: none -> 17.1 us  [the longest x1 9.2 us: per_device_small_ring(): pl.pallas_call(functools.partial(first_kernel, nq, nz), out_shape=(pltpu....]
    ppermute x0 -> x15, waiting for transfers between devices: none -> 11.4 us  [swap_along(): lax.ppermute(array, axis_name, [(i, i ^ partner) for i in range(size)])]
    pmax x1 -> x0, blocking collectives: 10.3 us -> none  [per_device(): top = lax.pmax(run_max, 'qring')]
  transfers between devices with their start and end apart: 4 -> 15, of which waited for: 3 -> 4; matrix products, arithmetic and copies ran while one was open for 6% -> 1% of each run, Pallas kernels for 0% -> 27%
where the time goes in v2:
time: 51.7 us; the launch traced here: 51.5 us
  starting transfers between devices  21 us (41%)
  Pallas kernels  17.1 us (33%)
  waiting for transfers between devices  11.4 us (22%)
  local copies, waits for them, and re-layouts  0.73 us (1%)
  between operations  0.68 us (1%)
  other arithmetic  0.63 us (1%)
    ppermute x15, starting transfers between devices, swap_along(): lax.ppermute(array, axis_name, [(i, i ^ partner) for i in range(size)])  21 us
    ppermute x15, waiting for transfers between devices, swap_along(): lax.ppermute(array, axis_name, [(i, i ^ partner) for i in range(size)])  11.4 us
    pallas_call x1, Pallas kernels, per_device_small_ring(): pl.pallas_call(functools.partial(first_kernel, nq, nz), out_shape=(pltpu....  9.2 us
    pallas_call x1, Pallas kernels, per_device_small_ring(): pl.pallas_call(functools.partial(own_kernel, nq), out_shape=slots_in_vmem...  2.75 us
    pallas_call x1, Pallas kernels, per_device_small_ring(): pl.pallas_call(functools.partial(last_kernel, nz), out_shape=jax.ShapeDty...  2.35 us
    pallas_call x1, Pallas kernels, per_device_small_ring(): pl.pallas_call(functools.partial(prep_kernel, rows, nq, nz), out_shape=(j...  1.96 us
  transfers between devices with their start and end apart: 15, of which 4 were waited for; matrix products, arithmetic and copies ran while one was open for 1% of the time, Pallas kernels for 27%

profile of v2, /device:TPU:0, one launch (start us, length us, event | category | flops | bytes accessed | tf_op | source)
XLA Modules:
  0.0 51.5 jit_solution(8225023450914728136)
XLA Ops:
  0.0 0.8 %join.1 = bf16[48,1024]{1,0:T(8,128)(2,1)S(1)} custom-call(bf16[48,512]{1,0:T(8,128)(2,1)} %k_ref.1, bf16[48,512]{1,0:T(8,128)(2,1)} %v_ref.1), custom_call_target="tpu_custom_call" | custom-call | tf_op jit(solution)/shard_map/join/pallas_call | solution.py:352
  0.8 3.1 %collective-permute-start.3 = (bf16[48,1024]{1,0:T(8,128)(2,1)S(1)}, bf16[48,1024]{1,0:T(8,128)(2,1)S(1)}, u32[]{:S(2)}, u32[]{:S(2)}) collective-permute-start(bf16[48,1024]{1,0:T(8,128)(2,1)S(1)} %join.1), channel_id=1, source_target_pairs={{0,1},{1,0},{2,3},{3,2},{4,5},{5,4},{6,7},{7,6},{8,9},{9,8},{10,11... | collective-permute-start | bytes 294920 | tf_op jit(solution)/shard_map/ppermute | solution.py:152
  3.9 2.6 %collective-permute-start.4 = (bf16[48,1024]{1,0:T(8,128)(2,1)S(1)}, bf16[48,1024]{1,0:T(8,128)(2,1)S(1)}, u32[]{:S(2)}, u32[]{:S(2)}) collective-permute-start(bf16[48,1024]{1,0:T(8,128)(2,1)S(1)} %join.1), channel_id=1, source_target_pairs={{0,2},{1,3},{2,0},{3,1},{4,6},{5,7},{6,4},{7,5},{8,10},{9,11},{10,... | collective-permute-start | bytes 294920 | tf_op jit(solution)/shard_map/ppermute | solution.py:152
  6.5 2.0 %prep.1 = (s32[33]{0:T(128)}, bf16[12,48,128]{2,1,0:T(8,128)(2,1)S(1)}, bf16[8,48,128]{2,1,0:T(8,128)(2,1)S(1)}, bf16[6,48,128]{2,1,0:T(8,128)(2,1)S(1)}, bf16[6...) custom-call(s32[32]{0:T(128)} %mask_ref.1, s32[768]{0:T(1024)} %doc_ref.1, bf16[48,4096]{1,0:T(8,128)(2,1)} %q_ref.1), custom_call_target="tpu_custom_call" | custom-call | flops 4000000000 | tf_op jit(solution)/shard_map/prep/pallas_call | solution.py:360
  8.5 0.6 %reduce_sum.9 = s32[]{:T(128)} reduce(s32[32]{0:T(128)S(1)} %copy-done.1, s32[]{:T(128)} %constant.1.clone.1), dimensions={0}, to_apply=%region_0.0 | reduce | flops 31 | bytes 136 | tf_op jit(solution)/shard_map/reduce_sum | solution.py:372
  9.7 4.6 %collective-permute-done.4 = bf16[48,1024]{1,0:T(8,128)(2,1)S(1)} collective-permute-done((bf16[48,1024]{1,0:T(8,128)(2,1)S(1)}, bf16[48,1024]{1,0:T(8,128)(2,1)S(1)}, u32[]{:S(2)}, u32[]{:S(2)}) %collective-permute-start.4) | collective-permute-done | bytes 98336 | tf_op jit(solution)/shard_map/ppermute | solution.py:152
  14.4 1.6 %collective-permute-start.10 = (bf16[192,1024]{1,0:T(8,128)(2,1)S(1)}, bf16[192,1024]{1,0:T(8,128)(2,1)S(1)}, u32[]{:S(2)}, u32[]{:S(2)}) collective-permute-start(bf16[192,1024]{1,0:T(8,128)(2,1)S(1)} %constant_dynamic-update-slice_fusion.refs_0_), channel_id=1, source_target_pairs={{0,8},{4,12},{8,0},{12,4},{1,9},{5,13},{9,1},{13,5},{2,10},{6,14},... | collective-permute-start | bytes 1179656 | tf_op jit(solution)/shard_map/ppermute | solution.py:152
  16.0 1.6 %collective-permute-start.6 = (bf16[8,48,128]{2,1,0:T(8,128)(2,1)S(1)}, bf16[8,48,128]{2,1,0:T(8,128)(2,1)S(1)}, u32[]{:S(2)}, u32[]{:S(2)}) collective-permute-start(bf16[8,48,128]{2,1,0:T(8,128)(2,1)S(1)} %get-tuple-element.47.refs_4_), channel_id=1, source_target_pairs={{0,1},{1,0},{2,3},{3,2},{4,5},{5,4},{6,7},{7,6},{8,9},{9,8},{10,11... | collective-permute-start | bytes 294920 | tf_op jit(solution)/shard_map/ppermute | solution.py:152
  17.6 1.5 %collective-permute-start.7 = (bf16[8,48,128]{2,1,0:T(8,128)(2,1)S(1)}, bf16[8,48,128]{2,1,0:T(8,128)(2,1)S(1)}, u32[]{:S(2)}, u32[]{:S(2)}) collective-permute-start(bf16[8,48,128]{2,1,0:T(8,128)(2,1)S(1)} %get-tuple-element.47.refs_4_), channel_id=1, source_target_pairs={{0,2},{1,3},{2,0},{3,1},{4,6},{5,7},{6,4},{7,5},{8,10},{9,11},{10,... | collective-permute-start | bytes 294920 | tf_op jit(solution)/shard_map/ppermute | solution.py:152
  19.1 1.3 %collective-permute-start.8 = (bf16[8,48,128]{2,1,0:T(8,128)(2,1)S(1)}, bf16[8,48,128]{2,1,0:T(8,128)(2,1)S(1)}, u32[]{:S(2)}, u32[]{:S(2)}) collective-permute-start(bf16[8,48,128]{2,1,0:T(8,128)(2,1)S(1)} %get-tuple-element.47.refs_4_), channel_id=1, source_target_pairs={{0,3},{1,2},{2,1},{3,0},{4,7},{5,6},{6,5},{7,4},{8,11},{9,10},{10,... | collective-permute-start | bytes 294920 | tf_op jit(solution)/shard_map/ppermute | solution.py:152
  20.5 0.7 %collective-permute-done.6.refs_5_ = bf16[8,48,128]{2,1,0:T(8,128)(2,1)S(1)} collective-permute-done((bf16[8,48,128]{2,1,0:T(8,128)(2,1)S(1)}, bf16[8,48,128]{2,1,0:T(8,128)(2,1)S(1)}, u32[]{:S(2)}, u32[]{:S(2)}) %collective-permute-start.6) | collective-permute-done | bytes 98336 | tf_op jit(solution)/shard_map/ppermute | solution.py:152
  21.2 5.5 %collective-permute-done.7.refs_6_ = bf16[8,48,128]{2,1,0:T(8,128)(2,1)S(1)} collective-permute-done((bf16[8,48,128]{2,1,0:T(8,128)(2,1)S(1)}, bf16[8,48,128]{2,1,0:T(8,128)(2,1)S(1)}, u32[]{:S(2)}, u32[]{:S(2)}) %collective-permute-start.7) | collective-permute-done | bytes 98336 | tf_op jit(solution)/shard_map/ppermute | solution.py:152
  26.7 0.5 collective-permute-start.11
  27.2 1.6 %collective-permute-start.15 = (bf16[6,48,128]{2,1,0:T(8,128)(2,1)S(1)}, bf16[6,48,128]{2,1,0:T(8,128)(2,1)S(1)}, u32[]{:S(2)}, u32[]{:S(2)}) collective-permute-start(bf16[6,48,128]{2,1,0:T(8,128)(2,1)S(1)} %get-tuple-element.51.refs_8_), channel_id=1, source_target_pairs={{0,1},{1,0},{2,3},{3,2},{4,5},{5,4},{6,7},{7,6},{8,9},{9,8},{10,11... | collective-permute-start | bytes 221192 | tf_op jit(solution)/shard_map/ppermute | solution.py:152
  28.8 1.2 %collective-permute-start.16 = (bf16[6,48,128]{2,1,0:T(8,128)(2,1)S(1)}, bf16[6,48,128]{2,1,0:T(8,128)(2,1)S(1)}, u32[]{:S(2)}, u32[]{:S(2)}) collective-permute-start(bf16[6,48,128]{2,1,0:T(8,128)(2,1)S(1)} %get-tuple-element.51.refs_8_), channel_id=1, source_target_pairs={{0,2},{1,3},{2,0},{3,1},{4,6},{5,7},{6,4},{7,5},{8,10},{9,11},{10,... | collective-permute-start | bytes 221192 | tf_op jit(solution)/shard_map/ppermute | solution.py:152
  30.0 1.6 %collective-permute-start.17 = (bf16[6,48,128]{2,1,0:T(8,128)(2,1)S(1)}, bf16[6,48,128]{2,1,0:T(8,128)(2,1)S(1)}, u32[]{:S(2)}, u32[]{:S(2)}) collective-permute-start(bf16[6,48,128]{2,1,0:T(8,128)(2,1)S(1)} %get-tuple-element.51.refs_8_), channel_id=1, source_target_pairs={{0,3},{1,2},{2,1},{3,0},{4,7},{5,6},{6,5},{7,4},{8,11},{9,10},{10,... | collective-permute-start | bytes 221192 | tf_op jit(solution)/shard_map/ppermute | solution.py:152
  31.6 0.7 %copy-done = s32[33]{0:T(128)S(1)} copy-done((s32[33]{0:T(128)S(1)}, s32[33]{0:T(128)}, u32[]{:S(2)}) %copy-start) | copy-done | bytes 156
  32.2 2.7 %own.1.refs_0_ = bf16[12,48,128]{2,1,0:T(8,128)(2,1)S(1)} custom-call(s32[33]{0:T(128)S(1)} %copy-done, bf16[192,1024]{1,0:T(8,128)(2,1)S(1)} %constant_dynamic-update-slice_fusion.refs_0_, bf16[192,1024]{1,0:T(8,128)(2,1)S(1)} %collective-permute-done.9.refs_1_, bf16[192,1024]{1,0:T(8,128)(2,1)S(1)} %collective-permute-done.10.refs_2_, ...), custom_call_target="tpu_custom_call" | custom-call | flops 2000000000 | tf_op jit(solution)/shard_map/own/pallas_call | solution.py:387
  35.0 0.8 %collective-permute-start.12 = (bf16[12,48,128]{2,1,0:T(8,128)(2,1)S(1)}, bf16[12,48,128]{2,1,0:T(8,128)(2,1)S(1)}, u32[]{:S(2)}, u32[]{:S(2)}) collective-permute-start(bf16[12,48,128]{2,1,0:T(8,128)(2,1)S(1)} %own.1.refs_0_), channel_id=1, source_target_pairs={{0,1},{1,0},{2,3},{3,2},{4,5},{5,4},{6,7},{7,6},{8,9},{9,8},{10,11... | collective-permute-start | bytes 442376 | tf_op jit(solution)/shard_map/ppermute | solution.py:152
  35.8 2.1 %collective-permute-start.13 = (bf16[12,48,128]{2,1,0:T(8,128)(2,1)S(1)}, bf16[12,48,128]{2,1,0:T(8,128)(2,1)S(1)}, u32[]{:S(2)}, u32[]{:S(2)}) collective-permute-start(bf16[12,48,128]{2,1,0:T(8,128)(2,1)S(1)} %own.1.refs_0_), channel_id=1, source_target_pairs={{0,2},{1,3},{2,0},{3,1},{4,6},{5,7},{6,4},{7,5},{8,10},{9,11},{10,... | collective-permute-start | bytes 442376 | tf_op jit(solution)/shard_map/ppermute | solution.py:152
  37.9 1.6 %collective-permute-start.14 = (bf16[12,48,128]{2,1,0:T(8,128)(2,1)S(1)}, bf16[12,48,128]{2,1,0:T(8,128)(2,1)S(1)}, u32[]{:S(2)}, u32[]{:S(2)}) collective-permute-start(bf16[12,48,128]{2,1,0:T(8,128)(2,1)S(1)} %own.1.refs_0_), channel_id=1, source_target_pairs={{0,3},{1,2},{2,1},{3,0},{4,7},{5,6},{6,5},{7,4},{8,11},{9,10},{10,... | collective-permute-start | bytes 442376 | tf_op jit(solution)/shard_map/ppermute | solution.py:152
  39.5 9.2 %first.1 = (f32[192,2048]{1,0:T(8,128)S(1)}, bf16[1536,2048]{1,0:T(8,128)(2,1)S(1)}) custom-call(s32[33]{0:T(128)S(1)} %copy-done, bf16[192,1024]{1,0:T(8,128)(2,1)S(1)} %constant_dynamic-update-slice_fusion.refs_0_, bf16[192,1024]{1,0:T(8,128)(2,1)S(1)} %collective-permute-done.9.refs_1_, bf16[192,1024]{1,0:T(8,128)(2,1)S(1)} %collective-permute-done.10.refs_2_, ...), custom_call_target="tpu_custom_call" | custom-call | flops 6000000000 | tf_op jit(solution)/shard_map/first/pallas_call | solution.py:397
  48.7 0.5 collective-permute-done.13.refs_2_
  49.2 2.3 %last.1 = bf16[192,2048]{1,0:T(8,128)(2,1)} custom-call(bf16[12,48,128]{2,1,0:T(8,128)(2,1)S(1)} %own.1.refs_0_, bf16[12,48,128]{2,1,0:T(8,128)(2,1)S(1)} %collective-permute-done.12.refs_1_, bf16[12,48,128]{2,1,0:T(8,128)(2,1)S(1)} %collective-permute-done.13.refs_2_, bf16[12,48,128]{2,1,0:T(8,128)(2,1)S(1)} %collective-permute-done.14.refs_3_, ...), custom_call_target="tpu_custom_call" | custom-call | tf_op jit(solution)/shard_map/last/pallas_call | solution.py:416
  (22 shorter events, 0.2 us)
Async XLA Ops:
  0.8 7.7 %copy-start.1 = (s32[32]{0:T(128)S(1)}, s32[32]{0:T(128)}, u32[]{:S(2)}) copy-start(s32[32]{0:T(128)} %mask_ref.1) | copy-start | bytes 388
  0.8 8.9 %collective-permute-start.3 = (bf16[48,1024]{1,0:T(8,128)(2,1)S(1)}, bf16[48,1024]{1,0:T(8,128)(2,1)S(1)}, u32[]{:S(2)}, u32[]{:S(2)}) collective-permute-start(bf16[48,1024]{1,0:T(8,128)(2,1)S(1)} %join.1), channel_id=1, source_target_pairs={{0,1},{1,0},{2,3},{3,2},{4,5},{5,4},{6,7},{7,6},{8,9},{9,8},{10,11... | collective-permute-start | bytes 294920 | tf_op jit(solution)/shard_map/ppermute | solution.py:152
  3.9 10.4 %collective-permute-start.4 = (bf16[48,1024]{1,0:T(8,128)(2,1)S(1)}, bf16[48,1024]{1,0:T(8,128)(2,1)S(1)}, u32[]{:S(2)}, u32[]{:S(2)}) collective-permute-start(bf16[48,1024]{1,0:T(8,128)(2,1)S(1)} %join.1), channel_id=1, source_target_pairs={{0,2},{1,3},{2,0},{3,1},{4,6},{5,7},{6,4},{7,5},{8,10},{9,11},{10,... | collective-permute-start | bytes 294920 | tf_op jit(solution)/shard_map/ppermute | solution.py:152
  6.5 7.8 %collective-permute-start.5 = (bf16[48,1024]{1,0:T(8,128)(2,1)S(1)}, bf16[48,1024]{1,0:T(8,128)(2,1)S(1)}, u32[]{:S(2)}, u32[]{:S(2)}) collective-permute-start(bf16[48,1024]{1,0:T(8,128)(2,1)S(1)} %join.1), channel_id=1, source_target_pairs={{0,3},{1,2},{2,1},{3,0},{4,7},{5,6},{6,5},{7,4},{8,11},{9,10},{10,... | collective-permute-start | bytes 294920 | tf_op jit(solution)/shard_map/ppermute | solution.py:152
  14.4 12.3 %collective-permute-start.10 = (bf16[192,1024]{1,0:T(8,128)(2,1)S(1)}, bf16[192,1024]{1,0:T(8,128)(2,1)S(1)}, u32[]{:S(2)}, u32[]{:S(2)}) collective-permute-start(bf16[192,1024]{1,0:T(8,128)(2,1)S(1)} %constant_dynamic-update-slice_fusion.refs_0_), channel_id=1, source_target_pairs={{0,8},{4,12},{8,0},{12,4},{1,9},{5,13},{9,1},{13,5},{2,10},{6,14},... | collective-permute-start | bytes 1179656 | tf_op jit(solution)/shard_map/ppermute | solution.py:152
  16.0 5.2 %collective-permute-start.6 = (bf16[8,48,128]{2,1,0:T(8,128)(2,1)S(1)}, bf16[8,48,128]{2,1,0:T(8,128)(2,1)S(1)}, u32[]{:S(2)}, u32[]{:S(2)}) collective-permute-start(bf16[8,48,128]{2,1,0:T(8,128)(2,1)S(1)} %get-tuple-element.47.refs_4_), channel_id=1, source_target_pairs={{0,1},{1,0},{2,3},{3,2},{4,5},{5,4},{6,7},{7,6},{8,9},{9,8},{10,11... | collective-permute-start | bytes 294920 | tf_op jit(solution)/shard_map/ppermute | solution.py:152
  17.6 9.0 %collective-permute-start.7 = (bf16[8,48,128]{2,1,0:T(8,128)(2,1)S(1)}, bf16[8,48,128]{2,1,0:T(8,128)(2,1)S(1)}, u32[]{:S(2)}, u32[]{:S(2)}) collective-permute-start(bf16[8,48,128]{2,1,0:T(8,128)(2,1)S(1)} %get-tuple-element.47.refs_4_), channel_id=1, source_target_pairs={{0,2},{1,3},{2,0},{3,1},{4,6},{5,7},{6,4},{7,5},{8,10},{9,11},{10,... | collective-permute-start | bytes 294920 | tf_op jit(solution)/shard_map/ppermute | solution.py:152
  19.1 7.5 %collective-permute-start.8 = (bf16[8,48,128]{2,1,0:T(8,128)(2,1)S(1)}, bf16[8,48,128]{2,1,0:T(8,128)(2,1)S(1)}, u32[]{:S(2)}, u32[]{:S(2)}) collective-permute-start(bf16[8,48,128]{2,1,0:T(8,128)(2,1)S(1)} %get-tuple-element.47.refs_4_), channel_id=1, source_target_pairs={{0,3},{1,2},{2,1},{3,0},{4,7},{5,6},{6,5},{7,4},{8,11},{9,10},{10,... | collective-permute-start | bytes 294920 | tf_op jit(solution)/shard_map/ppermute | solution.py:152
  26.7 4.9 %collective-permute-start.9 = (bf16[192,1024]{1,0:T(8,128)(2,1)S(1)}, bf16[192,1024]{1,0:T(8,128)(2,1)S(1)}, u32[]{:S(2)}, u32[]{:S(2)}) collective-permute-start(bf16[192,1024]{1,0:T(8,128)(2,1)S(1)} %constant_dynamic-update-slice_fusion.refs_0_), channel_id=1, source_target_pairs={{0,4},{4,0},{8,12},{12,8},{1,5},{5,1},{9,13},{13,9},{2,6},{6,2},{1... | collective-permute-start | bytes 1179656 | tf_op jit(solution)/shard_map/ppermute | solution.py:152
  26.7 4.9 %collective-permute-start.11 = (bf16[192,1024]{1,0:T(8,128)(2,1)S(1)}, bf16[192,1024]{1,0:T(8,128)(2,1)S(1)}, u32[]{:S(2)}, u32[]{:S(2)}) collective-permute-start(bf16[192,1024]{1,0:T(8,128)(2,1)S(1)} %collective-permute-done.10.refs_2_), channel_id=1, source_target_pairs={{0,4},{4,0},{8,12},{12,8},{1,5},{5,1},{9,13},{13,9},{2,6},{6,2},{1... | collective-permute-start | bytes 1179656 | tf_op jit(solution)/shard_map/ppermute | solution.py:152
  27.2 10.7 %collective-permute-start.15 = (bf16[6,48,128]{2,1,0:T(8,128)(2,1)S(1)}, bf16[6,48,128]{2,1,0:T(8,128)(2,1)S(1)}, u32[]{:S(2)}, u32[]{:S(2)}) collective-permute-start(bf16[6,48,128]{2,1,0:T(8,128)(2,1)S(1)} %get-tuple-element.51.refs_8_), channel_id=1, source_target_pairs={{0,1},{1,0},{2,3},{3,2},{4,5},{5,4},{6,7},{7,6},{8,9},{9,8},{10,11... | collective-permute-start | bytes 221192 | tf_op jit(solution)/shard_map/ppermute | solution.py:152
  28.8 10.7 %collective-permute-start.16 = (bf16[6,48,128]{2,1,0:T(8,128)(2,1)S(1)}, bf16[6,48,128]{2,1,0:T(8,128)(2,1)S(1)}, u32[]{:S(2)}, u32[]{:S(2)}) collective-permute-start(bf16[6,48,128]{2,1,0:T(8,128)(2,1)S(1)} %get-tuple-element.51.refs_8_), channel_id=1, source_target_pairs={{0,2},{1,3},{2,0},{3,1},{4,6},{5,7},{6,4},{7,5},{8,10},{9,11},{10,... | collective-permute-start | bytes 221192 | tf_op jit(solution)/shard_map/ppermute | solution.py:152
  30.0 9.5 %collective-permute-start.17 = (bf16[6,48,128]{2,1,0:T(8,128)(2,1)S(1)}, bf16[6,48,128]{2,1,0:T(8,128)(2,1)S(1)}, u32[]{:S(2)}, u32[]{:S(2)}) collective-permute-start(bf16[6,48,128]{2,1,0:T(8,128)(2,1)S(1)} %get-tuple-element.51.refs_8_), channel_id=1, source_target_pairs={{0,3},{1,2},{2,1},{3,0},{4,7},{5,6},{6,5},{7,4},{8,11},{9,10},{10,... | collective-permute-start | bytes 221192 | tf_op jit(solution)/shard_map/ppermute | solution.py:152
  31.6 0.7 %copy-start = (s32[33]{0:T(128)S(1)}, s32[33]{0:T(128)}, u32[]{:S(2)}) copy-start(s32[33]{0:T(128)} %get-tuple-element.35.order_ref) | copy-start | bytes 400
  35.0 13.7 %collective-permute-start.12 = (bf16[12,48,128]{2,1,0:T(8,128)(2,1)S(1)}, bf16[12,48,128]{2,1,0:T(8,128)(2,1)S(1)}, u32[]{:S(2)}, u32[]{:S(2)}) collective-permute-start(bf16[12,48,128]{2,1,0:T(8,128)(2,1)S(1)} %own.1.refs_0_), channel_id=1, source_target_pairs={{0,1},{1,0},{2,3},{3,2},{4,5},{5,4},{6,7},{7,6},{8,9},{9,8},{10,11... | collective-permute-start | bytes 442376 | tf_op jit(solution)/shard_map/ppermute | solution.py:152
  35.8 13.4 %collective-permute-start.13 = (bf16[12,48,128]{2,1,0:T(8,128)(2,1)S(1)}, bf16[12,48,128]{2,1,0:T(8,128)(2,1)S(1)}, u32[]{:S(2)}, u32[]{:S(2)}) collective-permute-start(bf16[12,48,128]{2,1,0:T(8,128)(2,1)S(1)} %own.1.refs_0_), channel_id=1, source_target_pairs={{0,2},{1,3},{2,0},{3,1},{4,6},{5,7},{6,4},{7,5},{8,10},{9,11},{10,... | collective-permute-start | bytes 442376 | tf_op jit(solution)/shard_map/ppermute | solution.py:152
  37.9 11.3 %collective-permute-start.14 = (bf16[12,48,128]{2,1,0:T(8,128)(2,1)S(1)}, bf16[12,48,128]{2,1,0:T(8,128)(2,1)S(1)}, u32[]{:S(2)}, u32[]{:S(2)}) collective-permute-start(bf16[12,48,128]{2,1,0:T(8,128)(2,1)S(1)} %own.1.refs_0_), channel_id=1, source_target_pairs={{0,3},{1,2},{2,1},{3,0},{4,7},{5,6},{6,5},{7,4},{8,11},{9,10},{10,... | collective-permute-start | bytes 442376 | tf_op jit(solution)/shard_map/ppermute | solution.py:152

commit v3 on v2

--- a/solution.py
+++ b/solution.py
@@ -137,9 +137,9 @@
 VMEM_LIMIT = 32 * 1024 * 1024
 LOG2E = math.log2(math.e)
 PAIR = 2
-NEAR_SPLIT = (8, 6)
+NEAR_SPLIT = (8, 8)
 NEAR_SLOTS = sum(NEAR_SPLIT)
-FAR_SLOTS = 12
+FAR_SLOTS = 10
 TILE = 1024
 
 
@@ -152,8 +152,13 @@
     return lax.ppermute(array, axis_name, [(i, i ^ partner) for i in range(size)])
 
 
+def partner_of(slot, count):
+    return (count - slot) % count
+
+
 def swaps_along(array, axis_name):
-    return [swap_along(array, axis_name, partner) for partner in range(1, lax.axis_size(axis_name))]
+    size = lax.axis_size(axis_name)
+    return [swap_along(array, axis_name, partner_of(slot, size)) for slot in range(1, size)]
 
 
 def in_vmem(*arrays):
@@ -199,12 +204,12 @@
     doc = doc_ref[...].reshape(1, total)
     row = lax.broadcasted_iota(jnp.int32, (quarter, 1), 0)
     row_z = slot_of(row, rows, nz)
-    row_pos = q_at * quarter + (row_z ^ z_at) * rows + row - row_z * rows
+    row_pos = q_at * quarter + (partner_of(row_z, nz) ^ z_at) * rows + row - row_z * rows
     col = lax.broadcasted_iota(jnp.int32, (1, total), 1)
     col_q = slot_of(col, quarter, nq)
     rest = col - col_q * quarter
     col_z = slot_of(rest, rows, nz)
-    col_pos = (col_q ^ q_at) * quarter + (col_z ^ z_at) * rows + rest - col_z * rows
+    col_pos = (((col_q & 1) * 2 + (col_q >> 1)) ^ q_at) * quarter + (partner_of(col_z, nz) ^ z_at) * rows + rest - col_z * rows
     own_doc = jnp.sum(jnp.where(col == row_pos, doc, 0), axis=1, keepdims=True)
     first = jnp.sum((doc < own_doc).astype(jnp.int32), axis=1, keepdims=True)
     bias_ref[...] = jnp.where((col_pos >= first) & (col_pos <= row_pos), 0.0, NEG)
@@ -232,8 +237,8 @@
     return (sums[:, :HD] * (keep / sums[:, HD:])).astype(jnp.bfloat16)
 
 
-def own_kernel(nq, order_ref, *refs):
-    kv_refs, (q_ref, bias_ref, att_ref) = refs[:nq], refs[nq:]
+def own_kernel(kvs, order_ref, *refs):
+    kv_refs, (q_ref, bias_ref, att_ref) = refs[:kvs], refs[kvs:]
     rows = q_ref.shape[1]
 
     def one_slot(slot):
@@ -243,10 +248,10 @@
     pl.loop(0, FAR_SLOTS, unroll=FAR_SLOTS // 2)(one_slot)
 
 
-def first_kernel(nq, nz, order_ref, *refs):
+def first_kernel(kvs, nz, order_ref, *refs):
     queries = nz * len(NEAR_SPLIT) + 1
-    kv_refs, query_refs = refs[:nq], refs[nq : nq + queries]
-    bias_ref, w_hbm, acc_ref, w_far_ref, w_ref, q_ref, att_ref, score_ref, sem = refs[nq + queries :]
+    kv_refs, query_refs = refs[:kvs], refs[kvs : kvs + queries]
+    bias_ref, w_hbm, acc_ref, w_far_ref, w_ref, q_ref, att_ref, score_ref, sem = refs[kvs + queries :]
     heads = order_ref.shape[0] - 1
     rest_slots = heads - FAR_SLOTS - NEAR_SLOTS
     kept = order_ref[heads]
@@ -325,7 +330,7 @@
         )
         mixed = mixed.astype(jnp.bfloat16)
         for slot in range(nz):
-            place = pl.multiple_of((z_at ^ slot) * rows, rows)
+            place = pl.multiple_of((z_at ^ partner_of(slot, nz)) * rows, rows)
             out_ref[pl.ds(place, rows), at : at + TILE] = mixed[slot * rows : (slot + 1) * rows]
 
 
@@ -360,7 +365,7 @@
     order, far, *near, rest, bias = pl.pallas_call(
         functools.partial(prep_kernel, rows, nq, nz),
         out_shape=(
-            jax.ShapeDtypeStruct((heads + 1,), jnp.int32),
+            pltpu.SMEM((heads + 1,), jnp.int32),
             *(slots_in_vmem(slots) for slots in (FAR_SLOTS, *NEAR_SPLIT, rest_slots)),
             pltpu.VMEM((quarter, total), jnp.float32),
         ),
@@ -380,14 +385,13 @@
         lambda array: jnp.zeros((nz * rest_slots, rows, HD), array.dtype),
         lax.optimization_barrier((rest, kv0))[0],
     )
-    kv0, rest_all, *near_parts[0] = lax.optimization_barrier((kv0, rest_all, *near_parts[0]))
-    kv1 = swap_along(kv0, "qring", 1)
-    kv3 = swap_along(kv2, "qring", 1)
-    kv = (kv0, kv1, kv2, kv3)
+    *near_parts[0], kv2, rest_all = lax.optimization_barrier((*near_parts[0], kv2, rest_all))
+    kv02 = jnp.concatenate([kv0, kv2], axis=0)
+    kv = (kv02, swap_along(kv02, "qring", 1))
     far_own = pl.pallas_call(
-        functools.partial(own_kernel, nq),
+        functools.partial(own_kernel, len(kv)),
         out_shape=slots_in_vmem(FAR_SLOTS),
-        in_specs=[smem] + [vmem] * (nq + 2),
+        in_specs=[smem] + [vmem] * (len(kv) + 2),
         out_specs=vmem,
         compiler_params=params,
         cost_estimate=cost(2),
@@ -395,12 +399,12 @@
     )(order, *in_vmem(*kv, far, bias))
     far_parts = [far_own, *swaps_along(far_own, "kvring")]
     acc, w_far = pl.pallas_call(
-        functools.partial(first_kernel, nq, nz),
+        functools.partial(first_kernel, len(kv), nz),
         out_shape=(
             pltpu.VMEM((quarter, width), jnp.float32),
             pltpu.VMEM((FAR_SLOTS * HD, width), jnp.bfloat16),
         ),
-        in_specs=[smem] + [vmem] * (nq + nz * len(near) + 2) + [hbm],
+        in_specs=[smem] + [vmem] * (len(kv) + nz * len(near) + 2) + [hbm],
         out_specs=(vmem, vmem),
         scratch_shapes=[
             pltpu.VMEM(((heads - FAR_SLOTS) * HD, width), jnp.bfloat16),

time: 51.7 us -> 50.7 us (0.981)
  Pallas kernels: 17.1 us -> 15.3 us
  waiting for transfers between devices: 11.4 us -> 12.9 us
  local copies, waits for them, and re-layouts: 0.73 us -> 0.13 us
    ppermute x15 -> x14, waiting for transfers between devices: 11.4 us -> 12.9 us  [swap_along(): lax.ppermute(array, axis_name, [(i, i ^ partner) for i in range(size)])]
    pallas_call x3, Pallas kernels: 13.9 us -> 12.3 us  [the longest x1 8.95 us: per_device_small_ring(): pl.pallas_call(functools.partial(first_kernel, len(kv), nz), out_shape=(p...]
    unnamed x7 -> x5, local copies, waits for them, and re-layouts: 0.68 us -> 0.05 us
    ppermute x15 -> x14, starting transfers between devices: 21 us -> 20.7 us  [swap_along(): lax.ppermute(array, axis_name, [(i, i ^ partner) for i in range(size)])]
  transfers between devices with their start and end apart: 15 -> 14, of which waited for: 4 -> 6; matrix products, arithmetic and copies ran while one was open for 1% -> 1% of each run, Pallas kernels for 27% -> 24%
where the time goes in v3:
time: 50.7 us; the launch traced here: 50.5 us
  starting transfers between devices  20.7 us (41%)
  Pallas kernels  15.3 us (30%)
  waiting for transfers between devices  12.9 us (25%)
  between operations  0.77 us (2%)
  other arithmetic  0.63 us (1%)
    ppermute x14, starting transfers between devices, swap_along(): lax.ppermute(array, axis_name, [(i, i ^ partner) for i in range(size)])  20.7 us
    ppermute x14, waiting for transfers between devices, swap_along(): lax.ppermute(array, axis_name, [(i, i ^ partner) for i in range(size)])  12.9 us
    pallas_call x1, Pallas kernels, per_device_small_ring(): pl.pallas_call(functools.partial(first_kernel, len(kv), nz), out_shape=(p...  8.95 us
    pallas_call x1, Pallas kernels, per_device_small_ring(): pl.pallas_call(functools.partial(last_kernel, nz), out_shape=jax.ShapeDty...  2.1 us
    pallas_call x1, Pallas kernels, per_device_small_ring(): pl.pallas_call(functools.partial(own_kernel, len(kv)), out_shape=slots_in...  1.93 us
    pallas_call x1, Pallas kernels, per_device_small_ring(): pl.pallas_call(functools.partial(prep_kernel, rows, nq, nz), out_shape=(p...  1.47 us
  transfers between devices with their start and end apart: 14, of which 6 were waited for; matrix products, arithmetic and copies ran while one was open for 1% of the time, Pallas kernels for 24%

profile of v3, /device:TPU:0, one launch (start us, length us, event | category | flops | bytes accessed | tf_op | source)
XLA Modules:
  0.0 50.5 jit_solution(6649891581397595140)
XLA Ops:
  0.0 0.8 %join.1 = bf16[48,1024]{1,0:T(8,128)(2,1)S(1)} custom-call(bf16[48,512]{1,0:T(8,128)(2,1)} %k_ref.1, bf16[48,512]{1,0:T(8,128)(2,1)} %v_ref.1), custom_call_target="tpu_custom_call" | custom-call | tf_op jit(solution)/shard_map/join/pallas_call | solution.py:357
  0.8 5.1 %collective-permute-start.3 = (bf16[48,1024]{1,0:T(8,128)(2,1)S(1)}, bf16[48,1024]{1,0:T(8,128)(2,1)S(1)}, u32[]{:S(2)}, u32[]{:S(2)}) collective-permute-start(bf16[48,1024]{1,0:T(8,128)(2,1)S(1)} %join.1), channel_id=1, source_target_pairs={{0,3},{1,2},{2,1},{3,0},{4,7},{5,6},{6,5},{7,4},{8,11},{9,10},{10,... | collective-permute-start | bytes 294920 | tf_op jit(solution)/shard_map/ppermute | solution.py:152
  5.9 0.0 collective-permute-start.4
  6.0 0.6 %collective-permute-start.5 = (bf16[48,1024]{1,0:T(8,128)(2,1)S(1)}, bf16[48,1024]{1,0:T(8,128)(2,1)S(1)}, u32[]{:S(2)}, u32[]{:S(2)}) collective-permute-start(bf16[48,1024]{1,0:T(8,128)(2,1)S(1)} %join.1), channel_id=1, source_target_pairs={{0,1},{1,0},{2,3},{3,2},{4,5},{5,4},{6,7},{7,6},{8,9},{9,8},{10,11... | collective-permute-start | bytes 294920 | tf_op jit(solution)/shard_map/ppermute | solution.py:152
  6.6 1.5 %prep.1 = (s32[33]{0:T(128)S(4)}, bf16[10,48,128]{2,1,0:T(8,128)(2,1)S(1)}, bf16[8,48,128]{2,1,0:T(8,128)(2,1)S(1)}, bf16[8,48,128]{2,1,0:T(8,128)(2,1)S(1)}, bf...) custom-call(s32[32]{0:T(128)} %mask_ref.1, s32[768]{0:T(1024)} %doc_ref.1, bf16[48,4096]{1,0:T(8,128)(2,1)} %q_ref.1), custom_call_target="tpu_custom_call" | custom-call | flops 4000000000 | tf_op jit(solution)/shard_map/prep/pallas_call | solution.py:365
  8.1 0.6 %reduce_sum.9 = s32[]{:T(128)} reduce(s32[32]{0:T(128)S(1)} %copy-done, s32[]{:T(128)} %constant.1.clone.1), dimensions={0}, to_apply=%region_0.0 | reduce | flops 31 | bytes 136 | tf_op jit(solution)/shard_map/reduce_sum | solution.py:377
  9.4 0.3 collective-permute-done.3
  9.6 4.6 %collective-permute-done.4 = bf16[48,1024]{1,0:T(8,128)(2,1)S(1)} collective-permute-done((bf16[48,1024]{1,0:T(8,128)(2,1)S(1)}, bf16[48,1024]{1,0:T(8,128)(2,1)S(1)}, u32[]{:S(2)}, u32[]{:S(2)}) %collective-permute-start.4) | collective-permute-done | bytes 98336 | tf_op jit(solution)/shard_map/ppermute | solution.py:152
  14.3 1.6 %collective-permute-start.9 = (bf16[192,1024]{1,0:T(8,128)(2,1)S(1)}, bf16[192,1024]{1,0:T(8,128)(2,1)S(1)}, u32[]{:S(2)}, u32[]{:S(2)}) collective-permute-start(bf16[192,1024]{1,0:T(8,128)(2,1)S(1)} %get-tuple-element.55), channel_id=1, source_target_pairs={{0,8},{4,12},{8,0},{12,4},{1,9},{5,13},{9,1},{13,5},{2,10},{6,14},... | collective-permute-start | bytes 1179656 | tf_op jit(solution)/shard_map/ppermute | solution.py:152
  15.9 2.5 %collective-permute-start.6 = (bf16[8,48,128]{2,1,0:T(8,128)(2,1)S(1)}, bf16[8,48,128]{2,1,0:T(8,128)(2,1)S(1)}, u32[]{:S(2)}, u32[]{:S(2)}) collective-permute-start(bf16[8,48,128]{2,1,0:T(8,128)(2,1)S(1)} %get-tuple-element.47.refs_2_), channel_id=1, source_target_pairs={{0,3},{1,2},{2,1},{3,0},{4,7},{5,6},{6,5},{7,4},{8,11},{9,10},{10,... | collective-permute-start | bytes 294920 | tf_op jit(solution)/shard_map/ppermute | solution.py:152
  18.4 0.1 collective-permute-start.7
  18.5 1.9 %collective-permute-start.8 = (bf16[8,48,128]{2,1,0:T(8,128)(2,1)S(1)}, bf16[8,48,128]{2,1,0:T(8,128)(2,1)S(1)}, u32[]{:S(2)}, u32[]{:S(2)}) collective-permute-start(bf16[8,48,128]{2,1,0:T(8,128)(2,1)S(1)} %get-tuple-element.47.refs_2_), channel_id=1, source_target_pairs={{0,1},{1,0},{2,3},{3,2},{4,5},{5,4},{6,7},{7,6},{8,9},{9,8},{10,11... | collective-permute-start | bytes 294920 | tf_op jit(solution)/shard_map/ppermute | solution.py:152
  20.4 3.0 %collective-permute-done.6.refs_3_ = bf16[8,48,128]{2,1,0:T(8,128)(2,1)S(1)} collective-permute-done((bf16[8,48,128]{2,1,0:T(8,128)(2,1)S(1)}, bf16[8,48,128]{2,1,0:T(8,128)(2,1)S(1)}, u32[]{:S(2)}, u32[]{:S(2)}) %collective-permute-start.6) | collective-permute-done | bytes 98336 | tf_op jit(solution)/shard_map/ppermute | solution.py:152
  23.3 3.2 %collective-permute-done.7.refs_4_ = bf16[8,48,128]{2,1,0:T(8,128)(2,1)S(1)} collective-permute-done((bf16[8,48,128]{2,1,0:T(8,128)(2,1)S(1)}, bf16[8,48,128]{2,1,0:T(8,128)(2,1)S(1)}, u32[]{:S(2)}, u32[]{:S(2)}) %collective-permute-start.7) | collective-permute-done | bytes 98336 | tf_op jit(solution)/shard_map/ppermute | solution.py:152
  26.5 0.1 collective-permute-start.10
  26.6 1.8 %collective-permute-start.14 = (bf16[8,48,128]{2,1,0:T(8,128)(2,1)S(1)}, bf16[8,48,128]{2,1,0:T(8,128)(2,1)S(1)}, u32[]{:S(2)}, u32[]{:S(2)}) collective-permute-start(bf16[8,48,128]{2,1,0:T(8,128)(2,1)S(1)} %get-tuple-element.51.refs_6_), channel_id=1, source_target_pairs={{0,3},{1,2},{2,1},{3,0},{4,7},{5,6},{6,5},{7,4},{8,11},{9,10},{10,... | collective-permute-start | bytes 294920 | tf_op jit(solution)/shard_map/ppermute | solution.py:152
  28.5 2.6 %collective-permute-start.16 = (bf16[8,48,128]{2,1,0:T(8,128)(2,1)S(1)}, bf16[8,48,128]{2,1,0:T(8,128)(2,1)S(1)}, u32[]{:S(2)}, u32[]{:S(2)}) collective-permute-start(bf16[8,48,128]{2,1,0:T(8,128)(2,1)S(1)} %get-tuple-element.51.refs_6_), channel_id=1, source_target_pairs={{0,1},{1,0},{2,3},{3,2},{4,5},{5,4},{6,7},{7,6},{8,9},{9,8},{10,11... | collective-permute-start | bytes 294920 | tf_op jit(solution)/shard_map/ppermute | solution.py:152
  31.1 1.9 %own.1.refs_0_ = bf16[10,48,128]{2,1,0:T(8,128)(2,1)S(1)} custom-call(s32[33]{0:T(128)S(4)} %get-tuple-element.35.order_ref, bf16[384,1024]{1,0:T(8,128)(2,1)S(1)} %constant_dynamic-update-slice_fusion.4.refs_0_, bf16[384,1024]{1,0:T(8,128)(2,1)S(1)} %collective-permute-done.10.refs_1_, bf16[10,48,128]{2,1,0:T(8,128)(2,1)S(1)} %get-tuple-element.45.refs_2_, ...), custom_call_target="tpu_custom_call" | custom-call | flops 2000000000 | tf_op jit(solution)/shard_map/own/pallas_call | solution.py:391
  33.0 1.8 %collective-permute-start.11 = (bf16[10,48,128]{2,1,0:T(8,128)(2,1)S(1)}, bf16[10,48,128]{2,1,0:T(8,128)(2,1)S(1)}, u32[]{:S(2)}, u32[]{:S(2)}) collective-permute-start(bf16[10,48,128]{2,1,0:T(8,128)(2,1)S(1)} %own.1.refs_0_), channel_id=1, source_target_pairs={{0,3},{1,2},{2,1},{3,0},{4,7},{5,6},{6,5},{7,4},{8,11},{9,10},{10,... | collective-permute-start | bytes 368648 | tf_op jit(solution)/shard_map/ppermute | solution.py:152
  34.8 2.6 %collective-permute-start.13 = (bf16[10,48,128]{2,1,0:T(8,128)(2,1)S(1)}, bf16[10,48,128]{2,1,0:T(8,128)(2,1)S(1)}, u32[]{:S(2)}, u32[]{:S(2)}) collective-permute-start(bf16[10,48,128]{2,1,0:T(8,128)(2,1)S(1)} %own.1.refs_0_), channel_id=1, source_target_pairs={{0,1},{1,0},{2,3},{3,2},{4,5},{5,4},{6,7},{7,6},{8,9},{9,8},{10,11... | collective-permute-start | bytes 368648 | tf_op jit(solution)/shard_map/ppermute | solution.py:152
  37.5 0.9 %collective-permute-done.15.refs_8_ = bf16[8,48,128]{2,1,0:T(8,128)(2,1)S(1)} collective-permute-done((bf16[8,48,128]{2,1,0:T(8,128)(2,1)S(1)}, bf16[8,48,128]{2,1,0:T(8,128)(2,1)S(1)}, u32[]{:S(2)}, u32[]{:S(2)}) %collective-permute-start.15) | collective-permute-done | bytes 98336 | tf_op jit(solution)/shard_map/ppermute | solution.py:152
  38.4 8.9 %first.1 = (f32[192,2048]{1,0:T(8,128)S(1)}, bf16[1280,2048]{1,0:T(8,128)(2,1)S(1)}) custom-call(s32[33]{0:T(128)S(4)} %get-tuple-element.35.order_ref, bf16[384,1024]{1,0:T(8,128)(2,1)S(1)} %constant_dynamic-update-slice_fusion.4.refs_0_, bf16[384,1024]{1,0:T(8,128)(2,1)S(1)} %collective-permute-done.10.refs_1_, ...), custom_call_target="tpu_custom_call" | custom-call | flops 6000000000 | tf_op jit(solution)/shard_map/first/pallas_call | solution.py:401
  47.4 1.0 %collective-permute-done.12.refs_2_ = bf16[10,48,128]{2,1,0:T(8,128)(2,1)S(1)} collective-permute-done((bf16[10,48,128]{2,1,0:T(8,128)(2,1)S(1)}, bf16[10,48,128]{2,1,0:T(8,128)(2,1)S(1)}, u32[]{:S(2)}, u32[]{:S(2)}) %collective-permute-start.12) | collective-permute-done | bytes 122912 | tf_op jit(solution)/shard_map/ppermute | solution.py:152
  48.4 2.1 %last.1 = bf16[192,2048]{1,0:T(8,128)(2,1)} custom-call(bf16[10,48,128]{2,1,0:T(8,128)(2,1)S(1)} %own.1.refs_0_, bf16[10,48,128]{2,1,0:T(8,128)(2,1)S(1)} %collective-permute-done.11.refs_1_, bf16[10,48,128]{2,1,0:T(8,128)(2,1)S(1)} %collective-permute-done.12.refs_2_, bf16[10,48,128]{2,1,0:T(8,128)(2,1)S(1)} %collective-permute-done.13.refs_3_, ...), custom_call_target="tpu_custom_call" | custom-call | tf_op jit(solution)/shard_map/last/pallas_call | solution.py:420
  (19 shorter events, 0.2 us)
Async XLA Ops:
  0.8 7.2 %copy-start = (s32[32]{0:T(128)S(1)}, s32[32]{0:T(128)}, u32[]{:S(2)}) copy-start(s32[32]{0:T(128)} %mask_ref.1) | copy-start | bytes 388
  0.8 8.8 %collective-permute-start.3 = (bf16[48,1024]{1,0:T(8,128)(2,1)S(1)}, bf16[48,1024]{1,0:T(8,128)(2,1)S(1)}, u32[]{:S(2)}, u32[]{:S(2)}) collective-permute-start(bf16[48,1024]{1,0:T(8,128)(2,1)S(1)} %join.1), channel_id=1, source_target_pairs={{0,3},{1,2},{2,1},{3,0},{4,7},{5,6},{6,5},{7,4},{8,11},{9,10},{10,... | collective-permute-start | bytes 294920 | tf_op jit(solution)/shard_map/ppermute | solution.py:152
  5.9 8.3 %collective-permute-start.4 = (bf16[48,1024]{1,0:T(8,128)(2,1)S(1)}, bf16[48,1024]{1,0:T(8,128)(2,1)S(1)}, u32[]{:S(2)}, u32[]{:S(2)}) collective-permute-start(bf16[48,1024]{1,0:T(8,128)(2,1)S(1)} %join.1), channel_id=1, source_target_pairs={{0,2},{1,3},{2,0},{3,1},{4,6},{5,7},{6,4},{7,5},{8,10},{9,11},{10,... | collective-permute-start | bytes 294920 | tf_op jit(solution)/shard_map/ppermute | solution.py:152
  6.0 8.3 %collective-permute-start.5 = (bf16[48,1024]{1,0:T(8,128)(2,1)S(1)}, bf16[48,1024]{1,0:T(8,128)(2,1)S(1)}, u32[]{:S(2)}, u32[]{:S(2)}) collective-permute-start(bf16[48,1024]{1,0:T(8,128)(2,1)S(1)} %join.1), channel_id=1, source_target_pairs={{0,1},{1,0},{2,3},{3,2},{4,5},{5,4},{6,7},{7,6},{8,9},{9,8},{10,11... | collective-permute-start | bytes 294920 | tf_op jit(solution)/shard_map/ppermute | solution.py:152
  14.3 12.2 %collective-permute-start.9 = (bf16[192,1024]{1,0:T(8,128)(2,1)S(1)}, bf16[192,1024]{1,0:T(8,128)(2,1)S(1)}, u32[]{:S(2)}, u32[]{:S(2)}) collective-permute-start(bf16[192,1024]{1,0:T(8,128)(2,1)S(1)} %get-tuple-element.55), channel_id=1, source_target_pairs={{0,8},{4,12},{8,0},{12,4},{1,9},{5,13},{9,1},{13,5},{2,10},{6,14},... | collective-permute-start | bytes 1179656 | tf_op jit(solution)/shard_map/ppermute | solution.py:152
  15.9 7.5 %collective-permute-start.6 = (bf16[8,48,128]{2,1,0:T(8,128)(2,1)S(1)}, bf16[8,48,128]{2,1,0:T(8,128)(2,1)S(1)}, u32[]{:S(2)}, u32[]{:S(2)}) collective-permute-start(bf16[8,48,128]{2,1,0:T(8,128)(2,1)S(1)} %get-tuple-element.47.refs_2_), channel_id=1, source_target_pairs={{0,3},{1,2},{2,1},{3,0},{4,7},{5,6},{6,5},{7,4},{8,11},{9,10},{10,... | collective-permute-start | bytes 294920 | tf_op jit(solution)/shard_map/ppermute | solution.py:152
  18.4 8.1 %collective-permute-start.7 = (bf16[8,48,128]{2,1,0:T(8,128)(2,1)S(1)}, bf16[8,48,128]{2,1,0:T(8,128)(2,1)S(1)}, u32[]{:S(2)}, u32[]{:S(2)}) collective-permute-start(bf16[8,48,128]{2,1,0:T(8,128)(2,1)S(1)} %get-tuple-element.47.refs_2_), channel_id=1, source_target_pairs={{0,2},{1,3},{2,0},{3,1},{4,6},{5,7},{6,4},{7,5},{8,10},{9,11},{10,... | collective-permute-start | bytes 294920 | tf_op jit(solution)/shard_map/ppermute | solution.py:152
  18.5 8.0 %collective-permute-start.8 = (bf16[8,48,128]{2,1,0:T(8,128)(2,1)S(1)}, bf16[8,48,128]{2,1,0:T(8,128)(2,1)S(1)}, u32[]{:S(2)}, u32[]{:S(2)}) collective-permute-start(bf16[8,48,128]{2,1,0:T(8,128)(2,1)S(1)} %get-tuple-element.47.refs_2_), channel_id=1, source_target_pairs={{0,1},{1,0},{2,3},{3,2},{4,5},{5,4},{6,7},{7,6},{8,9},{9,8},{10,11... | collective-permute-start | bytes 294920 | tf_op jit(solution)/shard_map/ppermute | solution.py:152
  26.5 4.5 %collective-permute-start.10 = (bf16[384,1024]{1,0:T(8,128)(2,1)S(1)}, bf16[384,1024]{1,0:T(8,128)(2,1)S(1)}, u32[]{:S(2)}, u32[]{:S(2)}) collective-permute-start(bf16[384,1024]{1,0:T(8,128)(2,1)S(1)} %constant_dynamic-update-slice_fusion.4.refs_0_), channel_id=1, source_target_pairs={{0,4},{4,0},{8,12},{12,8},{1,5},{5,1},{9,13},{13,9},{2,6},{6,2},{1... | collective-permute-start | bytes 2359304 | tf_op jit(solution)/shard_map/ppermute | solution.py:152
  26.6 8.2 %collective-permute-start.14 = (bf16[8,48,128]{2,1,0:T(8,128)(2,1)S(1)}, bf16[8,48,128]{2,1,0:T(8,128)(2,1)S(1)}, u32[]{:S(2)}, u32[]{:S(2)}) collective-permute-start(bf16[8,48,128]{2,1,0:T(8,128)(2,1)S(1)} %get-tuple-element.51.refs_6_), channel_id=1, source_target_pairs={{0,3},{1,2},{2,1},{3,0},{4,7},{5,6},{6,5},{7,4},{8,11},{9,10},{10,... | collective-permute-start | bytes 294920 | tf_op jit(solution)/shard_map/ppermute | solution.py:152
  28.4 9.9 %collective-permute-start.15 = (bf16[8,48,128]{2,1,0:T(8,128)(2,1)S(1)}, bf16[8,48,128]{2,1,0:T(8,128)(2,1)S(1)}, u32[]{:S(2)}, u32[]{:S(2)}) collective-permute-start(bf16[8,48,128]{2,1,0:T(8,128)(2,1)S(1)} %get-tuple-element.51.refs_6_), channel_id=1, source_target_pairs={{0,2},{1,3},{2,0},{3,1},{4,6},{5,7},{6,4},{7,5},{8,10},{9,11},{10,... | collective-permute-start | bytes 294920 | tf_op jit(solution)/shard_map/ppermute | solution.py:152
  28.5 9.9 %collective-permute-start.16 = (bf16[8,48,128]{2,1,0:T(8,128)(2,1)S(1)}, bf16[8,48,128]{2,1,0:T(8,128)(2,1)S(1)}, u32[]{:S(2)}, u32[]{:S(2)}) collective-permute-start(bf16[8,48,128]{2,1,0:T(8,128)(2,1)S(1)} %get-tuple-element.51.refs_6_), channel_id=1, source_target_pairs={{0,1},{1,0},{2,3},{3,2},{4,5},{5,4},{6,7},{7,6},{8,9},{9,8},{10,11... | collective-permute-start | bytes 294920 | tf_op jit(solution)/shard_map/ppermute | solution.py:152
  33.0 14.4 %collective-permute-start.11 = (bf16[10,48,128]{2,1,0:T(8,128)(2,1)S(1)}, bf16[10,48,128]{2,1,0:T(8,128)(2,1)S(1)}, u32[]{:S(2)}, u32[]{:S(2)}) collective-permute-start(bf16[10,48,128]{2,1,0:T(8,128)(2,1)S(1)} %own.1.refs_0_), channel_id=1, source_target_pairs={{0,3},{1,2},{2,1},{3,0},{4,7},{5,6},{6,5},{7,4},{8,11},{9,10},{10,... | collective-permute-start | bytes 368648 | tf_op jit(solution)/shard_map/ppermute | solution.py:152
  34.8 13.5 %collective-permute-start.12 = (bf16[10,48,128]{2,1,0:T(8,128)(2,1)S(1)}, bf16[10,48,128]{2,1,0:T(8,128)(2,1)S(1)}, u32[]{:S(2)}, u32[]{:S(2)}) collective-permute-start(bf16[10,48,128]{2,1,0:T(8,128)(2,1)S(1)} %own.1.refs_0_), channel_id=1, source_target_pairs={{0,2},{1,3},{2,0},{3,1},{4,6},{5,7},{6,4},{7,5},{8,10},{9,11},{10,... | collective-permute-start | bytes 368648 | tf_op jit(solution)/shard_map/ppermute | solution.py:152
  34.8 13.5 %collective-permute-start.13 = (bf16[10,48,128]{2,1,0:T(8,128)(2,1)S(1)}, bf16[10,48,128]{2,1,0:T(8,128)(2,1)S(1)}, u32[]{:S(2)}, u32[]{:S(2)}) collective-permute-start(bf16[10,48,128]{2,1,0:T(8,128)(2,1)S(1)} %own.1.refs_0_), channel_id=1, source_target_pairs={{0,1},{1,0},{2,3},{3,2},{4,5},{5,4},{6,7},{7,6},{8,9},{9,8},{10,11... | collective-permute-start | bytes 368648 | tf_op jit(solution)/shard_map/ppermute | solution.py:152

commit v4 on v3

--- a/solution.py
+++ b/solution.py
@@ -137,9 +137,9 @@
 VMEM_LIMIT = 32 * 1024 * 1024
 LOG2E = math.log2(math.e)
 PAIR = 2
-NEAR_SPLIT = (8, 8)
-NEAR_SLOTS = sum(NEAR_SPLIT)
-FAR_SLOTS = 10
+NEAR_SLOTS = 14
+EARLY = (1,)
+FAR_SLOTS = 12
 TILE = 1024
 
 
@@ -249,7 +249,7 @@
 
 
 def first_kernel(kvs, nz, order_ref, *refs):
-    queries = nz * len(NEAR_SPLIT) + 1
+    queries = nz + 1
     kv_refs, query_refs = refs[:kvs], refs[kvs : kvs + queries]
     bias_ref, w_hbm, acc_ref, w_far_ref, w_ref, q_ref, att_ref, score_ref, sem = refs[kvs + queries :]
     heads = order_ref.shape[0] - 1
@@ -274,12 +274,9 @@
         for slot in range(part_refs[0].shape[0]):
             q_ref[start + slot] = jnp.concatenate([ref[slot] for ref in part_refs], axis=0)
 
-    start = 0
-    for index, slots in enumerate(NEAR_SPLIT):
-        place_rows(start, query_refs[index * nz : (index + 1) * nz])
-        start += slots
+    place_rows(0, query_refs[:nz])
     rest_refs = [query_refs[-1].at[part * rest_slots : (part + 1) * rest_slots] for part in range(nz)]
-    pl.when(extra > 0)(lambda: place_rows(start, rest_refs))
+    pl.when(extra > 0)(lambda: place_rows(NEAR_SLOTS, rest_refs))
 
     def score(pair, place):
         slot = pair * PAIR + place
@@ -362,30 +359,33 @@
         name="join",
     )(keys, values)
     kv_parts = [kv_own, *swaps_along(kv_own, "kvring")]
-    order, far, *near, rest, bias = pl.pallas_call(
+    order, far, near, rest, bias = pl.pallas_call(
         functools.partial(prep_kernel, rows, nq, nz),
         out_shape=(
             pltpu.SMEM((heads + 1,), jnp.int32),
-            *(slots_in_vmem(slots) for slots in (FAR_SLOTS, *NEAR_SPLIT, rest_slots)),
+            *(slots_in_vmem(slots) for slots in (FAR_SLOTS, NEAR_SLOTS, rest_slots)),
             pltpu.VMEM((quarter, total), jnp.float32),
         ),
         in_specs=[smem, vmem, vmem],
-        out_specs=[smem] + [vmem] * (len(NEAR_SPLIT) + 3),
+        out_specs=[smem] + [vmem] * 4,
         cost_estimate=cost(4),
         name="prep",
     )(head_mask, doc_ids, queries)
     many = jnp.sum(head_mask) > NEAR_SLOTS + FAR_SLOTS
-    *kv_parts, near[0], near[1], order, many = lax.optimization_barrier((*kv_parts, *near, order, many))
+    *kv_parts, near, order, many = lax.optimization_barrier((*kv_parts, near, order, many))
     kv0 = jnp.concatenate(kv_parts, axis=0)
     kv2 = swap_along(kv0, "qring", 2)
-    near_parts = [[array, *swaps_along(array, "kvring")] for array in near]
+    near_parts = [near, *swaps_along(near, "kvring")]
     rest_all = lax.cond(
         many,
         lambda array: jnp.concatenate([array, *swaps_along(array, "kvring")]),
         lambda array: jnp.zeros((nz * rest_slots, rows, HD), array.dtype),
         lax.optimization_barrier((rest, kv0))[0],
     )
-    *near_parts[0], kv2, rest_all = lax.optimization_barrier((*near_parts[0], kv2, rest_all))
+    early = [near_parts[slot] for slot in EARLY]
+    *early, kv2, rest_all = lax.optimization_barrier((*early, kv2, rest_all))
+    for slot, part in zip(EARLY, early):
+        near_parts[slot] = part
     kv02 = jnp.concatenate([kv0, kv2], axis=0)
     kv = (kv02, swap_along(kv02, "qring", 1))
     far_own = pl.pallas_call(
@@ -404,7 +404,7 @@
             pltpu.VMEM((quarter, width), jnp.float32),
             pltpu.VMEM((FAR_SLOTS * HD, width), jnp.bfloat16),
         ),
-        in_specs=[smem] + [vmem] * (len(kv) + nz * len(near) + 2) + [hbm],
+        in_specs=[smem] + [vmem] * (len(kv) + nz + 2) + [hbm],
         out_specs=(vmem, vmem),
         scratch_shapes=[
             pltpu.VMEM(((heads - FAR_SLOTS) * HD, width), jnp.bfloat16),
@@ -416,7 +416,7 @@
         compiler_params=params,
         cost_estimate=cost(6),
         name="first",
-    )(order, *in_vmem(*kv, *sum(near_parts, []), rest_all, bias), w_out)
+    )(order, *in_vmem(*kv, *near_parts, rest_all, bias), w_out)
     return pl.pallas_call(
         functools.partial(last_kernel, nz),
         out_shape=jax.ShapeDtypeStruct((quarter, width), jnp.bfloat16),

time: 50.7 us -> 48.8 us (0.963)
  starting transfers between devices: 20.7 us -> 17.1 us
  waiting for transfers between devices: 12.9 us -> 14.6 us
    ppermute x14 -> x11, starting transfers between devices: 20.7 us -> 17.1 us  [swap_along(): lax.ppermute(array, axis_name, [(i, i ^ partner) for i in range(size)])]
    ppermute x14 -> x11, waiting for transfers between devices: 12.9 us -> 14.6 us  [swap_along(): lax.ppermute(array, axis_name, [(i, i ^ partner) for i in range(size)])]
    pallas_call x1, Pallas kernels: 8.95 us -> 8.19 us  [per_device_small_ring(): pl.pallas_call(functools.partial(first_kernel, len(kv), nz), out_shape=(p...]
  transfers between devices with their start and end apart: 14 -> 11, of which waited for: 6 -> 6; matrix products, arithmetic and copies ran while one was open for 1% -> 1% of each run, Pallas kernels for 24% -> 25%
where the time goes in v4:
time: 48.8 us; the launch traced here: 48.1 us
  starting transfers between devices  17.1 us (35%)
  Pallas kernels  14.9 us (31%)
  waiting for transfers between devices  14.6 us (30%)
  between operations  0.76 us (2%)
  other arithmetic  0.63 us (1%)
    ppermute x11, starting transfers between devices, swap_along(): lax.ppermute(array, axis_name, [(i, i ^ partner) for i in range(size)])  17.1 us
    ppermute x11, waiting for transfers between devices, swap_along(): lax.ppermute(array, axis_name, [(i, i ^ partner) for i in range(size)])  14.6 us
    pallas_call x1, Pallas kernels, per_device_small_ring(): pl.pallas_call(functools.partial(first_kernel, len(kv), nz), out_shape=(p...  8.19 us
    pallas_call x1, Pallas kernels, per_device_small_ring(): pl.pallas_call(functools.partial(last_kernel, nz), out_shape=jax.ShapeDty...  2.28 us
    pallas_call x1, Pallas kernels, per_device_small_ring(): pl.pallas_call(functools.partial(own_kernel, len(kv)), out_shape=slots_in...  2.16 us
    pallas_call x1, Pallas kernels, per_device_small_ring(): pl.pallas_call(functools.partial(prep_kernel, rows, nq, nz), out_shape=(p...  1.47 us
  transfers between devices with their start and end apart: 11, of which 6 were waited for; matrix products, arithmetic and copies ran while one was open for 1% of the time, Pallas kernels for 25%

profile of v4, /device:TPU:0, one launch (start us, length us, event | category | flops | bytes accessed | tf_op | source)
XLA Modules:
  0.0 48.1 jit_solution(4912630053675967300)
XLA Ops:
  0.0 0.8 %join.1 = bf16[48,1024]{1,0:T(8,128)(2,1)S(1)} custom-call(bf16[48,512]{1,0:T(8,128)(2,1)} %k_ref.1, bf16[48,512]{1,0:T(8,128)(2,1)} %v_ref.1), custom_call_target="tpu_custom_call" | custom-call | tf_op jit(solution)/shard_map/join/pallas_call | solution.py:354
  0.8 5.1 %collective-permute-start.3 = (bf16[48,1024]{1,0:T(8,128)(2,1)S(1)}, bf16[48,1024]{1,0:T(8,128)(2,1)S(1)}, u32[]{:S(2)}, u32[]{:S(2)}) collective-permute-start(bf16[48,1024]{1,0:T(8,128)(2,1)S(1)} %join.1), channel_id=1, source_target_pairs={{0,3},{1,2},{2,1},{3,0},{4,7},{5,6},{6,5},{7,4},{8,11},{9,10},{10,... | collective-permute-start | bytes 294920 | tf_op jit(solution)/shard_map/ppermute | solution.py:152
  5.9 0.0 collective-permute-start.4
  6.0 0.6 %collective-permute-start.5 = (bf16[48,1024]{1,0:T(8,128)(2,1)S(1)}, bf16[48,1024]{1,0:T(8,128)(2,1)S(1)}, u32[]{:S(2)}, u32[]{:S(2)}) collective-permute-start(bf16[48,1024]{1,0:T(8,128)(2,1)S(1)} %join.1), channel_id=1, source_target_pairs={{0,1},{1,0},{2,3},{3,2},{4,5},{5,4},{6,7},{7,6},{8,9},{9,8},{10,11... | collective-permute-start | bytes 294920 | tf_op jit(solution)/shard_map/ppermute | solution.py:152
  6.6 1.5 %prep.1 = (s32[33]{0:T(128)S(4)}, bf16[12,48,128]{2,1,0:T(8,128)(2,1)S(1)}, bf16[14,48,128]{2,1,0:T(8,128)(2,1)S(1)}, bf16[6,48,128]{2,1,0:T(8,128)(2,1)S(1)}, f32[192,768]{1,0:T(8,128)S(1)}) custom-call(s32[32]{0:T(128)} %mask_ref.1, s32[768]{0:T(1024)} %doc_ref.1, bf16[48,4096]{1,0:T(8,128)(2,1)} %q_ref.1), custom_call_target="tpu_custom_call" | custom-call | flops 4000000000 | tf_op jit(solution)/shard_map/prep/pallas_call | solution.py:362
  8.1 0.6 %reduce_sum.9 = s32[]{:T(128)} reduce(s32[32]{0:T(128)S(1)} %copy-done, s32[]{:T(128)} %constant.1.clone.1), dimensions={0}, to_apply=%region_0.0 | reduce | flops 31 | bytes 136 | tf_op jit(solution)/shard_map/reduce_sum | solution.py:374
  9.4 0.3 collective-permute-done.3
  9.6 4.6 %collective-permute-done.4 = bf16[48,1024]{1,0:T(8,128)(2,1)S(1)} collective-permute-done((bf16[48,1024]{1,0:T(8,128)(2,1)S(1)}, bf16[48,1024]{1,0:T(8,128)(2,1)S(1)}, u32[]{:S(2)}, u32[]{:S(2)}) %collective-permute-start.4) | collective-permute-done | bytes 98336 | tf_op jit(solution)/shard_map/ppermute | solution.py:152
  14.2 0.0 collective-permute-done.5
  14.3 1.6 %collective-permute-start.7 = (bf16[192,1024]{1,0:T(8,128)(2,1)S(1)}, bf16[192,1024]{1,0:T(8,128)(2,1)S(1)}, u32[]{:S(2)}, u32[]{:S(2)}) collective-permute-start(bf16[192,1024]{1,0:T(8,128)(2,1)S(1)} %get-tuple-element.45), channel_id=1, source_target_pairs={{0,8},{4,12},{8,0},{12,4},{1,9},{5,13},{9,1},{13,5},{2,10},{6,14},... | collective-permute-start | bytes 1179656 | tf_op jit(solution)/shard_map/ppermute | solution.py:152
  15.9 2.5 %collective-permute-start.6 = (bf16[14,48,128]{2,1,0:T(8,128)(2,1)S(1)}, bf16[14,48,128]{2,1,0:T(8,128)(2,1)S(1)}, u32[]{:S(2)}, u32[]{:S(2)}) collective-permute-start(bf16[14,48,128]{2,1,0:T(8,128)(2,1)S(1)} %get-tuple-element.34.refs_2_), channel_id=1, source_target_pairs={{0,3},{1,2},{2,1},{3,0},{4,7},{5,6},{6,5},{7,4},{8,11},{9,10},{10,... | collective-permute-start | bytes 516104 | tf_op jit(solution)/shard_map/ppermute | solution.py:152
  18.4 4.7 %collective-permute-done.6.refs_3_ = bf16[14,48,128]{2,1,0:T(8,128)(2,1)S(1)} collective-permute-done((bf16[14,48,128]{2,1,0:T(8,128)(2,1)S(1)}, bf16[14,48,128]{2,1,0:T(8,128)(2,1)S(1)}, u32[]{:S(2)}, u32[]{:S(2)}) %collective-permute-start.6) | collective-permute-done | bytes 172064 | tf_op jit(solution)/shard_map/ppermute | solution.py:152
  23.1 1.4 %collective-permute-done.7 = bf16[192,1024]{1,0:T(8,128)(2,1)S(1)} collective-permute-done((bf16[192,1024]{1,0:T(8,128)(2,1)S(1)}, bf16[192,1024]{1,0:T(8,128)(2,1)S(1)}, u32[]{:S(2)}, u32[]{:S(2)}) %collective-permute-start.7) | collective-permute-done | bytes 393248 | tf_op jit(solution)/shard_map/ppermute | solution.py:152
  24.6 0.1 collective-permute-start.8
  24.7 1.1 %collective-permute-start.12 = (bf16[14,48,128]{2,1,0:T(8,128)(2,1)S(1)}, bf16[14,48,128]{2,1,0:T(8,128)(2,1)S(1)}, u32[]{:S(2)}, u32[]{:S(2)}) collective-permute-start(bf16[14,48,128]{2,1,0:T(8,128)(2,1)S(1)} %get-tuple-element.34.refs_2_), channel_id=1, source_target_pairs={{0,2},{1,3},{2,0},{3,1},{4,6},{5,7},{6,4},{7,5},{8,10},{9,11},{10,... | collective-permute-start | bytes 516104 | tf_op jit(solution)/shard_map/ppermute | solution.py:152
  25.7 1.7 %collective-permute-start.13 = (bf16[14,48,128]{2,1,0:T(8,128)(2,1)S(1)}, bf16[14,48,128]{2,1,0:T(8,128)(2,1)S(1)}, u32[]{:S(2)}, u32[]{:S(2)}) collective-permute-start(bf16[14,48,128]{2,1,0:T(8,128)(2,1)S(1)} %get-tuple-element.34.refs_2_), channel_id=1, source_target_pairs={{0,1},{1,0},{2,3},{3,2},{4,5},{5,4},{6,7},{7,6},{8,9},{9,8},{10,11... | collective-permute-start | bytes 516104 | tf_op jit(solution)/shard_map/ppermute | solution.py:152
  27.4 2.2 %own.1.refs_0_ = bf16[12,48,128]{2,1,0:T(8,128)(2,1)S(1)} custom-call(s32[33]{0:T(128)S(4)} %get-tuple-element.29.order_ref, bf16[384,1024]{1,0:T(8,128)(2,1)S(1)} %constant_dynamic-update-slice_fusion.4.refs_0_, bf16[384,1024]{1,0:T(8,128)(2,1)S(1)} %collective-permute-done.8.refs_1_, bf16[12,48,128]{2,1,0:T(8,128)(2,1)S(1)} %get-tuple-element.39.refs_2_, ...), custom_call_target="tpu_custom_call" | custom-call | flops 2000000000 | tf_op jit(solution)/shard_map/own/pallas_call | solution.py:391
  29.5 1.0 %collective-permute-start.10 = (bf16[12,48,128]{2,1,0:T(8,128)(2,1)S(1)}, bf16[12,48,128]{2,1,0:T(8,128)(2,1)S(1)}, u32[]{:S(2)}, u32[]{:S(2)}) collective-permute-start(bf16[12,48,128]{2,1,0:T(8,128)(2,1)S(1)} %own.1.refs_0_), channel_id=1, source_target_pairs={{0,2},{1,3},{2,0},{3,1},{4,6},{5,7},{6,4},{7,5},{8,10},{9,11},{10,... | collective-permute-start | bytes 442376 | tf_op jit(solution)/shard_map/ppermute | solution.py:152
  30.6 1.3 %collective-permute-start.11 = (bf16[12,48,128]{2,1,0:T(8,128)(2,1)S(1)}, bf16[12,48,128]{2,1,0:T(8,128)(2,1)S(1)}, u32[]{:S(2)}, u32[]{:S(2)}) collective-permute-start(bf16[12,48,128]{2,1,0:T(8,128)(2,1)S(1)} %own.1.refs_0_), channel_id=1, source_target_pairs={{0,1},{1,0},{2,3},{3,2},{4,5},{5,4},{6,7},{7,6},{8,9},{9,8},{10,11... | collective-permute-start | bytes 442376 | tf_op jit(solution)/shard_map/ppermute | solution.py:152
  31.9 2.1 %collective-permute-start.9 = (bf16[12,48,128]{2,1,0:T(8,128)(2,1)S(1)}, bf16[12,48,128]{2,1,0:T(8,128)(2,1)S(1)}, u32[]{:S(2)}, u32[]{:S(2)}) collective-permute-start(bf16[12,48,128]{2,1,0:T(8,128)(2,1)S(1)} %own.1.refs_0_), channel_id=1, source_target_pairs={{0,3},{1,2},{2,1},{3,0},{4,7},{5,6},{6,5},{7,4},{8,11},{9,10},{10,... | collective-permute-start | bytes 442376 | tf_op jit(solution)/shard_map/ppermute | solution.py:152
  34.0 2.8 %collective-permute-done.12.refs_4_ = bf16[14,48,128]{2,1,0:T(8,128)(2,1)S(1)} collective-permute-done((bf16[14,48,128]{2,1,0:T(8,128)(2,1)S(1)}, bf16[14,48,128]{2,1,0:T(8,128)(2,1)S(1)}, u32[]{:S(2)}, u32[]{:S(2)}) %collective-permute-start.12) | collective-permute-done | bytes 172064 | tf_op jit(solution)/shard_map/ppermute | solution.py:152
  36.8 8.2 %first.1 = (f32[192,2048]{1,0:T(8,128)S(1)}, bf16[1536,2048]{1,0:T(8,128)(2,1)S(1)}) custom-call(s32[33]{0:T(128)S(4)} %get-tuple-element.29.order_ref, bf16[384,1024]{1,0:T(8,128)(2,1)S(1)} %constant_dynamic-update-slice_fusion.4.refs_0_, bf16[384,1024]{1,0:T(8,128)(2,1)S(1)} %collective-permute-done.8.refs_1_, ...), custom_call_target="tpu_custom_call" | custom-call | flops 6000000000 | tf_op jit(solution)/shard_map/first/pallas_call | solution.py:401
  45.0 0.8 %collective-permute-done.9.refs_1_ = bf16[12,48,128]{2,1,0:T(8,128)(2,1)S(1)} collective-permute-done((bf16[12,48,128]{2,1,0:T(8,128)(2,1)S(1)}, bf16[12,48,128]{2,1,0:T(8,128)(2,1)S(1)}, u32[]{:S(2)}, u32[]{:S(2)}) %collective-permute-start.9) | collective-permute-done | bytes 147488 | tf_op jit(solution)/shard_map/ppermute | solution.py:152
  45.8 2.3 %last.1 = bf16[192,2048]{1,0:T(8,128)(2,1)} custom-call(bf16[12,48,128]{2,1,0:T(8,128)(2,1)S(1)} %own.1.refs_0_, bf16[12,48,128]{2,1,0:T(8,128)(2,1)S(1)} %collective-permute-done.9.refs_1_, bf16[12,48,128]{2,1,0:T(8,128)(2,1)S(1)} %collective-permute-done.10.refs_2_, bf16[12,48,128]{2,1,0:T(8,128)(2,1)S(1)} %collective-permute-done.11.refs_3_, ...), custom_call_target="tpu_custom_call" | custom-call | tf_op jit(solution)/shard_map/last/pallas_call | solution.py:420
  (13 shorter events, 0.2 us)
Async XLA Ops:
  0.8 7.2 %copy-start = (s32[32]{0:T(128)S(1)}, s32[32]{0:T(128)}, u32[]{:S(2)}) copy-start(s32[32]{0:T(128)} %mask_ref.1) | copy-start | bytes 388
  0.8 8.8 %collective-permute-start.3 = (bf16[48,1024]{1,0:T(8,128)(2,1)S(1)}, bf16[48,1024]{1,0:T(8,128)(2,1)S(1)}, u32[]{:S(2)}, u32[]{:S(2)}) collective-permute-start(bf16[48,1024]{1,0:T(8,128)(2,1)S(1)} %join.1), channel_id=1, source_target_pairs={{0,3},{1,2},{2,1},{3,0},{4,7},{5,6},{6,5},{7,4},{8,11},{9,10},{10,... | collective-permute-start | bytes 294920 | tf_op jit(solution)/shard_map/ppermute | solution.py:152
  5.9 8.3 %collective-permute-start.4 = (bf16[48,1024]{1,0:T(8,128)(2,1)S(1)}, bf16[48,1024]{1,0:T(8,128)(2,1)S(1)}, u32[]{:S(2)}, u32[]{:S(2)}) collective-permute-start(bf16[48,1024]{1,0:T(8,128)(2,1)S(1)} %join.1), channel_id=1, source_target_pairs={{0,2},{1,3},{2,0},{3,1},{4,6},{5,7},{6,4},{7,5},{8,10},{9,11},{10,... | collective-permute-start | bytes 294920 | tf_op jit(solution)/shard_map/ppermute | solution.py:152
  6.0 8.3 %collective-permute-start.5 = (bf16[48,1024]{1,0:T(8,128)(2,1)S(1)}, bf16[48,1024]{1,0:T(8,128)(2,1)S(1)}, u32[]{:S(2)}, u32[]{:S(2)}) collective-permute-start(bf16[48,1024]{1,0:T(8,128)(2,1)S(1)} %join.1), channel_id=1, source_target_pairs={{0,1},{1,0},{2,3},{3,2},{4,5},{5,4},{6,7},{7,6},{8,9},{9,8},{10,11... | collective-permute-start | bytes 294920 | tf_op jit(solution)/shard_map/ppermute | solution.py:152
  14.3 10.2 %collective-permute-start.7 = (bf16[192,1024]{1,0:T(8,128)(2,1)S(1)}, bf16[192,1024]{1,0:T(8,128)(2,1)S(1)}, u32[]{:S(2)}, u32[]{:S(2)}) collective-permute-start(bf16[192,1024]{1,0:T(8,128)(2,1)S(1)} %get-tuple-element.45), channel_id=1, source_target_pairs={{0,8},{4,12},{8,0},{12,4},{1,9},{5,13},{9,1},{13,5},{2,10},{6,14},... | collective-permute-start | bytes 1179656 | tf_op jit(solution)/shard_map/ppermute | solution.py:152
  15.9 7.3 %collective-permute-start.6 = (bf16[14,48,128]{2,1,0:T(8,128)(2,1)S(1)}, bf16[14,48,128]{2,1,0:T(8,128)(2,1)S(1)}, u32[]{:S(2)}, u32[]{:S(2)}) collective-permute-start(bf16[14,48,128]{2,1,0:T(8,128)(2,1)S(1)} %get-tuple-element.34.refs_2_), channel_id=1, source_target_pairs={{0,3},{1,2},{2,1},{3,0},{4,7},{5,6},{6,5},{7,4},{8,11},{9,10},{10,... | collective-permute-start | bytes 516104 | tf_op jit(solution)/shard_map/ppermute | solution.py:152
  24.6 2.8 %collective-permute-start.8 = (bf16[384,1024]{1,0:T(8,128)(2,1)S(1)}, bf16[384,1024]{1,0:T(8,128)(2,1)S(1)}, u32[]{:S(2)}, u32[]{:S(2)}) collective-permute-start(bf16[384,1024]{1,0:T(8,128)(2,1)S(1)} %constant_dynamic-update-slice_fusion.4.refs_0_), channel_id=1, source_target_pairs={{0,4},{4,0},{8,12},{12,8},{1,5},{5,1},{9,13},{13,9},{2,6},{6,2},{1... | collective-permute-start | bytes 2359304 | tf_op jit(solution)/shard_map/ppermute | solution.py:152
  24.7 12.1 %collective-permute-start.12 = (bf16[14,48,128]{2,1,0:T(8,128)(2,1)S(1)}, bf16[14,48,128]{2,1,0:T(8,128)(2,1)S(1)}, u32[]{:S(2)}, u32[]{:S(2)}) collective-permute-start(bf16[14,48,128]{2,1,0:T(8,128)(2,1)S(1)} %get-tuple-element.34.refs_2_), channel_id=1, source_target_pairs={{0,2},{1,3},{2,0},{3,1},{4,6},{5,7},{6,4},{7,5},{8,10},{9,11},{10,... | collective-permute-start | bytes 516104 | tf_op jit(solution)/shard_map/ppermute | solution.py:152
  25.7 11.1 %collective-permute-start.13 = (bf16[14,48,128]{2,1,0:T(8,128)(2,1)S(1)}, bf16[14,48,128]{2,1,0:T(8,128)(2,1)S(1)}, u32[]{:S(2)}, u32[]{:S(2)}) collective-permute-start(bf16[14,48,128]{2,1,0:T(8,128)(2,1)S(1)} %get-tuple-element.34.refs_2_), channel_id=1, source_target_pairs={{0,1},{1,0},{2,3},{3,2},{4,5},{5,4},{6,7},{7,6},{8,9},{9,8},{10,11... | collective-permute-start | bytes 516104 | tf_op jit(solution)/shard_map/ppermute | solution.py:152
  29.5 15.4 %collective-permute-start.10 = (bf16[12,48,128]{2,1,0:T(8,128)(2,1)S(1)}, bf16[12,48,128]{2,1,0:T(8,128)(2,1)S(1)}, u32[]{:S(2)}, u32[]{:S(2)}) collective-permute-start(bf16[12,48,128]{2,1,0:T(8,128)(2,1)S(1)} %own.1.refs_0_), channel_id=1, source_target_pairs={{0,2},{1,3},{2,0},{3,1},{4,6},{5,7},{6,4},{7,5},{8,10},{9,11},{10,... | collective-permute-start | bytes 442376 | tf_op jit(solution)/shard_map/ppermute | solution.py:152
  30.6 14.4 %collective-permute-start.11 = (bf16[12,48,128]{2,1,0:T(8,128)(2,1)S(1)}, bf16[12,48,128]{2,1,0:T(8,128)(2,1)S(1)}, u32[]{:S(2)}, u32[]{:S(2)}) collective-permute-start(bf16[12,48,128]{2,1,0:T(8,128)(2,1)S(1)} %own.1.refs_0_), channel_id=1, source_target_pairs={{0,1},{1,0},{2,3},{3,2},{4,5},{5,4},{6,7},{7,6},{8,9},{9,8},{10,11... | collective-permute-start | bytes 442376 | tf_op jit(solution)/shard_map/ppermute | solution.py:152
  31.9 13.9 %collective-permute-start.9 = (bf16[12,48,128]{2,1,0:T(8,128)(2,1)S(1)}, bf16[12,48,128]{2,1,0:T(8,128)(2,1)S(1)}, u32[]{:S(2)}, u32[]{:S(2)}) collective-permute-start(bf16[12,48,128]{2,1,0:T(8,128)(2,1)S(1)} %own.1.refs_0_), channel_id=1, source_target_pairs={{0,3},{1,2},{2,1},{3,0},{4,7},{5,6},{6,5},{7,4},{8,11},{9,10},{10,... | collective-permute-start | bytes 442376 | tf_op jit(solution)/shard_map/ppermute | solution.py:152

commit v5 on v4

--- a/solution.py
+++ b/solution.py
@@ -134,12 +134,14 @@
     )
 
 
-VMEM_LIMIT = 32 * 1024 * 1024
+VMEM_LIMIT = 24 * 1024 * 1024
 LOG2E = math.log2(math.e)
 PAIR = 2
-NEAR_SLOTS = 14
-EARLY = (1,)
-FAR_SLOTS = 12
+NEAR_SLOTS = 16
+EARLY_PARTS = 2
+EARLY_COST = 0
+FIRST_COST = 6
+FAR_SLOTS = 10
 TILE = 1024
 
 
@@ -248,39 +250,74 @@
     pl.loop(0, FAR_SLOTS, unroll=FAR_SLOTS // 2)(one_slot)
 
 
-def first_kernel(kvs, nz, order_ref, *refs):
-    queries = nz + 1
-    kv_refs, query_refs = refs[:kvs], refs[kvs : kvs + queries]
-    bias_ref, w_hbm, acc_ref, w_far_ref, w_ref, q_ref, att_ref, score_ref, sem = refs[kvs + queries :]
+def pairs_of(order_ref):
     heads = order_ref.shape[0] - 1
     rest_slots = heads - FAR_SLOTS - NEAR_SLOTS
-    kept = order_ref[heads]
-    extra = jnp.clip((kept - FAR_SLOTS - NEAR_SLOTS + PAIR - 1) // PAIR, 0, rest_slots // PAIR)
-    pairs = NEAR_SLOTS // PAIR + extra
-
-    def near_copy(slot):
-        return pltpu.make_async_copy(
-            w_hbm.at[rows_of(order_ref[FAR_SLOTS + slot])], w_ref.at[rows_of(slot)], sem.at[slot]
-        )
-
-    def far_copy(slot):
-        return pltpu.make_async_copy(
-            w_hbm.at[rows_of(order_ref[slot])], w_far_ref.at[rows_of(slot)], sem.at[heads - FAR_SLOTS + slot]
-        )
-
-    pl.loop(0, pairs * PAIR)(lambda slot: near_copy(slot).start())
-    pl.loop(0, FAR_SLOTS)(lambda slot: far_copy(slot).start())
-    def place_rows(start, part_refs):
-        for slot in range(part_refs[0].shape[0]):
-            q_ref[start + slot] = jnp.concatenate([ref[slot] for ref in part_refs], axis=0)
-
-    place_rows(0, query_refs[:nz])
-    rest_refs = [query_refs[-1].at[part * rest_slots : (part + 1) * rest_slots] for part in range(nz)]
-    pl.when(extra > 0)(lambda: place_rows(NEAR_SLOTS, rest_refs))
-
+    extra = jnp.clip((order_ref[heads] - FAR_SLOTS - NEAR_SLOTS + PAIR - 1) // PAIR, 0, rest_slots // PAIR)
+    return NEAR_SLOTS // PAIR + extra, extra
+
+
+def place_queries(parts, extra, near_refs, rest_ref, q_ref):
+    rest_slots = q_ref.shape[0] - NEAR_SLOTS
+    for slot in range(NEAR_SLOTS):
+        q_ref[slot] = jnp.concatenate([ref[slot] for ref in near_refs], axis=0)
+
+    @pl.when(extra > 0)
+    def _():
+        for slot in range(rest_slots):
+            rows = [rest_ref[part * rest_slots + slot] for part in parts]
+            q_ref[NEAR_SLOTS + slot] = jnp.concatenate(rows, axis=0)
+
+
+def attend_pairs(pairs, q_ref, score_ref, bias, kv_refs, order_ref, keep, between):
     def score(pair, place):
         slot = pair * PAIR + place
         score_ref[place] = scores_of(q_ref[slot], FAR_SLOTS + slot, kv_refs, order_ref)
+
+    for place in range(PAIR):
+        score(0, place)
+
+    def one_pair(pair):
+        later = jnp.minimum(pair + 1, pairs - 1)
+        between(pair)
+        for place in range(PAIR):
+            slot = pair * PAIR + place
+            keep(slot, place, attended(score_ref[place], bias, FAR_SLOTS + slot, kv_refs, order_ref))
+            score(later, place)
+
+    pl.loop(0, pairs)(one_pair)
+
+
+def w_copy(order_ref, w_hbm, w_ref, sem, start, slot):
+    return pltpu.make_async_copy(w_hbm.at[rows_of(order_ref[start + slot])], w_ref.at[rows_of(slot)], sem.at[slot])
+
+
+def early_kernel(kvs, order_ref, *refs):
+    kv_refs, near_refs = refs[:kvs], refs[kvs : kvs + EARLY_PARTS]
+    rest_ref, bias_ref, w_hbm, early_ref, w_ref, q_ref, score_ref, sem = refs[kvs + EARLY_PARTS :]
+    pairs, extra = pairs_of(order_ref)
+    copy_of = functools.partial(w_copy, order_ref, w_hbm, w_ref, sem, FAR_SLOTS)
+    pl.loop(0, pairs * PAIR)(lambda slot: copy_of(slot).start())
+    place_queries(range(EARLY_PARTS), extra, near_refs, rest_ref, q_ref)
+    rows = q_ref.shape[1]
+
+    def keep(slot, place, rows_attended):
+        early_ref[slot] = rows_attended
+
+    attend_pairs(pairs, q_ref, score_ref, bias_ref[:rows], kv_refs, order_ref, keep, lambda pair: None)
+    pl.loop(0, pairs * PAIR)(lambda slot: copy_of(slot).wait())
+
+
+def first_kernel(kvs, nz, order_ref, *refs):
+    late = nz - EARLY_PARTS
+    kv_refs, near_refs = refs[:kvs], refs[kvs : kvs + late]
+    rest_ref, early_ref, bias_ref, w_ref, w_hbm, acc_ref, w_far_ref, q_ref, att_ref, score_ref, sem = refs[kvs + late :]
+    pairs, extra = pairs_of(order_ref)
+    copy_of = functools.partial(w_copy, order_ref, w_hbm, w_far_ref, sem, 0)
+    pl.loop(0, FAR_SLOTS)(lambda slot: copy_of(slot).start())
+
+    place_queries(range(EARLY_PARTS, nz), extra, near_refs, rest_ref, q_ref)
+    done = early_ref.shape[1]
 
     def project(pair):
         rows = pl.ds(pl.multiple_of(pair * PAIR * HD, HD), PAIR * HD)
@@ -289,34 +326,22 @@
                 att_ref[...], w_ref[rows, at : at + TILE], preferred_element_type=jnp.float32
             )
 
+    def keep(slot, place, rows_attended):
+        att_ref[:done, place * HD : (place + 1) * HD] = early_ref[slot]
+        att_ref[done:, place * HD : (place + 1) * HD] = rows_attended
+
+    def between(pair):
+        project(jnp.maximum(pair - 1, 0))
+
     acc_ref[...] = jnp.zeros_like(acc_ref)
     att_ref[...] = jnp.zeros_like(att_ref)
-    for place in range(PAIR):
-        score(0, place)
-        near_copy(place).wait()
-
-    def one_pair(pair):
-        later = jnp.minimum(pair + 1, pairs - 1)
-        project(jnp.maximum(pair - 1, 0))
-        for place in range(PAIR):
-            slot = pair * PAIR + place
-            att_ref[:, place * HD : (place + 1) * HD] = attended(
-                score_ref[place], bias_ref[...], FAR_SLOTS + slot, kv_refs, order_ref
-            )
-            score(later, place)
-
-        @pl.when(pair + 1 < pairs)
-        def _():
-            for place in range(PAIR):
-                near_copy((pair + 1) * PAIR + place).wait()
-
-    pl.loop(0, pairs)(one_pair)
+    attend_pairs(pairs, q_ref, score_ref, bias_ref[done:], kv_refs, order_ref, keep, between)
     project(pairs - 1)
-    pl.loop(0, FAR_SLOTS)(lambda slot: far_copy(slot).wait())
+    pl.loop(0, FAR_SLOTS)(lambda slot: copy_of(slot).wait())
 
 
 def last_kernel(nz, *refs):
-    att_refs, (w_ref, acc_ref, out_ref, att_ref) = refs[:nz], refs[nz:]
+    att_refs, (w_ref, acc_ref, out_ref, att_ref) = refs[:nz][::-1], refs[nz:]
     for slot in range(FAR_SLOTS):
         att_ref[:, slot * HD : (slot + 1) * HD] = jnp.concatenate([ref[slot] for ref in att_refs], axis=0)
     rows = att_refs[0].shape[1]
@@ -342,7 +367,7 @@
     rest_slots = heads - FAR_SLOTS - NEAR_SLOTS
     smem = pl.BlockSpec(memory_space=pltpu.SMEM)
     vmem = pl.BlockSpec(memory_space=pltpu.VMEM)
-    hbm = pl.BlockSpec(memory_space=pl.ANY)
+    hbm = pl.BlockSpec(memory_space=pltpu.HBM)
     params = pltpu.CompilerParams(vmem_limit_bytes=VMEM_LIMIT)
 
     def cost(micros):
@@ -382,10 +407,7 @@
         lambda array: jnp.zeros((nz * rest_slots, rows, HD), array.dtype),
         lax.optimization_barrier((rest, kv0))[0],
     )
-    early = [near_parts[slot] for slot in EARLY]
-    *early, kv2, rest_all = lax.optimization_barrier((*early, kv2, rest_all))
-    for slot, part in zip(EARLY, early):
-        near_parts[slot] = part
+    near_parts[1], kv2, rest_all = lax.optimization_barrier((near_parts[1], kv2, rest_all))
     kv02 = jnp.concatenate([kv0, kv2], axis=0)
     kv = (kv02, swap_along(kv02, "qring", 1))
     far_own = pl.pallas_call(
@@ -398,25 +420,46 @@
         name="own",
     )(order, *in_vmem(*kv, far, bias))
     far_parts = [far_own, *swaps_along(far_own, "kvring")]
+    near_slots = heads - FAR_SLOTS
+    early_rows = EARLY_PARTS * rows
+    late_rows = quarter - early_rows
+    order_early = lax.optimization_barrier((order, far_own))[0]
+    hbm = pl.BlockSpec(memory_space=pltpu.HBM)
+    early, w_near = pl.pallas_call(
+        functools.partial(early_kernel, len(kv)),
+        out_shape=(
+            pltpu.VMEM((near_slots, early_rows, HD), jnp.bfloat16),
+            pltpu.VMEM((near_slots * HD, width), jnp.bfloat16),
+        ),
+        in_specs=[smem] + [vmem] * (len(kv) + EARLY_PARTS + 2) + [hbm],
+        out_specs=(vmem, vmem),
+        scratch_shapes=[
+            pltpu.VMEM((near_slots, early_rows, HD), jnp.bfloat16),
+            pltpu.VMEM((PAIR, early_rows, total), jnp.float32),
+            pltpu.SemaphoreType.DMA((near_slots,)),
+        ],
+        compiler_params=params,
+        cost_estimate=cost(EARLY_COST),
+        name="early",
+    )(order_early, *in_vmem(*kv, *near_parts[:EARLY_PARTS], rest_all, bias), w_out)
     acc, w_far = pl.pallas_call(
         functools.partial(first_kernel, len(kv), nz),
         out_shape=(
             pltpu.VMEM((quarter, width), jnp.float32),
             pltpu.VMEM((FAR_SLOTS * HD, width), jnp.bfloat16),
         ),
-        in_specs=[smem] + [vmem] * (len(kv) + nz + 2) + [hbm],
+        in_specs=[smem] + [vmem] * (len(kv) + nz - EARLY_PARTS + 4) + [hbm],
         out_specs=(vmem, vmem),
         scratch_shapes=[
-            pltpu.VMEM(((heads - FAR_SLOTS) * HD, width), jnp.bfloat16),
-            pltpu.VMEM((heads - FAR_SLOTS, quarter, HD), jnp.bfloat16),
+            pltpu.VMEM((near_slots, late_rows, HD), jnp.bfloat16),
             pltpu.VMEM((quarter, PAIR * HD), jnp.bfloat16),
-            pltpu.VMEM((PAIR, quarter, total), jnp.float32),
-            pltpu.SemaphoreType.DMA((heads,)),
+            pltpu.VMEM((PAIR, late_rows, total), jnp.float32),
+            pltpu.SemaphoreType.DMA((FAR_SLOTS,)),
         ],
         compiler_params=params,
-        cost_estimate=cost(6),
+        cost_estimate=cost(FIRST_COST),
         name="first",
-    )(order, *in_vmem(*kv, *near_parts, rest_all, bias), w_out)
+    )(order, *in_vmem(*kv, *near_parts[EARLY_PARTS:], rest_all, early, bias, w_near), w_out)
     return pl.pallas_call(
         functools.partial(last_kernel, nz),
         out_shape=jax.ShapeDtypeStruct((quarter, width), jnp.bfloat16),
@@ -425,7 +468,7 @@
         scratch_shapes=[pltpu.VMEM((quarter, FAR_SLOTS * HD), jnp.bfloat16)],
         compiler_params=params,
         name="last",
-    )(*in_vmem(*far_parts, w_far, acc))
+    )(*in_vmem(*far_parts[::-1], w_far, acc))
 
 
 def solution(mesh):

time: 48.8 us -> 47.8 us (0.980)
  Pallas kernels: 14.9 us -> 18.2 us
  waiting for transfers between devices: 14.6 us -> 11.7 us
  starting transfers between devices: 17.1 us -> 16.2 us
    pallas_call x0 -> x1, Pallas kernels: none -> 4.75 us  [per_device_small_ring(): pl.pallas_call(functools.partial(early_kernel, len(kv)), out_shape=(pltpu...]
    ppermute x11, waiting for transfers between devices: 14.6 us -> 11.7 us  [swap_along(): lax.ppermute(array, axis_name, [(i, i ^ partner) for i in range(size)])]
    pallas_call x1, Pallas kernels: 8.19 us -> 7.1 us  [per_device_small_ring(): pl.pallas_call(functools.partial(first_kernel, len(kv), nz), out_shape=(p...]
    ppermute x11, starting transfers between devices: 17.1 us -> 16.2 us  [swap_along(): lax.ppermute(array, axis_name, [(i, i ^ partner) for i in range(size)])]
  transfers between devices with their start and end apart: 11 -> 11, of which waited for: 6 -> 5; matrix products, arithmetic and copies ran while one was open for 1% -> 1% of each run, Pallas kernels for 25% -> 32%
where the time goes in v5:
time: 47.8 us; the launch traced here: 47.6 us
  Pallas kernels  18.2 us (38%)
  starting transfers between devices  16.2 us (34%)
  waiting for transfers between devices  11.7 us (24%)
  between operations  0.77 us (2%)
  other arithmetic  0.63 us (1%)
    ppermute x11, starting transfers between devices, swap_along(): lax.ppermute(array, axis_name, [(i, i ^ partner) for i in range(size)])  16.2 us
    ppermute x11, waiting for transfers between devices, swap_along(): lax.ppermute(array, axis_name, [(i, i ^ partner) for i in range(size)])  11.7 us
    pallas_call x1, Pallas kernels, per_device_small_ring(): pl.pallas_call(functools.partial(first_kernel, len(kv), nz), out_shape=(p...  7.1 us
    pallas_call x1, Pallas kernels, per_device_small_ring(): pl.pallas_call(functools.partial(early_kernel, len(kv)), out_shape=(pltpu...  4.75 us
    pallas_call x1, Pallas kernels, per_device_small_ring(): pl.pallas_call(functools.partial(last_kernel, nz), out_shape=jax.ShapeDty...  2.09 us
    pallas_call x1, Pallas kernels, per_device_small_ring(): pl.pallas_call(functools.partial(own_kernel, len(kv)), out_shape=slots_in...  1.93 us
    pallas_call x1, Pallas kernels, per_device_small_ring(): pl.pallas_call(functools.partial(prep_kernel, rows, nq, nz), out_shape=(p...  1.47 us
  transfers between devices with their start and end apart: 11, of which 5 were waited for; matrix products, arithmetic and copies ran while one was open for 1% of the time, Pallas kernels for 32%

profile of v5, /device:TPU:0, one launch (start us, length us, event | category | flops | bytes accessed | tf_op | source)
XLA Modules:
  0.0 47.6 jit_solution(18088875475996581261)
XLA Ops:
  0.0 0.8 %join.1 = bf16[48,1024]{1,0:T(8,128)(2,1)S(1)} custom-call(bf16[48,512]{1,0:T(8,128)(2,1)} %k_ref.1, bf16[48,512]{1,0:T(8,128)(2,1)} %v_ref.1), custom_call_target="tpu_custom_call" | custom-call | tf_op jit(solution)/shard_map/join/pallas_call | solution.py:379
  0.8 5.1 %collective-permute-start.3 = (bf16[48,1024]{1,0:T(8,128)(2,1)S(1)}, bf16[48,1024]{1,0:T(8,128)(2,1)S(1)}, u32[]{:S(2)}, u32[]{:S(2)}) collective-permute-start(bf16[48,1024]{1,0:T(8,128)(2,1)S(1)} %join.1), channel_id=1, source_target_pairs={{0,3},{1,2},{2,1},{3,0},{4,7},{5,6},{6,5},{7,4},{8,11},{9,10},{10,... | collective-permute-start | bytes 294920 | tf_op jit(solution)/shard_map/ppermute | solution.py:154
  5.9 0.6 %collective-permute-start.5 = (bf16[48,1024]{1,0:T(8,128)(2,1)S(1)}, bf16[48,1024]{1,0:T(8,128)(2,1)S(1)}, u32[]{:S(2)}, u32[]{:S(2)}) collective-permute-start(bf16[48,1024]{1,0:T(8,128)(2,1)S(1)} %join.1), channel_id=1, source_target_pairs={{0,1},{1,0},{2,3},{3,2},{4,5},{5,4},{6,7},{7,6},{8,9},{9,8},{10,11... | collective-permute-start | bytes 294920 | tf_op jit(solution)/shard_map/ppermute | solution.py:154
  6.6 1.5 %prep.1 = (s32[33]{0:T(128)S(4)}, bf16[10,48,128]{2,1,0:T(8,128)(2,1)S(1)}, bf16[16,48,128]{2,1,0:T(8,128)(2,1)S(1)}, bf16[6,48,128]{2,1,0:T(8,128)(2,1)S(1)}, f32[192,768]{1,0:T(8,128)S(1)}) custom-call(s32[32]{0:T(128)} %mask_ref.1, s32[768]{0:T(1024)} %doc_ref.1, bf16[48,4096]{1,0:T(8,128)(2,1)} %q_ref.1), custom_call_target="tpu_custom_call" | custom-call | flops 4000000000 | tf_op jit(solution)/shard_map/prep/pallas_call | solution.py:387
  8.1 0.6 %reduce_sum.9 = s32[]{:T(128)} reduce(s32[32]{0:T(128)S(1)} %copy-done, s32[]{:T(128)} %constant.1.clone.1), dimensions={0}, to_apply=%region_0.0 | reduce | flops 31 | bytes 136 | tf_op jit(solution)/shard_map/reduce_sum | solution.py:399
  9.4 0.3 collective-permute-done.3
  9.6 4.6 %collective-permute-done.4 = bf16[48,1024]{1,0:T(8,128)(2,1)S(1)} collective-permute-done((bf16[48,1024]{1,0:T(8,128)(2,1)S(1)}, bf16[48,1024]{1,0:T(8,128)(2,1)S(1)}, u32[]{:S(2)}, u32[]{:S(2)}) %collective-permute-start.4) | collective-permute-done | bytes 98336 | tf_op jit(solution)/shard_map/ppermute | solution.py:154
  14.2 0.0 collective-permute-done.5
  14.3 1.6 %collective-permute-start.7 = (bf16[192,1024]{1,0:T(8,128)(2,1)S(1)}, bf16[192,1024]{1,0:T(8,128)(2,1)S(1)}, u32[]{:S(2)}, u32[]{:S(2)}) collective-permute-start(bf16[192,1024]{1,0:T(8,128)(2,1)S(1)} %get-tuple-element.51), channel_id=1, source_target_pairs={{0,8},{4,12},{8,0},{12,4},{1,9},{5,13},{9,1},{13,5},{2,10},{6,14},... | collective-permute-start | bytes 1179656 | tf_op jit(solution)/shard_map/ppermute | solution.py:154
  15.9 2.5 %collective-permute-start.6 = (bf16[16,48,128]{2,1,0:T(8,128)(2,1)S(1)}, bf16[16,48,128]{2,1,0:T(8,128)(2,1)S(1)}, u32[]{:S(2)}, u32[]{:S(2)}) collective-permute-start(bf16[16,48,128]{2,1,0:T(8,128)(2,1)S(1)} %get-tuple-element.37.refs_2_), channel_id=1, source_target_pairs={{0,3},{1,2},{2,1},{3,0},{4,7},{5,6},{6,5},{7,4},{8,11},{9,10},{10,... | collective-permute-start | bytes 589832 | tf_op jit(solution)/shard_map/ppermute | solution.py:154
  18.4 5.0 %collective-permute-done.6.refs_3_ = bf16[16,48,128]{2,1,0:T(8,128)(2,1)S(1)} collective-permute-done((bf16[16,48,128]{2,1,0:T(8,128)(2,1)S(1)}, bf16[16,48,128]{2,1,0:T(8,128)(2,1)S(1)}, u32[]{:S(2)}, u32[]{:S(2)}) %collective-permute-start.6) | collective-permute-done | bytes 196640 | tf_op jit(solution)/shard_map/ppermute | solution.py:154
  23.4 1.1 %collective-permute-done.7 = bf16[192,1024]{1,0:T(8,128)(2,1)S(1)} collective-permute-done((bf16[192,1024]{1,0:T(8,128)(2,1)S(1)}, bf16[192,1024]{1,0:T(8,128)(2,1)S(1)}, u32[]{:S(2)}, u32[]{:S(2)}) %collective-permute-start.7) | collective-permute-done | bytes 393248 | tf_op jit(solution)/shard_map/ppermute | solution.py:154
  24.6 0.1 collective-permute-start.8
  24.6 1.8 %collective-permute-start.12 = (bf16[16,48,128]{2,1,0:T(8,128)(2,1)S(1)}, bf16[16,48,128]{2,1,0:T(8,128)(2,1)S(1)}, u32[]{:S(2)}, u32[]{:S(2)}) collective-permute-start(bf16[16,48,128]{2,1,0:T(8,128)(2,1)S(1)} %get-tuple-element.37.refs_2_), channel_id=1, source_target_pairs={{0,2},{1,3},{2,0},{3,1},{4,6},{5,7},{6,4},{7,5},{8,10},{9,11},{10,... | collective-permute-start | bytes 589832 | tf_op jit(solution)/shard_map/ppermute | solution.py:154
  26.5 0.9 %collective-permute-start.13 = (bf16[16,48,128]{2,1,0:T(8,128)(2,1)S(1)}, bf16[16,48,128]{2,1,0:T(8,128)(2,1)S(1)}, u32[]{:S(2)}, u32[]{:S(2)}) collective-permute-start(bf16[16,48,128]{2,1,0:T(8,128)(2,1)S(1)} %get-tuple-element.37.refs_2_), channel_id=1, source_target_pairs={{0,1},{1,0},{2,3},{3,2},{4,5},{5,4},{6,7},{7,6},{8,9},{9,8},{10,11... | collective-permute-start | bytes 589832 | tf_op jit(solution)/shard_map/ppermute | solution.py:154
  27.4 1.9 %own.1.refs_3_ = bf16[10,48,128]{2,1,0:T(8,128)(2,1)S(1)} custom-call(s32[33]{0:T(128)S(4)} %get-tuple-element.45.order_ref, bf16[384,1024]{1,0:T(8,128)(2,1)S(1)} %constant_dynamic-update-slice_fusion.4.refs_0_, bf16[384,1024]{1,0:T(8,128)(2,1)S(1)} %collective-permute-done.8.refs_1_, bf16[10,48,128]{2,1,0:T(8,128)(2,1)S(1)} %get-tuple-element.42.refs_2_, ...), custom_call_target="tpu_custom_call" | custom-call | flops 2000000000 | tf_op jit(solution)/shard_map/own/pallas_call | solution.py:413
  29.3 1.9 %collective-permute-start.10 = (bf16[10,48,128]{2,1,0:T(8,128)(2,1)S(1)}, bf16[10,48,128]{2,1,0:T(8,128)(2,1)S(1)}, u32[]{:S(2)}, u32[]{:S(2)}) collective-permute-start(bf16[10,48,128]{2,1,0:T(8,128)(2,1)S(1)} %own.1.refs_3_), channel_id=1, source_target_pairs={{0,2},{1,3},{2,0},{3,1},{4,6},{5,7},{6,4},{7,5},{8,10},{9,11},{10,... | collective-permute-start | bytes 368648 | tf_op jit(solution)/shard_map/ppermute | solution.py:154
  31.2 1.6 %collective-permute-start.11 = (bf16[10,48,128]{2,1,0:T(8,128)(2,1)S(1)}, bf16[10,48,128]{2,1,0:T(8,128)(2,1)S(1)}, u32[]{:S(2)}, u32[]{:S(2)}) collective-permute-start(bf16[10,48,128]{2,1,0:T(8,128)(2,1)S(1)} %own.1.refs_3_), channel_id=1, source_target_pairs={{0,3},{1,2},{2,1},{3,0},{4,7},{5,6},{6,5},{7,4},{8,11},{9,10},{10,... | collective-permute-start | bytes 368648 | tf_op jit(solution)/shard_map/ppermute | solution.py:154
  32.9 0.0 collective-permute-start.9
  32.9 4.7 %early.1 = (bf16[22,96,128]{2,1,0:T(8,128)(2,1)S(1)}, bf16[2816,2048]{1,0:T(8,128)(2,1)S(1)}) custom-call(s32[33]{0:T(128)S(4)} %get-tuple-element.45.order_ref, bf16[384,1024]{1,0:T(8,128)(2,1)S(1)} %constant_dynamic-update-slice_fusion.4.refs_0_, bf16[384,1024]{1,0:T(8,128)(2,1)S(1)} %collective-permute-done.8.refs_1_, ...), custom_call_target="tpu_custom_call" | custom-call | tf_op jit(solution)/shard_map/early/pallas_call | solution.py:428
  37.6 0.0 collective-permute-done.12.refs_2_
  37.7 7.1 %first.1 = (f32[192,2048]{1,0:T(8,128)S(1)}, bf16[1280,2048]{1,0:T(8,128)(2,1)S(1)}) custom-call(s32[33]{0:T(128)S(4)} %get-tuple-element.45.order_ref, bf16[384,1024]{1,0:T(8,128)(2,1)S(1)} %constant_dynamic-update-slice_fusion.4.refs_0_, bf16[384,1024]{1,0:T(8,128)(2,1)S(1)} %collective-permute-done.8.refs_1_, ...), custom_call_target="tpu_custom_call" | custom-call | flops 6000000000 | tf_op jit(solution)/shard_map/first/pallas_call | solution.py:445
  44.8 0.7 %collective-permute-done.10.refs_1_ = bf16[10,48,128]{2,1,0:T(8,128)(2,1)S(1)} collective-permute-done((bf16[10,48,128]{2,1,0:T(8,128)(2,1)S(1)}, bf16[10,48,128]{2,1,0:T(8,128)(2,1)S(1)}, u32[]{:S(2)}, u32[]{:S(2)}) %collective-permute-start.10) | collective-permute-done | bytes 122912 | tf_op jit(solution)/shard_map/ppermute | solution.py:154
  45.5 2.1 %last.1 = bf16[192,2048]{1,0:T(8,128)(2,1)} custom-call(bf16[10,48,128]{2,1,0:T(8,128)(2,1)S(1)} %collective-permute-done.9.refs_0_, bf16[10,48,128]{2,1,0:T(8,128)(2,1)S(1)} %collective-permute-done.10.refs_1_, bf16[10,48,128]{2,1,0:T(8,128)(2,1)S(1)} %collective-permute-done.11.refs_2_, bf16[10,48,128]{2,1,0:T(8,128)(2,1)S(1)} %own.1.refs_3_, ...), custom_call_target="tpu_custom_call" | custom-call | tf_op jit(solution)/shard_map/last/pallas_call | solution.py:463
  (14 shorter events, 0.2 us)
Async XLA Ops:
  0.0 8.1 %copy-start = (s32[32]{0:T(128)S(1)}, s32[32]{0:T(128)}, u32[]{:S(2)}) copy-start(s32[32]{0:T(128)} %mask_ref.1) | copy-start | bytes 388
  0.8 8.8 %collective-permute-start.3 = (bf16[48,1024]{1,0:T(8,128)(2,1)S(1)}, bf16[48,1024]{1,0:T(8,128)(2,1)S(1)}, u32[]{:S(2)}, u32[]{:S(2)}) collective-permute-start(bf16[48,1024]{1,0:T(8,128)(2,1)S(1)} %join.1), channel_id=1, source_target_pairs={{0,3},{1,2},{2,1},{3,0},{4,7},{5,6},{6,5},{7,4},{8,11},{9,10},{10,... | collective-permute-start | bytes 294920 | tf_op jit(solution)/shard_map/ppermute | solution.py:154
  5.9 8.3 %collective-permute-start.4 = (bf16[48,1024]{1,0:T(8,128)(2,1)S(1)}, bf16[48,1024]{1,0:T(8,128)(2,1)S(1)}, u32[]{:S(2)}, u32[]{:S(2)}) collective-permute-start(bf16[48,1024]{1,0:T(8,128)(2,1)S(1)} %join.1), channel_id=1, source_target_pairs={{0,2},{1,3},{2,0},{3,1},{4,6},{5,7},{6,4},{7,5},{8,10},{9,11},{10,... | collective-permute-start | bytes 294920 | tf_op jit(solution)/shard_map/ppermute | solution.py:154
  5.9 8.3 %collective-permute-start.5 = (bf16[48,1024]{1,0:T(8,128)(2,1)S(1)}, bf16[48,1024]{1,0:T(8,128)(2,1)S(1)}, u32[]{:S(2)}, u32[]{:S(2)}) collective-permute-start(bf16[48,1024]{1,0:T(8,128)(2,1)S(1)} %join.1), channel_id=1, source_target_pairs={{0,1},{1,0},{2,3},{3,2},{4,5},{5,4},{6,7},{7,6},{8,9},{9,8},{10,11... | collective-permute-start | bytes 294920 | tf_op jit(solution)/shard_map/ppermute | solution.py:154
  14.3 10.2 %collective-permute-start.7 = (bf16[192,1024]{1,0:T(8,128)(2,1)S(1)}, bf16[192,1024]{1,0:T(8,128)(2,1)S(1)}, u32[]{:S(2)}, u32[]{:S(2)}) collective-permute-start(bf16[192,1024]{1,0:T(8,128)(2,1)S(1)} %get-tuple-element.51), channel_id=1, source_target_pairs={{0,8},{4,12},{8,0},{12,4},{1,9},{5,13},{9,1},{13,5},{2,10},{6,14},... | collective-permute-start | bytes 1179656 | tf_op jit(solution)/shard_map/ppermute | solution.py:154
  15.9 7.6 %collective-permute-start.6 = (bf16[16,48,128]{2,1,0:T(8,128)(2,1)S(1)}, bf16[16,48,128]{2,1,0:T(8,128)(2,1)S(1)}, u32[]{:S(2)}, u32[]{:S(2)}) collective-permute-start(bf16[16,48,128]{2,1,0:T(8,128)(2,1)S(1)} %get-tuple-element.37.refs_2_), channel_id=1, source_target_pairs={{0,3},{1,2},{2,1},{3,0},{4,7},{5,6},{6,5},{7,4},{8,11},{9,10},{10,... | collective-permute-start | bytes 589832 | tf_op jit(solution)/shard_map/ppermute | solution.py:154
  24.6 2.8 %collective-permute-start.8 = (bf16[384,1024]{1,0:T(8,128)(2,1)S(1)}, bf16[384,1024]{1,0:T(8,128)(2,1)S(1)}, u32[]{:S(2)}, u32[]{:S(2)}) collective-permute-start(bf16[384,1024]{1,0:T(8,128)(2,1)S(1)} %constant_dynamic-update-slice_fusion.4.refs_0_), channel_id=1, source_target_pairs={{0,4},{4,0},{8,12},{12,8},{1,5},{5,1},{9,13},{13,9},{2,6},{6,2},{1... | collective-permute-start | bytes 2359304 | tf_op jit(solution)/shard_map/ppermute | solution.py:154
  24.6 13.0 %collective-permute-start.12 = (bf16[16,48,128]{2,1,0:T(8,128)(2,1)S(1)}, bf16[16,48,128]{2,1,0:T(8,128)(2,1)S(1)}, u32[]{:S(2)}, u32[]{:S(2)}) collective-permute-start(bf16[16,48,128]{2,1,0:T(8,128)(2,1)S(1)} %get-tuple-element.37.refs_2_), channel_id=1, source_target_pairs={{0,2},{1,3},{2,0},{3,1},{4,6},{5,7},{6,4},{7,5},{8,10},{9,11},{10,... | collective-permute-start | bytes 589832 | tf_op jit(solution)/shard_map/ppermute | solution.py:154
  26.5 11.2 %collective-permute-start.13 = (bf16[16,48,128]{2,1,0:T(8,128)(2,1)S(1)}, bf16[16,48,128]{2,1,0:T(8,128)(2,1)S(1)}, u32[]{:S(2)}, u32[]{:S(2)}) collective-permute-start(bf16[16,48,128]{2,1,0:T(8,128)(2,1)S(1)} %get-tuple-element.37.refs_2_), channel_id=1, source_target_pairs={{0,1},{1,0},{2,3},{3,2},{4,5},{5,4},{6,7},{7,6},{8,9},{9,8},{10,11... | collective-permute-start | bytes 589832 | tf_op jit(solution)/shard_map/ppermute | solution.py:154
  29.3 16.2 %collective-permute-start.10 = (bf16[10,48,128]{2,1,0:T(8,128)(2,1)S(1)}, bf16[10,48,128]{2,1,0:T(8,128)(2,1)S(1)}, u32[]{:S(2)}, u32[]{:S(2)}) collective-permute-start(bf16[10,48,128]{2,1,0:T(8,128)(2,1)S(1)} %own.1.refs_3_), channel_id=1, source_target_pairs={{0,2},{1,3},{2,0},{3,1},{4,6},{5,7},{6,4},{7,5},{8,10},{9,11},{10,... | collective-permute-start | bytes 368648 | tf_op jit(solution)/shard_map/ppermute | solution.py:154
  31.2 14.2 %collective-permute-start.11 = (bf16[10,48,128]{2,1,0:T(8,128)(2,1)S(1)}, bf16[10,48,128]{2,1,0:T(8,128)(2,1)S(1)}, u32[]{:S(2)}, u32[]{:S(2)}) collective-permute-start(bf16[10,48,128]{2,1,0:T(8,128)(2,1)S(1)} %own.1.refs_3_), channel_id=1, source_target_pairs={{0,3},{1,2},{2,1},{3,0},{4,7},{5,6},{6,5},{7,4},{8,11},{9,10},{10,... | collective-permute-start | bytes 368648 | tf_op jit(solution)/shard_map/ppermute | solution.py:154
  32.9 12.6 %collective-permute-start.9 = (bf16[10,48,128]{2,1,0:T(8,128)(2,1)S(1)}, bf16[10,48,128]{2,1,0:T(8,128)(2,1)S(1)}, u32[]{:S(2)}, u32[]{:S(2)}) collective-permute-start(bf16[10,48,128]{2,1,0:T(8,128)(2,1)S(1)} %own.1.refs_3_), channel_id=1, source_target_pairs={{0,1},{1,0},{2,3},{3,2},{4,5},{5,4},{6,7},{7,6},{8,9},{9,8},{10,11... | collective-permute-start | bytes 368648 | tf_op jit(solution)/shard_map/ppermute | solution.py:154

commit v6 on v5

--- a/solution.py
+++ b/solution.py
@@ -143,6 +143,7 @@
 FIRST_COST = 6
 FAR_SLOTS = 10
 TILE = 1024
+LAST_TILE = 512
 
 
 def small_ring(mesh):
@@ -341,19 +342,25 @@
 
 
 def last_kernel(nz, *refs):
+    *refs, out_hbm, att_ref, out_ref, sem = refs
+    refs = [*refs, out_ref, att_ref]
+    copies = []
     att_refs, (w_ref, acc_ref, out_ref, att_ref) = refs[:nz][::-1], refs[nz:]
     for slot in range(FAR_SLOTS):
         att_ref[:, slot * HD : (slot + 1) * HD] = jnp.concatenate([ref[slot] for ref in att_refs], axis=0)
     rows = att_refs[0].shape[1]
     z_at = lax.axis_index("kvring")
-    for at in range(0, acc_ref.shape[1], TILE):
-        mixed = acc_ref[:, at : at + TILE] + jnp.dot(
-            att_ref[...], w_ref[:, at : at + TILE], preferred_element_type=jnp.float32
-        )
+    for index, at in enumerate(range(0, acc_ref.shape[1], LAST_TILE)):
+        tile = slice(at, at + LAST_TILE)
+        mixed = acc_ref[:, tile] + jnp.dot(att_ref[...], w_ref[:, tile], preferred_element_type=jnp.float32)
         mixed = mixed.astype(jnp.bfloat16)
         for slot in range(nz):
             place = pl.multiple_of((z_at ^ partner_of(slot, nz)) * rows, rows)
-            out_ref[pl.ds(place, rows), at : at + TILE] = mixed[slot * rows : (slot + 1) * rows]
+            out_ref[pl.ds(place, rows), tile] = mixed[slot * rows : (slot + 1) * rows]
+        copies.append(pltpu.make_async_copy(out_ref.at[:, tile], out_hbm.at[:, tile], sem.at[index]))
+        copies[-1].start()
+    for copy in copies:
+        copy.wait()
 
 
 def per_device_small_ring(queries, keys, values, doc_ids, head_mask, w_out):
@@ -441,7 +448,7 @@
         compiler_params=params,
         cost_estimate=cost(EARLY_COST),
         name="early",
-    )(order_early, *in_vmem(*kv, *near_parts[:EARLY_PARTS], rest_all, bias), w_out)
+    )(order_early, *in_vmem(*kv, *near_parts[:EARLY_PARTS], rest_all, bias), pltpu.with_memory_space_constraint(w_out, pltpu.HBM))
     acc, w_far = pl.pallas_call(
         functools.partial(first_kernel, len(kv), nz),
         out_shape=(
@@ -459,13 +466,17 @@
         compiler_params=params,
         cost_estimate=cost(FIRST_COST),
         name="first",
-    )(order, *in_vmem(*kv, *near_parts[EARLY_PARTS:], rest_all, early, bias, w_near), w_out)
+    )(order, *in_vmem(*kv, *near_parts[EARLY_PARTS:], rest_all, early, bias, w_near), pltpu.with_memory_space_constraint(w_out, pltpu.HBM))
     return pl.pallas_call(
         functools.partial(last_kernel, nz),
         out_shape=jax.ShapeDtypeStruct((quarter, width), jnp.bfloat16),
         in_specs=[vmem] * (nz + 2),
-        out_specs=vmem,
-        scratch_shapes=[pltpu.VMEM((quarter, FAR_SLOTS * HD), jnp.bfloat16)],
+        out_specs=hbm,
+        scratch_shapes=[
+            pltpu.VMEM((quarter, FAR_SLOTS * HD), jnp.bfloat16),
+            pltpu.VMEM((quarter, width), jnp.bfloat16),
+            pltpu.SemaphoreType.DMA((width // LAST_TILE,)),
+        ],
         compiler_params=params,
         name="last",
     )(*in_vmem(*far_parts[::-1], w_far, acc))

time: 47.8 us -> 47.6 us (level)
  no operation moved by 1% of the time
where the time goes in v6:
time: 47.6 us; the launch traced here: 47.4 us
  Pallas kernels  18.1 us (38%)
  starting transfers between devices  16.2 us (34%)
  waiting for transfers between devices  11.6 us (24%)
  between operations  0.77 us (2%)
  other arithmetic  0.63 us (1%)
    ppermute x11, starting transfers between devices, swap_along(): lax.ppermute(array, axis_name, [(i, i ^ partner) for i in range(size)])  16.2 us
    ppermute x11, waiting for transfers between devices, swap_along(): lax.ppermute(array, axis_name, [(i, i ^ partner) for i in range(size)])  11.6 us
    pallas_call x1, Pallas kernels, per_device_small_ring(): pl.pallas_call(functools.partial(first_kernel, len(kv), nz), out_shape=(p...  7.15 us
    pallas_call x1, Pallas kernels, per_device_small_ring(): pl.pallas_call(functools.partial(early_kernel, len(kv)), out_shape=(pltpu...  4.76 us
    pallas_call x1, Pallas kernels, per_device_small_ring(): pl.pallas_call(functools.partial(own_kernel, len(kv)), out_shape=slots_in...  1.93 us
    pallas_call x1, Pallas kernels, per_device_small_ring(): pl.pallas_call(functools.partial(last_kernel, nz), out_shape=jax.ShapeDty...  1.92 us
    pallas_call x1, Pallas kernels, per_device_small_ring(): pl.pallas_call(functools.partial(prep_kernel, rows, nq, nz), out_shape=(p...  1.47 us
  transfers between devices with their start and end apart: 11, of which 5 were waited for; matrix products, arithmetic and copies ran while one was open for 1% of the time, Pallas kernels for 32%

profile of v6, /device:TPU:0, one launch (start us, length us, event | category | flops | bytes accessed | tf_op | source)
XLA Modules:
  0.0 47.4 jit_solution(17040493288658381580)
XLA Ops:
  0.0 0.8 %join.1 = bf16[48,1024]{1,0:T(8,128)(2,1)S(1)} custom-call(bf16[48,512]{1,0:T(8,128)(2,1)} %k_ref.1, bf16[48,512]{1,0:T(8,128)(2,1)} %v_ref.1), custom_call_target="tpu_custom_call" | custom-call | tf_op jit(solution)/shard_map/join/pallas_call | solution.py:386
  0.8 5.1 %collective-permute-start.3 = (bf16[48,1024]{1,0:T(8,128)(2,1)S(1)}, bf16[48,1024]{1,0:T(8,128)(2,1)S(1)}, u32[]{:S(2)}, u32[]{:S(2)}) collective-permute-start(bf16[48,1024]{1,0:T(8,128)(2,1)S(1)} %join.1), channel_id=1, source_target_pairs={{0,3},{1,2},{2,1},{3,0},{4,7},{5,6},{6,5},{7,4},{8,11},{9,10},{10,... | collective-permute-start | bytes 294920 | tf_op jit(solution)/shard_map/ppermute | solution.py:155
  5.9 0.6 %collective-permute-start.5 = (bf16[48,1024]{1,0:T(8,128)(2,1)S(1)}, bf16[48,1024]{1,0:T(8,128)(2,1)S(1)}, u32[]{:S(2)}, u32[]{:S(2)}) collective-permute-start(bf16[48,1024]{1,0:T(8,128)(2,1)S(1)} %join.1), channel_id=1, source_target_pairs={{0,1},{1,0},{2,3},{3,2},{4,5},{5,4},{6,7},{7,6},{8,9},{9,8},{10,11... | collective-permute-start | bytes 294920 | tf_op jit(solution)/shard_map/ppermute | solution.py:155
  6.6 1.5 %prep.1 = (s32[33]{0:T(128)S(4)}, bf16[10,48,128]{2,1,0:T(8,128)(2,1)S(1)}, bf16[16,48,128]{2,1,0:T(8,128)(2,1)S(1)}, bf16[6,48,128]{2,1,0:T(8,128)(2,1)S(1)}, f32[192,768]{1,0:T(8,128)S(1)}) custom-call(s32[32]{0:T(128)} %mask_ref.1, s32[768]{0:T(1024)} %doc_ref.1, bf16[48,4096]{1,0:T(8,128)(2,1)} %q_ref.1), custom_call_target="tpu_custom_call" | custom-call | flops 4000000000 | tf_op jit(solution)/shard_map/prep/pallas_call | solution.py:394
  8.1 0.6 %reduce_sum.9 = s32[]{:T(128)} reduce(s32[32]{0:T(128)S(1)} %copy-done, s32[]{:T(128)} %constant.1.clone.1), dimensions={0}, to_apply=%region_0.0 | reduce | flops 31 | bytes 136 | tf_op jit(solution)/shard_map/reduce_sum | solution.py:406
  9.4 0.3 collective-permute-done.3
  9.6 4.6 %collective-permute-done.4 = bf16[48,1024]{1,0:T(8,128)(2,1)S(1)} collective-permute-done((bf16[48,1024]{1,0:T(8,128)(2,1)S(1)}, bf16[48,1024]{1,0:T(8,128)(2,1)S(1)}, u32[]{:S(2)}, u32[]{:S(2)}) %collective-permute-start.4) | collective-permute-done | bytes 98336 | tf_op jit(solution)/shard_map/ppermute | solution.py:155
  14.2 0.0 collective-permute-done.5
  14.3 1.6 %collective-permute-start.7 = (bf16[192,1024]{1,0:T(8,128)(2,1)S(1)}, bf16[192,1024]{1,0:T(8,128)(2,1)S(1)}, u32[]{:S(2)}, u32[]{:S(2)}) collective-permute-start(bf16[192,1024]{1,0:T(8,128)(2,1)S(1)} %get-tuple-element.51), channel_id=1, source_target_pairs={{0,8},{4,12},{8,0},{12,4},{1,9},{5,13},{9,1},{13,5},{2,10},{6,14},... | collective-permute-start | bytes 1179656 | tf_op jit(solution)/shard_map/ppermute | solution.py:155
  15.9 2.5 %collective-permute-start.6 = (bf16[16,48,128]{2,1,0:T(8,128)(2,1)S(1)}, bf16[16,48,128]{2,1,0:T(8,128)(2,1)S(1)}, u32[]{:S(2)}, u32[]{:S(2)}) collective-permute-start(bf16[16,48,128]{2,1,0:T(8,128)(2,1)S(1)} %get-tuple-element.37.refs_2_), channel_id=1, source_target_pairs={{0,3},{1,2},{2,1},{3,0},{4,7},{5,6},{6,5},{7,4},{8,11},{9,10},{10,... | collective-permute-start | bytes 589832 | tf_op jit(solution)/shard_map/ppermute | solution.py:155
  18.4 5.0 %collective-permute-done.6.refs_3_ = bf16[16,48,128]{2,1,0:T(8,128)(2,1)S(1)} collective-permute-done((bf16[16,48,128]{2,1,0:T(8,128)(2,1)S(1)}, bf16[16,48,128]{2,1,0:T(8,128)(2,1)S(1)}, u32[]{:S(2)}, u32[]{:S(2)}) %collective-permute-start.6) | collective-permute-done | bytes 196640 | tf_op jit(solution)/shard_map/ppermute | solution.py:155
  23.4 1.1 %collective-permute-done.7 = bf16[192,1024]{1,0:T(8,128)(2,1)S(1)} collective-permute-done((bf16[192,1024]{1,0:T(8,128)(2,1)S(1)}, bf16[192,1024]{1,0:T(8,128)(2,1)S(1)}, u32[]{:S(2)}, u32[]{:S(2)}) %collective-permute-start.7) | collective-permute-done | bytes 393248 | tf_op jit(solution)/shard_map/ppermute | solution.py:155
  24.6 0.1 collective-permute-start.8
  24.6 1.8 %collective-permute-start.12 = (bf16[16,48,128]{2,1,0:T(8,128)(2,1)S(1)}, bf16[16,48,128]{2,1,0:T(8,128)(2,1)S(1)}, u32[]{:S(2)}, u32[]{:S(2)}) collective-permute-start(bf16[16,48,128]{2,1,0:T(8,128)(2,1)S(1)} %get-tuple-element.37.refs_2_), channel_id=1, source_target_pairs={{0,2},{1,3},{2,0},{3,1},{4,6},{5,7},{6,4},{7,5},{8,10},{9,11},{10,... | collective-permute-start | bytes 589832 | tf_op jit(solution)/shard_map/ppermute | solution.py:155
  26.5 0.9 %collective-permute-start.13 = (bf16[16,48,128]{2,1,0:T(8,128)(2,1)S(1)}, bf16[16,48,128]{2,1,0:T(8,128)(2,1)S(1)}, u32[]{:S(2)}, u32[]{:S(2)}) collective-permute-start(bf16[16,48,128]{2,1,0:T(8,128)(2,1)S(1)} %get-tuple-element.37.refs_2_), channel_id=1, source_target_pairs={{0,1},{1,0},{2,3},{3,2},{4,5},{5,4},{6,7},{7,6},{8,9},{9,8},{10,11... | collective-permute-start | bytes 589832 | tf_op jit(solution)/shard_map/ppermute | solution.py:155
  27.4 0.0 collective-permute-done.8.refs_1_
  27.4 1.9 %own.1.refs_3_ = bf16[10,48,128]{2,1,0:T(8,128)(2,1)S(1)} custom-call(s32[33]{0:T(128)S(4)} %get-tuple-element.45.order_ref, bf16[384,1024]{1,0:T(8,128)(2,1)S(1)} %constant_dynamic-update-slice_fusion.4.refs_0_, bf16[384,1024]{1,0:T(8,128)(2,1)S(1)} %collective-permute-done.8.refs_1_, bf16[10,48,128]{2,1,0:T(8,128)(2,1)S(1)} %get-tuple-element.42.refs_2_, ...), custom_call_target="tpu_custom_call" | custom-call | flops 2000000000 | tf_op jit(solution)/shard_map/own/pallas_call | solution.py:420
  29.3 1.9 %collective-permute-start.10 = (bf16[10,48,128]{2,1,0:T(8,128)(2,1)S(1)}, bf16[10,48,128]{2,1,0:T(8,128)(2,1)S(1)}, u32[]{:S(2)}, u32[]{:S(2)}) collective-permute-start(bf16[10,48,128]{2,1,0:T(8,128)(2,1)S(1)} %own.1.refs_3_), channel_id=1, source_target_pairs={{0,2},{1,3},{2,0},{3,1},{4,6},{5,7},{6,4},{7,5},{8,10},{9,11},{10,... | collective-permute-start | bytes 368648 | tf_op jit(solution)/shard_map/ppermute | solution.py:155
  31.2 1.6 %collective-permute-start.11 = (bf16[10,48,128]{2,1,0:T(8,128)(2,1)S(1)}, bf16[10,48,128]{2,1,0:T(8,128)(2,1)S(1)}, u32[]{:S(2)}, u32[]{:S(2)}) collective-permute-start(bf16[10,48,128]{2,1,0:T(8,128)(2,1)S(1)} %own.1.refs_3_), channel_id=1, source_target_pairs={{0,3},{1,2},{2,1},{3,0},{4,7},{5,6},{6,5},{7,4},{8,11},{9,10},{10,... | collective-permute-start | bytes 368648 | tf_op jit(solution)/shard_map/ppermute | solution.py:155
  32.9 0.0 collective-permute-start.9
  32.9 4.8 %early.1 = (bf16[22,96,128]{2,1,0:T(8,128)(2,1)S(1)}, bf16[2816,2048]{1,0:T(8,128)(2,1)S(1)}) custom-call(s32[33]{0:T(128)S(4)} %get-tuple-element.45.order_ref, bf16[384,1024]{1,0:T(8,128)(2,1)S(1)} %constant_dynamic-update-slice_fusion.4.refs_0_, bf16[384,1024]{1,0:T(8,128)(2,1)S(1)} %collective-permute-done.8.refs_1_, ...), custom_call_target="tpu_custom_call" | custom-call | tf_op jit(solution)/shard_map/early/pallas_call | solution.py:435
  37.7 7.1 %first.1 = (f32[192,2048]{1,0:T(8,128)S(1)}, bf16[1280,2048]{1,0:T(8,128)(2,1)S(1)}) custom-call(s32[33]{0:T(128)S(4)} %get-tuple-element.45.order_ref, bf16[384,1024]{1,0:T(8,128)(2,1)S(1)} %constant_dynamic-update-slice_fusion.4.refs_0_, bf16[384,1024]{1,0:T(8,128)(2,1)S(1)} %collective-permute-done.8.refs_1_, ...), custom_call_target="tpu_custom_call" | custom-call | flops 6000000000 | tf_op jit(solution)/shard_map/first/pallas_call | solution.py:452
  44.8 0.6 %collective-permute-done.10.refs_1_ = bf16[10,48,128]{2,1,0:T(8,128)(2,1)S(1)} collective-permute-done((bf16[10,48,128]{2,1,0:T(8,128)(2,1)S(1)}, bf16[10,48,128]{2,1,0:T(8,128)(2,1)S(1)}, u32[]{:S(2)}, u32[]{:S(2)}) %collective-permute-start.10) | collective-permute-done | bytes 122912 | tf_op jit(solution)/shard_map/ppermute | solution.py:155
  45.5 1.9 %last.1 = bf16[192,2048]{1,0:T(8,128)(2,1)} custom-call(bf16[10,48,128]{2,1,0:T(8,128)(2,1)S(1)} %collective-permute-done.9.refs_0_, bf16[10,48,128]{2,1,0:T(8,128)(2,1)S(1)} %collective-permute-done.10.refs_1_, bf16[10,48,128]{2,1,0:T(8,128)(2,1)S(1)} %collective-permute-done.11.refs_2_, bf16[10,48,128]{2,1,0:T(8,128)(2,1)S(1)} %own.1.refs_3_, ...), custom_call_target="tpu_custom_call" | custom-call | tf_op jit(solution)/shard_map/last/pallas_call | solution.py:470
  (14 shorter events, 0.2 us)
Async XLA Ops:
  0.0 8.1 %copy-start = (s32[32]{0:T(128)S(1)}, s32[32]{0:T(128)}, u32[]{:S(2)}) copy-start(s32[32]{0:T(128)} %mask_ref.1) | copy-start | bytes 388
  0.8 8.8 %collective-permute-start.3 = (bf16[48,1024]{1,0:T(8,128)(2,1)S(1)}, bf16[48,1024]{1,0:T(8,128)(2,1)S(1)}, u32[]{:S(2)}, u32[]{:S(2)}) collective-permute-start(bf16[48,1024]{1,0:T(8,128)(2,1)S(1)} %join.1), channel_id=1, source_target_pairs={{0,3},{1,2},{2,1},{3,0},{4,7},{5,6},{6,5},{7,4},{8,11},{9,10},{10,... | collective-permute-start | bytes 294920 | tf_op jit(solution)/shard_map/ppermute | solution.py:155
  5.9 8.3 %collective-permute-start.4 = (bf16[48,1024]{1,0:T(8,128)(2,1)S(1)}, bf16[48,1024]{1,0:T(8,128)(2,1)S(1)}, u32[]{:S(2)}, u32[]{:S(2)}) collective-permute-start(bf16[48,1024]{1,0:T(8,128)(2,1)S(1)} %join.1), channel_id=1, source_target_pairs={{0,2},{1,3},{2,0},{3,1},{4,6},{5,7},{6,4},{7,5},{8,10},{9,11},{10,... | collective-permute-start | bytes 294920 | tf_op jit(solution)/shard_map/ppermute | solution.py:155
  5.9 8.3 %collective-permute-start.5 = (bf16[48,1024]{1,0:T(8,128)(2,1)S(1)}, bf16[48,1024]{1,0:T(8,128)(2,1)S(1)}, u32[]{:S(2)}, u32[]{:S(2)}) collective-permute-start(bf16[48,1024]{1,0:T(8,128)(2,1)S(1)} %join.1), channel_id=1, source_target_pairs={{0,1},{1,0},{2,3},{3,2},{4,5},{5,4},{6,7},{7,6},{8,9},{9,8},{10,11... | collective-permute-start | bytes 294920 | tf_op jit(solution)/shard_map/ppermute | solution.py:155
  14.3 10.2 %collective-permute-start.7 = (bf16[192,1024]{1,0:T(8,128)(2,1)S(1)}, bf16[192,1024]{1,0:T(8,128)(2,1)S(1)}, u32[]{:S(2)}, u32[]{:S(2)}) collective-permute-start(bf16[192,1024]{1,0:T(8,128)(2,1)S(1)} %get-tuple-element.51), channel_id=1, source_target_pairs={{0,8},{4,12},{8,0},{12,4},{1,9},{5,13},{9,1},{13,5},{2,10},{6,14},... | collective-permute-start | bytes 1179656 | tf_op jit(solution)/shard_map/ppermute | solution.py:155
  15.9 7.6 %collective-permute-start.6 = (bf16[16,48,128]{2,1,0:T(8,128)(2,1)S(1)}, bf16[16,48,128]{2,1,0:T(8,128)(2,1)S(1)}, u32[]{:S(2)}, u32[]{:S(2)}) collective-permute-start(bf16[16,48,128]{2,1,0:T(8,128)(2,1)S(1)} %get-tuple-element.37.refs_2_), channel_id=1, source_target_pairs={{0,3},{1,2},{2,1},{3,0},{4,7},{5,6},{6,5},{7,4},{8,11},{9,10},{10,... | collective-permute-start | bytes 589832 | tf_op jit(solution)/shard_map/ppermute | solution.py:155
  24.6 2.8 %collective-permute-start.8 = (bf16[384,1024]{1,0:T(8,128)(2,1)S(1)}, bf16[384,1024]{1,0:T(8,128)(2,1)S(1)}, u32[]{:S(2)}, u32[]{:S(2)}) collective-permute-start(bf16[384,1024]{1,0:T(8,128)(2,1)S(1)} %constant_dynamic-update-slice_fusion.4.refs_0_), channel_id=1, source_target_pairs={{0,4},{4,0},{8,12},{12,8},{1,5},{5,1},{9,13},{13,9},{2,6},{6,2},{1... | collective-permute-start | bytes 2359304 | tf_op jit(solution)/shard_map/ppermute | solution.py:155
  24.6 13.0 %collective-permute-start.12 = (bf16[16,48,128]{2,1,0:T(8,128)(2,1)S(1)}, bf16[16,48,128]{2,1,0:T(8,128)(2,1)S(1)}, u32[]{:S(2)}, u32[]{:S(2)}) collective-permute-start(bf16[16,48,128]{2,1,0:T(8,128)(2,1)S(1)} %get-tuple-element.37.refs_2_), channel_id=1, source_target_pairs={{0,2},{1,3},{2,0},{3,1},{4,6},{5,7},{6,4},{7,5},{8,10},{9,11},{10,... | collective-permute-start | bytes 589832 | tf_op jit(solution)/shard_map/ppermute | solution.py:155
  26.5 11.2 %collective-permute-start.13 = (bf16[16,48,128]{2,1,0:T(8,128)(2,1)S(1)}, bf16[16,48,128]{2,1,0:T(8,128)(2,1)S(1)}, u32[]{:S(2)}, u32[]{:S(2)}) collective-permute-start(bf16[16,48,128]{2,1,0:T(8,128)(2,1)S(1)} %get-tuple-element.37.refs_2_), channel_id=1, source_target_pairs={{0,1},{1,0},{2,3},{3,2},{4,5},{5,4},{6,7},{7,6},{8,9},{9,8},{10,11... | collective-permute-start | bytes 589832 | tf_op jit(solution)/shard_map/ppermute | solution.py:155
  29.3 16.2 %collective-permute-start.10 = (bf16[10,48,128]{2,1,0:T(8,128)(2,1)S(1)}, bf16[10,48,128]{2,1,0:T(8,128)(2,1)S(1)}, u32[]{:S(2)}, u32[]{:S(2)}) collective-permute-start(bf16[10,48,128]{2,1,0:T(8,128)(2,1)S(1)} %own.1.refs_3_), channel_id=1, source_target_pairs={{0,2},{1,3},{2,0},{3,1},{4,6},{5,7},{6,4},{7,5},{8,10},{9,11},{10,... | collective-permute-start | bytes 368648 | tf_op jit(solution)/shard_map/ppermute | solution.py:155
  31.2 14.2 %collective-permute-start.11 = (bf16[10,48,128]{2,1,0:T(8,128)(2,1)S(1)}, bf16[10,48,128]{2,1,0:T(8,128)(2,1)S(1)}, u32[]{:S(2)}, u32[]{:S(2)}) collective-permute-start(bf16[10,48,128]{2,1,0:T(8,128)(2,1)S(1)} %own.1.refs_3_), channel_id=1, source_target_pairs={{0,3},{1,2},{2,1},{3,0},{4,7},{5,6},{6,5},{7,4},{8,11},{9,10},{10,... | collective-permute-start | bytes 368648 | tf_op jit(solution)/shard_map/ppermute | solution.py:155
  32.9 12.6 %collective-permute-start.9 = (bf16[10,48,128]{2,1,0:T(8,128)(2,1)S(1)}, bf16[10,48,128]{2,1,0:T(8,128)(2,1)S(1)}, u32[]{:S(2)}, u32[]{:S(2)}) collective-permute-start(bf16[10,48,128]{2,1,0:T(8,128)(2,1)S(1)} %own.1.refs_3_), channel_id=1, source_target_pairs={{0,1},{1,0},{2,3},{3,2},{4,5},{5,4},{6,7},{7,6},{8,9},{9,8},{10,11... | collective-permute-start | bytes 368648 | tf_op jit(solution)/shard_map/ppermute | solution.py:155

commit v7 on v6

--- a/solution.py
+++ b/solution.py
@@ -139,7 +139,7 @@
 PAIR = 2
 NEAR_SLOTS = 16
 EARLY_PARTS = 2
-EARLY_COST = 0
+EARLY_COST = 4
 FIRST_COST = 6
 FAR_SLOTS = 10
 TILE = 1024
@@ -248,7 +248,7 @@
         scores = scores_of(q_ref[slot], slot, kv_refs, order_ref)
         att_ref[slot] = attended(scores, bias_ref[:rows], slot, kv_refs, order_ref)
 
-    pl.loop(0, FAR_SLOTS, unroll=FAR_SLOTS // 2)(one_slot)
+    pl.loop(0, FAR_SLOTS, unroll=FAR_SLOTS)(one_slot)
 
 
 def pairs_of(order_ref):
@@ -423,7 +423,7 @@
         in_specs=[smem] + [vmem] * (len(kv) + 2),
         out_specs=vmem,
         compiler_params=params,
-        cost_estimate=cost(2),
+        cost_estimate=cost(0),
         name="own",
     )(order, *in_vmem(*kv, far, bias))
     far_parts = [far_own, *swaps_along(far_own, "kvring")]

time: 47.6 us -> 47.6 us (level)
  Pallas kernels: 18.1 us -> 17.6 us
  waiting for transfers between devices: 11.6 us -> 12.1 us
    ppermute x11, waiting for transfers between devices: 11.6 us -> 12.1 us  [swap_along(): lax.ppermute(array, axis_name, [(i, i ^ partner) for i in range(size)])]
  transfers between devices with their start and end apart: 11 -> 11, of which waited for: 5 -> 6; matrix products, arithmetic and copies ran while one was open for 1% -> 1% of each run, Pallas kernels for 32% -> 31%
where the time goes in v7:
time: 47.6 us; the launch traced here: 47.4 us
  Pallas kernels  17.6 us (37%)
  starting transfers between devices  16.2 us (34%)
  waiting for transfers between devices  12.1 us (25%)
  between operations  0.75 us (2%)
  other arithmetic  0.63 us (1%)
    ppermute x11, starting transfers between devices, swap_along(): lax.ppermute(array, axis_name, [(i, i ^ partner) for i in range(size)])  16.2 us
    ppermute x11, waiting for transfers between devices, swap_along(): lax.ppermute(array, axis_name, [(i, i ^ partner) for i in range(size)])  12.1 us
    pallas_call x1, Pallas kernels, per_device_small_ring(): pl.pallas_call(functools.partial(first_kernel, len(kv), nz), out_shape=(p...  7.04 us
    pallas_call x1, Pallas kernels, per_device_small_ring(): pl.pallas_call(functools.partial(early_kernel, len(kv)), out_shape=(pltpu...  4.75 us
    pallas_call x1, Pallas kernels, per_device_small_ring(): pl.pallas_call(functools.partial(last_kernel, nz), out_shape=jax.ShapeDty...  1.92 us
    pallas_call x1, Pallas kernels, per_device_small_ring(): pl.pallas_call(functools.partial(own_kernel, len(kv)), out_shape=slots_in...  1.55 us
    pallas_call x1, Pallas kernels, per_device_small_ring(): pl.pallas_call(functools.partial(prep_kernel, rows, nq, nz), out_shape=(p...  1.47 us
  transfers between devices with their start and end apart: 11, of which 6 were waited for; matrix products, arithmetic and copies ran while one was open for 1% of the time, Pallas kernels for 31%

profile of v7, /device:TPU:0, one launch (start us, length us, event | category | flops | bytes accessed | tf_op | source)
XLA Modules:
  0.0 47.4 jit_solution(2608922821284393534)
XLA Ops:
  0.0 0.8 %join.1 = bf16[48,1024]{1,0:T(8,128)(2,1)S(1)} custom-call(bf16[48,512]{1,0:T(8,128)(2,1)} %k_ref.1, bf16[48,512]{1,0:T(8,128)(2,1)} %v_ref.1), custom_call_target="tpu_custom_call" | custom-call | tf_op jit(solution)/shard_map/join/pallas_call | solution.py:386
  0.8 5.1 %collective-permute-start.3 = (bf16[48,1024]{1,0:T(8,128)(2,1)S(1)}, bf16[48,1024]{1,0:T(8,128)(2,1)S(1)}, u32[]{:S(2)}, u32[]{:S(2)}) collective-permute-start(bf16[48,1024]{1,0:T(8,128)(2,1)S(1)} %join.1), channel_id=1, source_target_pairs={{0,3},{1,2},{2,1},{3,0},{4,7},{5,6},{6,5},{7,4},{8,11},{9,10},{10,... | collective-permute-start | bytes 294920 | tf_op jit(solution)/shard_map/ppermute | solution.py:155
  5.9 0.0 collective-permute-start.4
  5.9 0.6 %collective-permute-start.5 = (bf16[48,1024]{1,0:T(8,128)(2,1)S(1)}, bf16[48,1024]{1,0:T(8,128)(2,1)S(1)}, u32[]{:S(2)}, u32[]{:S(2)}) collective-permute-start(bf16[48,1024]{1,0:T(8,128)(2,1)S(1)} %join.1), channel_id=1, source_target_pairs={{0,1},{1,0},{2,3},{3,2},{4,5},{5,4},{6,7},{7,6},{8,9},{9,8},{10,11... | collective-permute-start | bytes 294920 | tf_op jit(solution)/shard_map/ppermute | solution.py:155
  6.6 1.5 %prep.1 = (s32[33]{0:T(128)S(4)}, bf16[10,48,128]{2,1,0:T(8,128)(2,1)S(1)}, bf16[16,48,128]{2,1,0:T(8,128)(2,1)S(1)}, bf16[6,48,128]{2,1,0:T(8,128)(2,1)S(1)}, f32[192,768]{1,0:T(8,128)S(1)}) custom-call(s32[32]{0:T(128)} %mask_ref.1, s32[768]{0:T(1024)} %doc_ref.1, bf16[48,4096]{1,0:T(8,128)(2,1)} %q_ref.1), custom_call_target="tpu_custom_call" | custom-call | flops 4000000000 | tf_op jit(solution)/shard_map/prep/pallas_call | solution.py:394
  8.1 0.6 %reduce_sum.9 = s32[]{:T(128)} reduce(s32[32]{0:T(128)S(1)} %copy-done, s32[]{:T(128)} %constant.1.clone.1), dimensions={0}, to_apply=%region_0.0 | reduce | flops 31 | bytes 136 | tf_op jit(solution)/shard_map/reduce_sum | solution.py:406
  9.4 0.3 collective-permute-done.3
  9.6 4.6 %collective-permute-done.4 = bf16[48,1024]{1,0:T(8,128)(2,1)S(1)} collective-permute-done((bf16[48,1024]{1,0:T(8,128)(2,1)S(1)}, bf16[48,1024]{1,0:T(8,128)(2,1)S(1)}, u32[]{:S(2)}, u32[]{:S(2)}) %collective-permute-start.4) | collective-permute-done | bytes 98336 | tf_op jit(solution)/shard_map/ppermute | solution.py:155
  14.3 1.6 %collective-permute-start.7 = (bf16[192,1024]{1,0:T(8,128)(2,1)S(1)}, bf16[192,1024]{1,0:T(8,128)(2,1)S(1)}, u32[]{:S(2)}, u32[]{:S(2)}) collective-permute-start(bf16[192,1024]{1,0:T(8,128)(2,1)S(1)} %get-tuple-element.51), channel_id=1, source_target_pairs={{0,8},{4,12},{8,0},{12,4},{1,9},{5,13},{9,1},{13,5},{2,10},{6,14},... | collective-permute-start | bytes 1179656 | tf_op jit(solution)/shard_map/ppermute | solution.py:155
  15.9 2.5 %collective-permute-start.6 = (bf16[16,48,128]{2,1,0:T(8,128)(2,1)S(1)}, bf16[16,48,128]{2,1,0:T(8,128)(2,1)S(1)}, u32[]{:S(2)}, u32[]{:S(2)}) collective-permute-start(bf16[16,48,128]{2,1,0:T(8,128)(2,1)S(1)} %get-tuple-element.37.refs_2_), channel_id=1, source_target_pairs={{0,3},{1,2},{2,1},{3,0},{4,7},{5,6},{6,5},{7,4},{8,11},{9,10},{10,... | collective-permute-start | bytes 589832 | tf_op jit(solution)/shard_map/ppermute | solution.py:155
  18.4 5.0 %collective-permute-done.6.refs_3_ = bf16[16,48,128]{2,1,0:T(8,128)(2,1)S(1)} collective-permute-done((bf16[16,48,128]{2,1,0:T(8,128)(2,1)S(1)}, bf16[16,48,128]{2,1,0:T(8,128)(2,1)S(1)}, u32[]{:S(2)}, u32[]{:S(2)}) %collective-permute-start.6) | collective-permute-done | bytes 196640 | tf_op jit(solution)/shard_map/ppermute | solution.py:155
  23.4 1.1 %collective-permute-done.7 = bf16[192,1024]{1,0:T(8,128)(2,1)S(1)} collective-permute-done((bf16[192,1024]{1,0:T(8,128)(2,1)S(1)}, bf16[192,1024]{1,0:T(8,128)(2,1)S(1)}, u32[]{:S(2)}, u32[]{:S(2)}) %collective-permute-start.7) | collective-permute-done | bytes 393248 | tf_op jit(solution)/shard_map/ppermute | solution.py:155
  24.6 0.1 collective-permute-start.8
  24.6 1.8 %collective-permute-start.12 = (bf16[16,48,128]{2,1,0:T(8,128)(2,1)S(1)}, bf16[16,48,128]{2,1,0:T(8,128)(2,1)S(1)}, u32[]{:S(2)}, u32[]{:S(2)}) collective-permute-start(bf16[16,48,128]{2,1,0:T(8,128)(2,1)S(1)} %get-tuple-element.37.refs_2_), channel_id=1, source_target_pairs={{0,2},{1,3},{2,0},{3,1},{4,6},{5,7},{6,4},{7,5},{8,10},{9,11},{10,... | collective-permute-start | bytes 589832 | tf_op jit(solution)/shard_map/ppermute | solution.py:155
  26.5 0.9 %collective-permute-start.13 = (bf16[16,48,128]{2,1,0:T(8,128)(2,1)S(1)}, bf16[16,48,128]{2,1,0:T(8,128)(2,1)S(1)}, u32[]{:S(2)}, u32[]{:S(2)}) collective-permute-start(bf16[16,48,128]{2,1,0:T(8,128)(2,1)S(1)} %get-tuple-element.37.refs_2_), channel_id=1, source_target_pairs={{0,1},{1,0},{2,3},{3,2},{4,5},{5,4},{6,7},{7,6},{8,9},{9,8},{10,11... | collective-permute-start | bytes 589832 | tf_op jit(solution)/shard_map/ppermute | solution.py:155
  27.4 1.6 %own.1.refs_3_ = bf16[10,48,128]{2,1,0:T(8,128)(2,1)S(1)} custom-call(s32[33]{0:T(128)S(4)} %get-tuple-element.45.order_ref, bf16[384,1024]{1,0:T(8,128)(2,1)S(1)} %constant_dynamic-update-slice_fusion.4.refs_0_, bf16[384,1024]{1,0:T(8,128)(2,1)S(1)} %collective-permute-done.8.refs_1_, bf16[10,48,128]{2,1,0:T(8,128)(2,1)S(1)} %get-tuple-element.42.refs_2_, ...), custom_call_target="tpu_custom_call" | custom-call | tf_op jit(solution)/shard_map/own/pallas_call | solution.py:420
  28.9 1.9 %collective-permute-start.10 = (bf16[10,48,128]{2,1,0:T(8,128)(2,1)S(1)}, bf16[10,48,128]{2,1,0:T(8,128)(2,1)S(1)}, u32[]{:S(2)}, u32[]{:S(2)}) collective-permute-start(bf16[10,48,128]{2,1,0:T(8,128)(2,1)S(1)} %own.1.refs_3_), channel_id=1, source_target_pairs={{0,2},{1,3},{2,0},{3,1},{4,6},{5,7},{6,4},{7,5},{8,10},{9,11},{10,... | collective-permute-start | bytes 368648 | tf_op jit(solution)/shard_map/ppermute | solution.py:155
  30.9 1.6 %collective-permute-start.11 = (bf16[10,48,128]{2,1,0:T(8,128)(2,1)S(1)}, bf16[10,48,128]{2,1,0:T(8,128)(2,1)S(1)}, u32[]{:S(2)}, u32[]{:S(2)}) collective-permute-start(bf16[10,48,128]{2,1,0:T(8,128)(2,1)S(1)} %own.1.refs_3_), channel_id=1, source_target_pairs={{0,3},{1,2},{2,1},{3,0},{4,7},{5,6},{6,5},{7,4},{8,11},{9,10},{10,... | collective-permute-start | bytes 368648 | tf_op jit(solution)/shard_map/ppermute | solution.py:155
  32.5 4.7 %early.1 = (bf16[22,96,128]{2,1,0:T(8,128)(2,1)S(1)}, bf16[2816,2048]{1,0:T(8,128)(2,1)S(1)}) custom-call(s32[33]{0:T(128)S(4)} %get-tuple-element.45.order_ref, bf16[384,1024]{1,0:T(8,128)(2,1)S(1)} %constant_dynamic-update-slice_fusion.4.refs_0_, bf16[384,1024]{1,0:T(8,128)(2,1)S(1)} %collective-permute-done.8.refs_1_, ...), custom_call_target="tpu_custom_call" | custom-call | flops 4000000000 | tf_op jit(solution)/shard_map/early/pallas_call | solution.py:435
  37.3 0.4 collective-permute-done.12.refs_2_
  37.6 7.0 %first.1 = (f32[192,2048]{1,0:T(8,128)S(1)}, bf16[1280,2048]{1,0:T(8,128)(2,1)S(1)}) custom-call(s32[33]{0:T(128)S(4)} %get-tuple-element.45.order_ref, bf16[384,1024]{1,0:T(8,128)(2,1)S(1)} %constant_dynamic-update-slice_fusion.4.refs_0_, bf16[384,1024]{1,0:T(8,128)(2,1)S(1)} %collective-permute-done.8.refs_1_, ...), custom_call_target="tpu_custom_call" | custom-call | flops 6000000000 | tf_op jit(solution)/shard_map/first/pallas_call | solution.py:452
  44.7 0.8 %collective-permute-done.10.refs_1_ = bf16[10,48,128]{2,1,0:T(8,128)(2,1)S(1)} collective-permute-done((bf16[10,48,128]{2,1,0:T(8,128)(2,1)S(1)}, bf16[10,48,128]{2,1,0:T(8,128)(2,1)S(1)}, u32[]{:S(2)}, u32[]{:S(2)}) %collective-permute-start.10) | collective-permute-done | bytes 122912 | tf_op jit(solution)/shard_map/ppermute | solution.py:155
  45.5 0.0 collective-permute-done.11.refs_2_
  45.5 1.9 %last.1 = bf16[192,2048]{1,0:T(8,128)(2,1)} custom-call(bf16[10,48,128]{2,1,0:T(8,128)(2,1)S(1)} %collective-permute-done.9.refs_0_, bf16[10,48,128]{2,1,0:T(8,128)(2,1)S(1)} %collective-permute-done.10.refs_1_, bf16[10,48,128]{2,1,0:T(8,128)(2,1)S(1)} %collective-permute-done.11.refs_2_, bf16[10,48,128]{2,1,0:T(8,128)(2,1)S(1)} %own.1.refs_3_, ...), custom_call_target="tpu_custom_call" | custom-call | tf_op jit(solution)/shard_map/last/pallas_call | solution.py:470
  (14 shorter events, 0.2 us)
Async XLA Ops:
  0.0 8.1 %copy-start = (s32[32]{0:T(128)S(1)}, s32[32]{0:T(128)}, u32[]{:S(2)}) copy-start(s32[32]{0:T(128)} %mask_ref.1) | copy-start | bytes 388
  0.8 8.8 %collective-permute-start.3 = (bf16[48,1024]{1,0:T(8,128)(2,1)S(1)}, bf16[48,1024]{1,0:T(8,128)(2,1)S(1)}, u32[]{:S(2)}, u32[]{:S(2)}) collective-permute-start(bf16[48,1024]{1,0:T(8,128)(2,1)S(1)} %join.1), channel_id=1, source_target_pairs={{0,3},{1,2},{2,1},{3,0},{4,7},{5,6},{6,5},{7,4},{8,11},{9,10},{10,... | collective-permute-start | bytes 294920 | tf_op jit(solution)/shard_map/ppermute | solution.py:155
  5.9 8.3 %collective-permute-start.4 = (bf16[48,1024]{1,0:T(8,128)(2,1)S(1)}, bf16[48,1024]{1,0:T(8,128)(2,1)S(1)}, u32[]{:S(2)}, u32[]{:S(2)}) collective-permute-start(bf16[48,1024]{1,0:T(8,128)(2,1)S(1)} %join.1), channel_id=1, source_target_pairs={{0,2},{1,3},{2,0},{3,1},{4,6},{5,7},{6,4},{7,5},{8,10},{9,11},{10,... | collective-permute-start | bytes 294920 | tf_op jit(solution)/shard_map/ppermute | solution.py:155
  5.9 8.3 %collective-permute-start.5 = (bf16[48,1024]{1,0:T(8,128)(2,1)S(1)}, bf16[48,1024]{1,0:T(8,128)(2,1)S(1)}, u32[]{:S(2)}, u32[]{:S(2)}) collective-permute-start(bf16[48,1024]{1,0:T(8,128)(2,1)S(1)} %join.1), channel_id=1, source_target_pairs={{0,1},{1,0},{2,3},{3,2},{4,5},{5,4},{6,7},{7,6},{8,9},{9,8},{10,11... | collective-permute-start | bytes 294920 | tf_op jit(solution)/shard_map/ppermute | solution.py:155
  14.3 10.2 %collective-permute-start.7 = (bf16[192,1024]{1,0:T(8,128)(2,1)S(1)}, bf16[192,1024]{1,0:T(8,128)(2,1)S(1)}, u32[]{:S(2)}, u32[]{:S(2)}) collective-permute-start(bf16[192,1024]{1,0:T(8,128)(2,1)S(1)} %get-tuple-element.51), channel_id=1, source_target_pairs={{0,8},{4,12},{8,0},{12,4},{1,9},{5,13},{9,1},{13,5},{2,10},{6,14},... | collective-permute-start | bytes 1179656 | tf_op jit(solution)/shard_map/ppermute | solution.py:155
  15.9 7.6 %collective-permute-start.6 = (bf16[16,48,128]{2,1,0:T(8,128)(2,1)S(1)}, bf16[16,48,128]{2,1,0:T(8,128)(2,1)S(1)}, u32[]{:S(2)}, u32[]{:S(2)}) collective-permute-start(bf16[16,48,128]{2,1,0:T(8,128)(2,1)S(1)} %get-tuple-element.37.refs_2_), channel_id=1, source_target_pairs={{0,3},{1,2},{2,1},{3,0},{4,7},{5,6},{6,5},{7,4},{8,11},{9,10},{10,... | collective-permute-start | bytes 589832 | tf_op jit(solution)/shard_map/ppermute | solution.py:155
  24.6 2.8 %collective-permute-start.8 = (bf16[384,1024]{1,0:T(8,128)(2,1)S(1)}, bf16[384,1024]{1,0:T(8,128)(2,1)S(1)}, u32[]{:S(2)}, u32[]{:S(2)}) collective-permute-start(bf16[384,1024]{1,0:T(8,128)(2,1)S(1)} %constant_dynamic-update-slice_fusion.4.refs_0_), channel_id=1, source_target_pairs={{0,4},{4,0},{8,12},{12,8},{1,5},{5,1},{9,13},{13,9},{2,6},{6,2},{1... | collective-permute-start | bytes 2359304 | tf_op jit(solution)/shard_map/ppermute | solution.py:155
  24.6 13.0 %collective-permute-start.12 = (bf16[16,48,128]{2,1,0:T(8,128)(2,1)S(1)}, bf16[16,48,128]{2,1,0:T(8,128)(2,1)S(1)}, u32[]{:S(2)}, u32[]{:S(2)}) collective-permute-start(bf16[16,48,128]{2,1,0:T(8,128)(2,1)S(1)} %get-tuple-element.37.refs_2_), channel_id=1, source_target_pairs={{0,2},{1,3},{2,0},{3,1},{4,6},{5,7},{6,4},{7,5},{8,10},{9,11},{10,... | collective-permute-start | bytes 589832 | tf_op jit(solution)/shard_map/ppermute | solution.py:155
  26.5 11.1 %collective-permute-start.13 = (bf16[16,48,128]{2,1,0:T(8,128)(2,1)S(1)}, bf16[16,48,128]{2,1,0:T(8,128)(2,1)S(1)}, u32[]{:S(2)}, u32[]{:S(2)}) collective-permute-start(bf16[16,48,128]{2,1,0:T(8,128)(2,1)S(1)} %get-tuple-element.37.refs_2_), channel_id=1, source_target_pairs={{0,1},{1,0},{2,3},{3,2},{4,5},{5,4},{6,7},{7,6},{8,9},{9,8},{10,11... | collective-permute-start | bytes 589832 | tf_op jit(solution)/shard_map/ppermute | solution.py:155
  28.9 16.5 %collective-permute-start.10 = (bf16[10,48,128]{2,1,0:T(8,128)(2,1)S(1)}, bf16[10,48,128]{2,1,0:T(8,128)(2,1)S(1)}, u32[]{:S(2)}, u32[]{:S(2)}) collective-permute-start(bf16[10,48,128]{2,1,0:T(8,128)(2,1)S(1)} %own.1.refs_3_), channel_id=1, source_target_pairs={{0,2},{1,3},{2,0},{3,1},{4,6},{5,7},{6,4},{7,5},{8,10},{9,11},{10,... | collective-permute-start | bytes 368648 | tf_op jit(solution)/shard_map/ppermute | solution.py:155
  30.9 14.6 %collective-permute-start.11 = (bf16[10,48,128]{2,1,0:T(8,128)(2,1)S(1)}, bf16[10,48,128]{2,1,0:T(8,128)(2,1)S(1)}, u32[]{:S(2)}, u32[]{:S(2)}) collective-permute-start(bf16[10,48,128]{2,1,0:T(8,128)(2,1)S(1)} %own.1.refs_3_), channel_id=1, source_target_pairs={{0,3},{1,2},{2,1},{3,0},{4,7},{5,6},{6,5},{7,4},{8,11},{9,10},{10,... | collective-permute-start | bytes 368648 | tf_op jit(solution)/shard_map/ppermute | solution.py:155
  32.5 13.0 %collective-permute-start.9 = (bf16[10,48,128]{2,1,0:T(8,128)(2,1)S(1)}, bf16[10,48,128]{2,1,0:T(8,128)(2,1)S(1)}, u32[]{:S(2)}, u32[]{:S(2)}) collective-permute-start(bf16[10,48,128]{2,1,0:T(8,128)(2,1)S(1)} %own.1.refs_3_), channel_id=1, source_target_pairs={{0,1},{1,0},{2,3},{3,2},{4,5},{5,4},{6,7},{7,6},{8,9},{9,8},{10,11... | collective-permute-start | bytes 368648 | tf_op jit(solution)/shard_map/ppermute | solution.py:155
